TPU v7x, 128 devices: a whole 4x4x4 slice. The times are simulated.
128 devices in a mesh: replica: 8 (over x, y_lo), tensor: 16 (over y_hi, z, core).
Axes of the slice: x: 4, y: 4 (y_hi: 2, y_lo: 2; y = y_hi * 2 + y_lo), z: 4, core: 2. Of those that a mesh axis runs over, the one named last changes fastest.
Arguments:
- tokens: bfloat16 [8192, 8192], P(('replica', 'tensor')), may hold values from -16 to 16
- norm_gain: float32 [8192], replicated, may hold values from 0.5 to 1.5
- query_weight: bfloat16 [8192, 8192], P(None, 'tensor'), may hold values from -0.5 to 0.5
- kv_weight: bfloat16 [8192, 2048], P(None, 'tensor'), may hold values from -0.5 to 0.5
- out_weight: bfloat16 [8192, 8192], P('tensor'), may hold values from -0.5 to 0.5
- pseudo_grad: bfloat16 [8, 8192, 1024], P('replica', 'tensor'), may hold values from -6 to 6
- grad_exps: int32 [8, 8192, 8], P('replica', 'tensor'), may hold values from -2 to 1
- params: bfloat16 [8192, 1024], P('tensor'), may hold values from -4 to 4
- momentum: float32 [8192, 1024], P('tensor', 'replica'), may hold values from -4 to 4
Outputs:
- attended: bfloat16 [8192, 8192], P(('replica', 'tensor'))
- new_params: bfloat16 [8192, 1024], P('tensor')
- new_momentum: float32 [8192, 1024], P('tensor', 'replica')
All inputs are finite; a program needn't handle non-finite values. Where the computation divides by a largest or mean magnitude, that divisor is 1e-20 or more.
Results may differ from a plain program's by a relative error of at most 0.019.
Values may be sent and summed in bfloat16 or wider, within the bound.
No kernel may reach another device: no remote copies, remote signals or barrier semaphores. Data moves between devices by JAX's collectives and lax.ppermute only.
A program may use at most 128 MiB of HBM per device.

v0:
```python
import functools
import math

import jax
import jax.numpy as jnp
from jax import lax
from jax.experimental import pallas as pl
from jax.experimental.pallas import tpu as pltpu
from jax.sharding import Mesh
from jax.sharding import PartitionSpec as P

HEAD = 128
REPLICA = ("x", "ylo")
TENSOR = ("yhi", "z", "core")
ROWS = 64
RING = (0, 1, -1, 2)
Y = ("ylo", "yhi")
HALVES = 2
TILE = 1024
MIB = 1024 * 1024


def params(mib=8):
    return pltpu.CompilerParams(vmem_limit_bytes=mib * MIB)


def cost(flops, moved):
    return pl.CostEstimate(flops=int(flops), bytes_accessed=int(moved), transcendentals=0)


def hadamard_table(width):
    index = jnp.arange(width, dtype=jnp.int32)
    common = jnp.bitwise_and(index[:, None], index[None, :])
    parity = jnp.zeros((width, width), jnp.int32)
    for bit in range(int(math.log2(width))):
        parity = parity + jnp.bitwise_and(jnp.right_shift(common, bit), 1)
    sign = 1.0 - 2.0 * jnp.bitwise_and(parity, 1).astype(jnp.float32)
    return sign / math.sqrt(width)


def norm_body(rows_ref, gain_ref, whole_ref, *half_refs):
    values = rows_ref[...].astype(jnp.float32)
    power = jnp.mean(values * values, axis=-1, keepdims=True)
    normed = (values * lax.rsqrt(power + 1e-05) * gain_ref[...]).astype(jnp.bfloat16)
    whole_ref[...] = normed
    count = normed.shape[0] // HALVES
    for at, half_ref in enumerate(half_refs):
        half_ref[...] = normed[at * count : (at + 1) * count]


def normalize(rows, gain):
    count, width = rows.shape
    return pl.pallas_call(
        norm_body,
        out_shape=[
            jax.ShapeDtypeStruct((c, width), jnp.bfloat16)
            for c in [count] + [count // HALVES] * HALVES
        ],
        compiler_params=params(12),
        cost_estimate=cost(4 * rows.size, 6 * rows.size),
        name="normalize",
    )(rows, gain.reshape(1, width))


def project_body(core_ref, *refs):
    blocks, refs = refs[:-12], refs[-12:]
    weights, (query_out, pair_out, total), held, arrived = refs[:4], refs[4:7], refs[7:11], refs[11]
    half = weights[0].shape[1]
    depth = weights[0].shape[0]
    chunks = arrived.shape[1]
    chunk = depth // chunks

    def copies_of(at):
        span = pl.ds(pl.multiple_of(at * chunk, chunk), chunk)
        return [
            pltpu.make_async_copy(weight.at[span, :], place.at[span, :], arrived.at[kind, at])
            for kind, (weight, place) in enumerate(zip(weights, held))
        ]

    for at in range(chunks):
        for copy in copies_of(at):
            copy.start()
    total[...] = jnp.zeros_like(total)
    qa_ref, qb_ref, ka_ref, kb_ref = held

    def step(at, carry):
        for copy in copies_of(at):
            copy.wait()
        span = pl.ds(pl.multiple_of(at * chunk, chunk), chunk)
        rows = jnp.concatenate([ref[:, span] for ref in blocks], axis=0)
        both = jnp.concatenate([ka_ref[span, :], kb_ref[span, :]], axis=1)
        for start, weight in ((0, qa_ref[span, :]), (half, qb_ref[span, :]), (2 * half, both)):
            total[:, start : start + weight.shape[1]] += jnp.dot(
                rows, weight, preferred_element_type=jnp.float32
            )
        return carry

    lax.fori_loop(0, chunks, step, 0)
    flip = core_ref[0] == 0
    value = total[...].astype(jnp.bfloat16)
    query_out[...] = value[:, : 2 * half]
    left, right = value[:, 2 * half : 2 * half + HEAD], value[:, 2 * half + HEAD :]
    pair_out[:, :HEAD] = jnp.where(flip, left, right)
    pair_out[:, HEAD:] = jnp.where(flip, right, left)


def project(core, blocks, weights):
    width = blocks[0].shape[1]
    count = sum(block.shape[0] for block in blocks)
    qcols = 2 * weights[0].shape[1]
    kcols = 2 * weights[2].shape[1]
    vmem = pl.BlockSpec(memory_space=pltpu.VMEM)
    return pl.pallas_call(
        project_body,
        in_specs=[pl.BlockSpec(memory_space=pltpu.SMEM)]
        + [vmem] * len(blocks)
        + [pl.BlockSpec(memory_space=pl.ANY)] * len(weights),
        out_specs=[vmem, vmem],
        out_shape=[
            jax.ShapeDtypeStruct((count, qcols), jnp.bfloat16),
            jax.ShapeDtypeStruct((count, kcols), jnp.bfloat16),
        ],
        scratch_shapes=[pltpu.VMEM((count, qcols + kcols), jnp.float32)]
        + [pltpu.VMEM(weight.shape, jnp.bfloat16) for weight in weights]
        + [pltpu.SemaphoreType.DMA((len(weights), width // TILE))],
        compiler_params=params(56),
        cost_estimate=cost(
            3 * count * width * (qcols + kcols), 2 * width * (count + qcols + kcols)
        ),
        name="project",
    )(core, *blocks, *weights)


def copies_of(weights, held, arrived, first, at):
    half = weights[0].shape[0]
    span = pl.ds(pl.multiple_of(at * TILE, TILE), TILE)
    return [
        pltpu.make_async_copy(
            weight.at[:, pl.ds(pl.multiple_of(first + at * TILE, TILE), TILE)],
            held.at[pl.ds(kind * half, half), span],
            arrived.at[at, kind],
        )
        for kind, weight in enumerate(weights)
    ]


def fetch(weights, held, arrived, first):
    for at in range(held.shape[1] // TILE):
        for copy in copies_of(weights, held, arrived, first, at):
            copy.start()


def multiply(rows_of, weights, held, arrived, first, out_refs):
    tiles = held.shape[1] // TILE
    parts = max(len(pieces) for pieces in out_refs)
    for part in range(parts):

        def step(at, carry, part=part):
            for copy in copies_of(weights, held, arrived, first, at):
                copy.wait()
            span = pl.ds(pl.multiple_of(at * TILE, TILE), TILE)
            result = jnp.dot(rows_of(), held[:, span], preferred_element_type=jnp.float32)
            result = result.astype(jnp.bfloat16)
            for block, pieces in enumerate(out_refs):
                back = part * (tiles // parts) if len(pieces) == parts else 0
                there = pl.ds(pl.multiple_of((at - back) * TILE, TILE), TILE)
                pieces[part if len(pieces) == parts else 0][:, there] = result[
                    block * ROWS : (block + 1) * ROWS
                ]
            return carry

        lax.fori_loop(part * (tiles // parts), (part + 1) * (tiles // parts), step, 0)


def attend_body(order, core_ref, place_ref, *refs):
    blocks = len(RING)
    ins, refs = refs[: -8 - blocks], refs[-8 - blocks :]
    weights, mixed_ref, out_refs = refs[:2], refs[2], refs[3 : 3 + blocks]
    query_ref, own_ref, other_ref, held, arrived = refs[3 + blocks :]
    fetch(weights, held, arrived, 0)
    core = core_ref[0]
    parts = len(ins) // 3
    for kind, whole in enumerate((query_ref, own_ref, other_ref)):
        at = 0
        for part in ins[kind * parts : (kind + 1) * parts]:
            for top in range(0, part.shape[0], ROWS):
                place = pl.ds(pl.multiple_of(place_ref[order[at]] * ROWS, ROWS), ROWS)
                whole[place, :] = part[top : top + ROWS]
                at += 1
    count, qcols = query_ref.shape
    heads = qcols // HEAD
    block = 2 * ROWS
    scale = 1.0 / math.sqrt(HEAD)
    shift = ROWS.bit_length() - 1
    for step in range(count // block):
        rows = slice(step * block, (step + 1) * block)
        span = (step + 1) * block
        query = jnp.concatenate(
            [query_ref[rows, h * HEAD : (h + 1) * HEAD] for h in range(heads)], axis=0
        )
        contract = (((1,), (1,)), ((), ()))
        row = lax.broadcasted_iota(jnp.int32, (block, block), 0)
        col = lax.broadcasted_iota(jnp.int32, (block, block), 1)
        own_seen = jnp.concatenate([col <= row] * heads, axis=0)
        other_seen = jnp.concatenate(
            [jnp.right_shift(col, shift) < jnp.right_shift(row, shift) + core] * heads, axis=0
        )

        def scores_of(ref, seen):
            raw = lax.dot_general(
                query, ref[:span, :HEAD], contract, preferred_element_type=jnp.float32
            )
            tail = jnp.where(seen, raw[:, span - block :], -jnp.inf)
            if span == block:
                return tail
            return jnp.concatenate([raw[:, : span - block], tail], axis=1)

        scores = jnp.concatenate(
            [scores_of(own_ref, own_seen), scores_of(other_ref, other_seen)], axis=1
        )
        peak = jnp.max(scores, axis=-1, keepdims=True)
        probs = jnp.exp((scores - peak) * scale).astype(jnp.bfloat16)
        ones = jnp.ones((span, HEAD), jnp.bfloat16)
        total = jnp.zeros((block * heads, 2 * HEAD), jnp.float32)
        for part, ref in enumerate((own_ref, other_ref)):
            values = jnp.concatenate([ref[:span, HEAD:], ones], axis=1)
            total += jnp.dot(
                probs[:, part * span : (part + 1) * span],
                values,
                preferred_element_type=jnp.float32,
            )
        mixed = (total[:, :HEAD] / total[:, HEAD:]).astype(jnp.bfloat16)
        for part in range(block // ROWS):
            slot = place_ref[8 + step * (block // ROWS) + part]
            place = pl.ds(pl.multiple_of(slot * ROWS, ROWS), ROWS)
            for h in range(heads):
                top = h * block + part * ROWS
                mixed_ref[place, h * HEAD : (h + 1) * HEAD] = mixed[top : top + ROWS]

    multiply(
        lambda: mixed_ref[count // 2 :], weights, held, arrived, 0, [[ref] for ref in out_refs]
    )


def attend(core, places, order, queries, own, other, weights):
    count, qcols = sum(q.shape[0] for q in queries), queries[0].shape[1]
    kcols = own[0].shape[1]
    args = [*queries, *own, *other]
    vmem = pl.BlockSpec(memory_space=pltpu.VMEM)
    depth, width = weights[0].shape
    return pl.pallas_call(
        functools.partial(attend_body, order),
        in_specs=[pl.BlockSpec(memory_space=pltpu.SMEM)] * 2
        + [vmem] * len(args)
        + [pl.BlockSpec(memory_space=pl.ANY)] * 2,
        out_specs=[vmem] * (1 + len(RING)),
        out_shape=[jax.ShapeDtypeStruct((count, qcols), jnp.bfloat16)]
        + [jax.ShapeDtypeStruct((ROWS, width // HALVES), jnp.bfloat16)] * len(RING),
        scratch_shapes=[pltpu.VMEM((count, cols), jnp.bfloat16) for cols in (qcols, kcols, kcols)]
        + [
            pltpu.VMEM((2 * depth, width // HALVES), jnp.bfloat16),
            pltpu.SemaphoreType.DMA((width // HALVES // TILE, 2)),
        ],
        compiler_params=params(56),
        cost_estimate=cost(8 * count * count * qcols, 4 * count * qcols + 4 * depth * width),
        name="attend",
    )(core, places, *args, *weights)


def output_body(side, first, pieces, mixed_ref, *refs):
    weights, out_refs, (held, arrived) = refs[:2], list(refs[2:-2]), refs[-2:]
    fetch(weights, held, arrived, first)
    count = mixed_ref.shape[0] // 2
    outs = [[out_refs.pop(0) for _ in range(piece)] for piece in pieces]
    rows_of = lambda: mixed_ref[side * count : (side + 1) * count]
    multiply(rows_of, weights, held, arrived, first, outs)


def output(mixed, weights, side, first, width, pieces):
    depth = weights[0].shape[0]
    count = mixed.shape[0] // 2
    vmem = pl.BlockSpec(memory_space=pltpu.VMEM)
    widths = [width // piece for piece in pieces for _ in range(piece)]
    result = list(
        pl.pallas_call(
            functools.partial(output_body, side, first, pieces),
            in_specs=[vmem] + [pl.BlockSpec(memory_space=pl.ANY)] * 2,
            out_specs=[vmem] * len(widths),
            out_shape=[jax.ShapeDtypeStruct((ROWS, w), jnp.bfloat16) for w in widths],
            scratch_shapes=[
                pltpu.VMEM((2 * depth, width), jnp.bfloat16),
                pltpu.SemaphoreType.DMA((width // TILE, 2)),
            ],
            compiler_params=params(56),
            cost_estimate=cost(
                4 * count * depth * width, 2 * (2 * depth * width + count * width)
            ),
            name="output",
        )(mixed, *weights)
    )
    return [[result.pop(0) for _ in range(piece)] for piece in pieces]


def mark_body(*refs):
    del refs


def mark(*blocks):
    anywhere = [pl.BlockSpec(memory_space=pl.ANY)] * len(blocks)
    return pl.pallas_call(
        mark_body,
        in_specs=anywhere,
        out_specs=anywhere,
        out_shape=[jax.ShapeDtypeStruct(block.shape, block.dtype) for block in blocks],
        input_output_aliases={at: at for at in range(len(blocks))},
        compiler_params=params(),
        cost_estimate=cost(7e10, 4096),
        name="mark",
    )(*blocks)


def pick_body(below_ref, above_ref, first_ref, second_ref):
    count = first_ref.shape[0]
    first_ref[...] = below_ref[:count]
    second_ref[...] = above_ref[count:]


def pick(below, above):
    shape = jax.ShapeDtypeStruct((below.shape[0] // HALVES, below.shape[1]), below.dtype)
    return pl.pallas_call(
        pick_body,
        out_shape=[shape, shape],
        compiler_params=params(),
        cost_estimate=cost(1e8, 4 * below.size),
        name="pick",
    )(below, above)


def sums_body(shapes, *refs):
    outs = refs[-len(shapes) :]
    first = 0
    for out_ref, (offset, starts) in zip(outs, shapes):
        step = min(ref.shape[1] for ref in refs[first : first + len(starts)])
        for left in range(0, out_ref.shape[1], step):
            total = None
            for at, start in enumerate(starts):
                ref = refs[first + at]
                col = offset + left - start
                if 0 <= col < ref.shape[1]:
                    term = ref[:, col : col + step].astype(jnp.float32)
                    total = term if total is None else total + term
            out_ref[:, left : left + step] = total.astype(jnp.bfloat16)
        first += len(starts)


def sums(*groups, name="sums", after=()):
    args = [array for _, terms in groups for array, _ in terms]
    shapes = tuple((first, tuple(start for _, start in terms)) for (first, _), terms in groups)
    result = pl.pallas_call(
        functools.partial(sums_body, shapes),
        in_specs=[pl.BlockSpec(memory_space=pltpu.VMEM)] * len(args)
        + [pl.BlockSpec(memory_space=pl.ANY)] * len(after),
        out_shape=[
            jax.ShapeDtypeStruct((terms[0][0].shape[0], width), jnp.bfloat16)
            for (_, width), terms in groups
        ],
        compiler_params=params(16),
        cost_estimate=cost(sum(a.size for a in args), 3 * sum(a.size for a in args)),
        name=name,
    )(*args, *after)
    return result if len(groups) > 1 else result[0]


def terms_body(block_ref, codes_ref, exps_ref, *out_refs):
    scale = jnp.exp2(exps_ref[...].astype(jnp.float32))
    lane = lax.broadcasted_iota(jnp.int32, scale.shape, 1)
    count = codes_ref.shape[0]
    for at, out_ref in enumerate(out_refs):
        for side in range(2):
            block = block_ref[2 * at + side]
            cols = pl.ds(pl.multiple_of(block * HEAD, HEAD), HEAD)
            mine = jnp.sum(jnp.where(lane == block, scale, 0.0), axis=1, keepdims=True)
            out_ref[side * count : (side + 1) * count] = (
                codes_ref[:, cols].astype(jnp.float32) * mine
            ).astype(jnp.bfloat16)


def terms(blocks, codes, exps):
    count, width = codes.shape
    vmem = pl.BlockSpec(memory_space=pltpu.VMEM)
    return pl.pallas_call(
        terms_body,
        in_specs=[pl.BlockSpec(memory_space=pltpu.SMEM), vmem, vmem],
        out_shape=[jax.ShapeDtypeStruct((2 * count, HEAD), jnp.bfloat16)] * len(RING),
        compiler_params=params(),
        cost_estimate=cost(codes.size, 4 * codes.size),
        name="terms",
    )(blocks, codes, exps)


def outer_body(replicas, *refs):
    mine_refs, theirs_ref, momentum_ref, table_ref, momentum_out, rebuilt_ref = (
        refs[:3],
        *refs[3:],
    )
    table = table_ref[...]

    def rotate(values):
        return jnp.dot(
            values, table, precision=lax.Precision.HIGHEST, preferred_element_type=jnp.float32
        )

    summed = theirs_ref[...].astype(jnp.float32)
    for ref in mine_refs:
        summed += ref[: summed.shape[0]].astype(jnp.float32)
    averaged = rotate(summed / replicas)
    fresh = 0.9 * momentum_ref[...] + averaged
    momentum_out[...] = fresh
    turned = rotate(0.7 * (averaged + 0.9 * fresh))
    scales = (jnp.max(jnp.abs(turned), axis=-1, keepdims=True) + 1e-06).astype(jnp.bfloat16)
    scales = scales.astype(jnp.float32)
    codes = (turned / scales).astype(jnp.bfloat16)
    rebuilt_ref[...] = rotate(codes.astype(jnp.float32) * scales).astype(jnp.bfloat16)


def outer(mine, theirs, momentum, table, replicas):
    return pl.pallas_call(
        functools.partial(outer_body, replicas),
        out_shape=[
            jax.ShapeDtypeStruct(momentum.shape, jnp.float32),
            jax.ShapeDtypeStruct(momentum.shape, jnp.bfloat16),
        ],
        compiler_params=params(),
        cost_estimate=cost(40 * theirs.size * HEAD, 12 * theirs.size),
        name="outer",
    )(*mine, theirs, momentum, table)


def apply_body(block_ref, params_ref, *refs):
    rebuilt_refs, out_ref = refs[:-1], refs[-1]
    count = out_ref.shape[0]
    for at, rebuilt_ref in enumerate(rebuilt_refs):
        for side in range(2):
            cols = pl.ds(pl.multiple_of(block_ref[2 * at + side] * HEAD, HEAD), HEAD)
            rebuilt = rebuilt_ref[side * count : (side + 1) * count].astype(jnp.float32)
            out_ref[:, cols] = (params_ref[:, cols].astype(jnp.float32) - rebuilt).astype(
                jnp.bfloat16
            )


def apply(blocks, old, rebuilt):
    vmem = pl.BlockSpec(memory_space=pltpu.VMEM)
    return pl.pallas_call(
        apply_body,
        in_specs=[pl.BlockSpec(memory_space=pltpu.SMEM)] + [vmem] * (1 + len(rebuilt)),
        out_shape=jax.ShapeDtypeStruct(old.shape, jnp.bfloat16),
        compiler_params=params(),
        cost_estimate=cost(old.size, 6 * old.size),
        name="apply",
    )(blocks, old, *rebuilt)


def swap(block, axis):
    return lax.ppermute(block, axis, [(0, 1), (1, 0)])


def hop(block, axis, way):
    at = (0, 2, 1, 3) if axis == Y else (0, 1, 2, 3)
    return lax.ppermute(block, axis, [(at[i], at[(i + way) % 4]) for i in range(4)])


def add(*blocks):
    total = blocks[0].astype(jnp.float32)
    for block in blocks[1:]:
        total = total + block.astype(jnp.float32)
    return total.astype(jnp.bfloat16)


def wait(*blocks):
    return lax.optimization_barrier(blocks)


def tie(block, *others):
    return lax.optimization_barrier((block, *others))[0]


def local(
    tokens, norm_gain, query_weight, kv_weight, out_weight, pseudo_grad, grad_exps, old, momentum
):
    core, z, yhi = lax.axis_index("core"), lax.axis_index("z"), lax.axis_index("yhi")
    x, ylo = lax.axis_index("x"), lax.axis_index("ylo")
    replicas = lax.axis_size(REPLICA)
    place = jnp.stack([(yhi ^ side) * 4 + (z + r) % 4 for side in range(2) for r in RING])
    chip = jnp.arange(8, dtype=jnp.int32)
    away = (chip % 4 - z) % 4
    slots = ((chip // 4) ^ yhi) * 4 + jnp.where(away < 2, away, 5 - away)
    share = jnp.stack([((x + r) % 4) * 2 + (ylo ^ side) for r in RING for side in range(2)])
    core, place, slots, share = (
        v.astype(jnp.int32).reshape(-1) for v in (core, place, slots, share)
    )
    places = jnp.concatenate([place, slots])

    block, h1, h2 = normalize(tokens, norm_gain)
    relay1, relay2 = hop(h1, Y, 1), hop(h2, Y, -1)
    below, above = hop(block, "z", 1), hop(block, "z", -1)
    kv_theirs = swap(tie(kv_weight, block), "core")
    at0, at1, at3, at2 = terms(share, tie(pseudo_grad[0], block), grad_exps[0])
    relay1, relay2, kv_theirs, at0, at1, at2, at3, query_weight = wait(
        relay1, relay2, kv_theirs, at0, at1, at2, at3, query_weight
    )
    query_theirs = swap(query_weight, "core")
    partner = jnp.concatenate([hop(relay1, Y, 1), hop(relay2, Y, -1)], axis=0)
    below, above = mark(below, above)
    far1, far2 = pick(below, above)
    partner, above, below = wait(partner, above, below)
    far1, far2 = hop(far1, "z", 1), hop(far2, "z", -1)
    pbelow, pabove = hop(partner, "z", 1), hop(partner, "z", -1)
    weights = [query_weight, query_theirs, kv_weight, kv_theirs]
    query_a, pair_a = project(core, [block, above, below, far1, far2], weights)
    query_a, far1, far2, at2, at3 = wait(query_a, far1, far2, at2, at3)
    x2, x3 = hop(at2, "x", 1), hop(at3, "x", -1)
    pabove, pbelow, query_a, pair_a, x2, x3, at1, out_weight = wait(
        pabove, pbelow, query_a, pair_a, x2, x3, at1, out_weight
    )
    pfar1, pfar2 = pick(pbelow, pabove)
    pfar1, pfar2 = hop(pfar1, "z", 1), hop(pfar2, "z", -1)
    out_theirs = swap(out_weight, "core")
    query_m, pair_m = project(core, [partner, pabove, pbelow], weights)
    passed = hop(add(at1, x2), "x", 1)
    other_a, other_m = swap(pair_a, "core"), swap(pair_m, "core")
    pfar1, pfar2, passed, query_m = wait(pfar1, pfar2, passed, query_m)
    query_l, pair_l = project(core, [pfar1, pfar2], weights)
    other_l = swap(pair_l, "core")
    out_weights = (out_weight, out_theirs)
    mixed, q0a, qupa, qdowna, qfara = attend(
        core,
        places,
        tuple(range(8)),
        (query_a, query_m, query_l),
        (pair_a, pair_m, pair_l),
        (other_a, other_m, other_l),
        out_weights,
    )

    full = out_weight.shape[1]
    half = full // HALVES
    mixed, far_a = wait(mixed, qfara)
    far_a = hop(far_a, "z", 1)
    (q0b,), (qupb,), (qdownb,), (qfarb,) = output(mixed, out_weights, 1, half, half, (1, 1, 1, 1))
    far_b = hop(qfarb, "z", -1)
    mine = (at0, passed, x3)
    count = momentum.shape[0]
    sent, q0b, mixed = wait(add(*(part[count:] for part in mine)), q0b, mixed)
    theirs = swap(sent, "ylo")
    (o0,), (oup,), (odown,), (ofara, ofarb) = output(mixed, out_weights, 0, 0, full, (1, 1, 1, 2))
    far_a, far_b, o0 = wait(far_a, far_b, o0)
    up, down = sums(
        ((0, full), ((qupa, 0), (qupb, half), (far_a, 0))),
        ((0, full), ((qdowna, 0), (qdownb, half), (far_b, half))),
    )
    up, down, theirs, ofara, ofarb = wait(up, down, theirs, ofara, ofarb)
    up, down = hop(up, "z", 1), hop(down, "z", -1)
    ofara, ofarb = hop(ofara, "z", 1), hop(ofarb, "z", -1)
    new_momentum, rebuilt = outer(mine, theirs, momentum, hadamard_table(HEAD), replicas)
    beside = swap(rebuilt, "ylo")
    both = jnp.concatenate([rebuilt, beside], axis=0)
    before = hop(both, "x", 1)
    up, down, before, both = wait(up, down, before, both)
    s1, s2 = sums(
        *(((at, half), ((q0a, 0), (q0b, half), (up, 0), (down, 0))) for at in (0, half))
    )
    oup, odown = sums(
        ((0, full), ((oup, 0), (ofara, 0))),
        ((0, full), ((odown, 0), (ofarb, half))),
        after=(s1,),
    )
    oup, odown = hop(oup, "z", 1), hop(odown, "z", -1)
    s1, s2 = hop(s1, Y, 1), hop(s2, Y, -1)
    after = hop(both, "x", -1)
    s1, s2, before = wait(s1, s2, before)
    s1, s2 = hop(s1, Y, 1), hop(s2, Y, -1)
    ahead = hop(before, "x", 1)
    new_params = apply(share, old, [both, after, before, ahead])
    o0, new_params = wait(o0, new_params)
    attended = sums(
        ((0, full), ((o0, 0), (oup, 0), (odown, 0), (s1, 0), (s2, half))), name="finish"
    )
    return (attended, new_params, new_momentum)


def solution(mesh):
    fine = Mesh(mesh.devices.reshape(4, 2, 2, 4, 2), ("x", "ylo", "yhi", "z", "core"))
    every = REPLICA + TENSOR
    return jax.shard_map(
        local,
        mesh=fine,
        in_specs=(
            P(every, None),
            P(),
            P(None, TENSOR),
            P(None, TENSOR),
            P(TENSOR, None),
            P(REPLICA, TENSOR, None),
            P(REPLICA, TENSOR, None),
            P(TENSOR, None),
            P(TENSOR, REPLICA),
        ),
        out_specs=(P(every, None), P(TENSOR, None), P(TENSOR, REPLICA)),
        check_vma=False,
    )
```

profile of v0, /device:TPU:0, one launch (start us, length us, event | category | flops | bytes accessed | tf_op | source)
XLA Modules:
  0.0 201.7 jit_solution(870006036092967445)
XLA Ops:
  0.7 1.3 copy-done.8
  2.0 0.8 copy-done.18
  2.7 1.8 normalize.1
  4.5 1.7 collective-permute-start
  6.1 1.6 collective-permute-start.1
  7.7 2.0 collective-permute-start.5
  9.7 2.1 %collective-permute-start.6 = (bf16[64,8192]{1,0:T(8,128)(2,1)}, bf16[64,8192]{1,0:T(8,128)(2,1)}, u32[]{:S(2)}, u32[]{:S(2)}) collective-permute-start(bf16[64,8192]{1,0:T(8,128)(2,1)} %get-tuple-element.96.refs_0_), channel_id=1, source_target_pairs={{0,6},{2,0},{4,2},{6,4},{1,7},{3,1},{5,3},{7,5},{8,14},{10,8},{12,... | collective-permute-start | bytes 3145736 | tf_op jit(solution)/shard_map/ppermute | solution.py:469
  11.8 0.8 copy.14
  12.8 1.2 terms.1
  14.0 6.5 %collective-permute-done = bf16[32,8192]{1,0:T(8,128)(2,1)} collective-permute-done((bf16[32,8192]{1,0:T(8,128)(2,1)}, bf16[32,8192]{1,0:T(8,128)(2,1)}, u32[]{:S(2)}, u32[]{:S(2)}) %collective-permute-start) | collective-permute-done | bytes 524320 | tf_op jit(solution)/shard_map/ppermute | solution.py:469
  20.5 2.7 %collective-permute-start.4 = (bf16[32,8192]{1,0:T(8,128)(2,1)}, bf16[32,8192]{1,0:T(8,128)(2,1)S(1)}, u32[]{:S(2)}, u32[]{:S(2)}) collective-permute-start(bf16[32,8192]{1,0:T(8,128)(2,1)} %collective-permute-done.1), channel_id=1, source_target_pairs={{0,24},{16,0},{8,16},{24,8},{1,25},{17,1},{9,17},{25,9},{2,26},{18... | collective-permute-start | bytes 1572872 | tf_op jit(solution)/shard_map/ppermute | solution.py:469
  23.2 12.1 %collective-permute-done.5.refs_0_ = bf16[64,8192]{1,0:T(8,128)(2,1)S(1)} collective-permute-done((bf16[64,8192]{1,0:T(8,128)(2,1)}, bf16[64,8192]{1,0:T(8,128)(2,1)S(1)}, u32[]{:S(2)}, u32[]{:S(2)}) %collective-permute-start.5) | collective-permute-done | bytes 1048608 | tf_op jit(solution)/shard_map/ppermute | solution.py:469
  35.4 2.6 %pick.2 = (bf16[32,8192]{1,0:T(8,128)(2,1)}, bf16[32,8192]{1,0:T(8,128)(2,1)}) custom-call(bf16[64,8192]{1,0:T(8,128)(2,1)S(1)} %get-tuple-element.109.below_ref.refs_2_, bf16[64,8192]{1,0:T(8,128)(2,1)} %get-tuple-element.108.above_ref.refs_1_), custom_call_target="tpu_custom_call" | custom-call | flops 100000000 | bytes 2097152 | tf_op jit(solution)/shard_map/pick/pallas_call | solution.py:330
  38.0 1.4 collective-permute-start.9
  39.4 1.9 collective-permute-start.10
  41.3 1.1 pad_maximum_fusion.refs_0_
  42.3 1.8 collective-permute-start.7
  44.4 10.0 %collective-permute-done.9.refs_3_ = bf16[32,8192]{1,0:T(8,128)(2,1)} collective-permute-done((bf16[32,8192]{1,0:T(8,128)(2,1)}, bf16[32,8192]{1,0:T(8,128)(2,1)}, u32[]{:S(2)}, u32[]{:S(2)}) %collective-permute-start.9) | collective-permute-done | bytes 524320 | tf_op jit(solution)/shard_map/ppermute | solution.py:469
  54.6 12.1 %project.3 = (bf16[256,1024]{1,0:T(8,128)(2,1)}, bf16[256,256]{1,0:T(8,128)(2,1)}) custom-call(s32[1]{0:T(128)} %bitcast.core_ref, bf16[64,8192]{1,0:T(8,128)(2,1)} %get-tuple-element.96.refs_0_, bf16[64,8192]{1,0:T(8,128)(2,1)} %get-tuple-element.108.above_ref.refs_1_, bf16[64,8192]{1,0:T(8,128)(2,1)} %copy-done.10, ...), custom_call_target="tpu_custom_call" | custom-call | flops 8053063680 | bytes 25165824 | tf_op jit(solution)/shard_map/project/pallas_call | solution.py:113
  66.7 1.6 collective-permute-start.12
  68.2 1.7 collective-permute-start.13
  70.0 4.6 %collective-permute-done.7.above_ref.refs_1_ = bf16[64,8192]{1,0:T(8,128)(2,1)S(1)} collective-permute-done((bf16[64,8192]{1,0:T(8,128)(2,1)}, bf16[64,8192]{1,0:T(8,128)(2,1)S(1)}, u32[]{:S(2)}, u32[]{:S(2)}) %collective-permute-start.7) | collective-permute-done | bytes 1048608 | tf_op jit(solution)/shard_map/ppermute | solution.py:469
  74.6 0.6 collective-permute-done.8.below_ref.refs_2_
  75.2 0.7 copy-done.25
  76.1 1.0 collective-permute-start.14
  77.0 2.3 %collective-permute-start.15 = (bf16[32,8192]{1,0:T(8,128)(2,1)S(1)}, bf16[32,8192]{1,0:T(8,128)(2,1)S(1)}, u32[]{:S(2)}, u32[]{:S(2)}) collective-permute-start(bf16[32,8192]{1,0:T(8,128)(2,1)S(1)} %get-tuple-element.126), channel_id=1, source_target_pairs={{0,6},{2,0},{4,2},{6,4},{1,7},{3,1},{5,3},{7,5},{8,14},{10,8},{12,... | collective-permute-start | bytes 1572872 | tf_op jit(solution)/shard_map/ppermute | solution.py:469
  79.4 1.6 collective-permute-start.16
  81.0 10.6 %project.4 = (bf16[192,1024]{1,0:T(8,128)(2,1)}, bf16[192,256]{1,0:T(8,128)(2,1)}) custom-call(s32[1]{0:T(128)} %bitcast.core_ref, bf16[64,8192]{1,0:T(8,128)(2,1)} %pad_maximum_fusion.refs_0_, bf16[64,8192]{1,0:T(8,128)(2,1)} %copy-done, bf16[64,8192]{1,0:T(8,128)(2,1)} %copy-done.1, bf16[8192,512]{1,0:T(8,128)(2,1)} %refs_2_, ...), custom_call_target="tpu_custom_call" | custom-call | flops 6039797760 | bytes 24117248 | tf_op jit(solution)/shard_map/project/pallas_call | solution.py:113
  91.6 0.6 collective-permute-start.18
  92.3 0.8 copy-done.23
  93.2 9.6 %project.5 = (bf16[64,1024]{1,0:T(8,128)(2,1)}, bf16[64,256]{1,0:T(8,128)(2,1)}) custom-call(s32[1]{0:T(128)} %bitcast.core_ref, bf16[32,8192]{1,0:T(8,128)(2,1)} %copy-done.23, bf16[32,8192]{1,0:T(8,128)(2,1)} %copy-done.24, bf16[8192,512]{1,0:T(8,128)(2,1)} %refs_2_, bf16[8192,512]{1,0:T(8,128)(2,1)} %collective-permute-done.11.refs_6_.refs_4_.refs_3_, ...), custom_call_target="tpu_custom_call" | custom-call | flops 2013265920 | bytes 22020096 | tf_op jit(solution)/shard_map/project/pallas_call | solution.py:113
  103.2 0.6 concatenate.9.place_ref
  103.8 0.7 collective-permute-done.19.refs_8_
  104.5 0.6 copy-done.29
  105.1 10.5 %attend.1 = (bf16[512,1024]{1,0:T(8,128)(2,1)}, bf16[64,4096]{1,0:T(8,128)(2,1)}, bf16[64,4096]{1,0:T(8,128)(2,1)}, bf16[64,4096]{1,0:T(8,128)(2,1)}, bf16[64,4096]{1,0:T(8,128)(2,1)}) custom-call(s32[1]{0:T(128)} %bitcast.core_ref, s32[16]{0:T(128)} %concatenate.9.place_ref, bf16[256,1024]{1,0:T(8,128)(2,1)} %get-tuple-element.122.refs_0_, ...), custom_call_target="tpu_custom_call" | custom-call | flops 2147483648 | bytes 18874368 | tf_op jit(solution)/shard_map/attend/pallas_call | solution.py:251
  115.7 0.5 collective-permute-start.21
  116.2 7.0 %output.2 = (bf16[64,4096]{1,0:T(8,128)(2,1)}, bf16[64,4096]{1,0:T(8,128)(2,1)}, bf16[64,4096]{1,0:T(8,128)(2,1)}, bf16[64,4096]{1,0:T(8,128)(2,1)}) custom-call(bf16[512,1024]{1,0:T(8,128)(2,1)} %get-tuple-element.147.mixed_ref, bf16[512,8192]{1,0:T(8,128)(2,1)} %refs_0_.1, bf16[512,8192]{1,0:T(8,128)(2,1)} %collective-permute-done.20.refs_10_.refs_1_), custom_call_target="tpu_custom_call" | custom-call | flops 2147483648 | bytes 10485760 | tf_op jit(solution)/shard_map/output/pallas_call | solution.py:285
  123.2 2.9 %collective-permute-start.22 = (bf16[64,4096]{1,0:T(8,128)(2,1)}, bf16[64,4096]{1,0:T(8,128)(2,1)S(1)}, u32[]{:S(2)}, u32[]{:S(2)}) collective-permute-start(bf16[64,4096]{1,0:T(8,128)(2,1)} %get-tuple-element.142), channel_id=1, source_target_pairs={{0,6},{2,0},{4,2},{6,4},{1,7},{3,1},{5,3},{7,5},{8,14},{10,8},{12,... | collective-permute-start | bytes 1572872 | tf_op jit(solution)/shard_map/ppermute | solution.py:469
  126.5 10.7 %output.3 = (bf16[64,8192]{1,0:T(8,128)(2,1)}, bf16[64,8192]{1,0:T(8,128)(2,1)}, bf16[64,8192]{1,0:T(8,128)(2,1)}, bf16[64,4096]{1,0:T(8,128)(2,1)}, bf16[64,4096]{1,0:T(8,128)(2,1)}) custom-call(bf16[512,1024]{1,0:T(8,128)(2,1)} %get-tuple-element.147.mixed_ref, bf16[512,8192]{1,0:T(8,128)(2,1)} %refs_0_.1, ...), custom_call_target="tpu_custom_call" | custom-call | flops 4294967296 | bytes 20971520 | tf_op jit(solution)/shard_map/output/pallas_call | solution.py:285
  137.2 0.4 collective-permute-done.22.refs_5_
  138.0 1.4 collective-permute-start.24
  139.3 2.4 %collective-permute-start.25 = (bf16[64,8192]{1,0:T(8,128)(2,1)S(1)}, bf16[64,8192]{1,0:T(8,128)(2,1)S(1)}, u32[]{:S(2)}, u32[]{:S(2)}) collective-permute-start(bf16[64,8192]{1,0:T(8,128)(2,1)S(1)} %get-tuple-element.162), channel_id=1, source_target_pairs={{0,6},{2,0},{4,2},{6,4},{1,7},{3,1},{5,3},{7,5},{8,14},{10,8},{12,... | collective-permute-start | bytes 3145736 | tf_op jit(solution)/shard_map/ppermute | solution.py:469
  141.9 3.2 %collective-permute-start.33 = (bf16[64,4096]{1,0:T(8,128)(2,1)S(1)}, bf16[64,4096]{1,0:T(8,128)(2,1)S(1)}, u32[]{:S(2)}, u32[]{:S(2)}) collective-permute-start(bf16[64,4096]{1,0:T(8,128)(2,1)S(1)} %copy-done.30), channel_id=1, source_target_pairs={{0,6},{2,0},{4,2},{6,4},{1,7},{3,1},{5,3},{7,5},{8,14},{10,8},{12,... | collective-permute-start | bytes 1572872 | tf_op jit(solution)/shard_map/ppermute | solution.py:469
  145.1 1.5 outer.1
  146.6 0.9 collective-permute-start.26
  147.5 4.1 %collective-permute-done.26 = bf16[512,128]{1,0:T(8,128)(2,1)S(1)} collective-permute-done((bf16[512,128]{1,0:T(8,128)(2,1)S(1)}, bf16[512,128]{1,0:T(8,128)(2,1)S(1)}, u32[]{:S(2)}, u32[]{:S(2)}) %collective-permute-start.26) | collective-permute-done | bytes 131104 | tf_op jit(solution)/shard_map/ppermute | solution.py:464
  151.6 1.6 collective-permute-start.27
  153.2 6.1 %collective-permute-done.27.refs_2_ = bf16[1024,128]{1,0:T(8,128)(2,1)S(1)} collective-permute-done((bf16[1024,128]{1,0:T(8,128)(2,1)S(1)}, bf16[1024,128]{1,0:T(8,128)(2,1)S(1)}, u32[]{:S(2)}, u32[]{:S(2)}) %collective-permute-start.27) | collective-permute-done | bytes 262176 | tf_op jit(solution)/shard_map/ppermute | solution.py:469
  159.3 6.4 %collective-permute-done.24.refs_2_.refs_6_ = bf16[64,8192]{1,0:T(8,128)(2,1)S(1)} collective-permute-done((bf16[64,8192]{1,0:T(8,128)(2,1)S(1)}, bf16[64,8192]{1,0:T(8,128)(2,1)S(1)}, u32[]{:S(2)}, u32[]{:S(2)}) %collective-permute-start.24) | collective-permute-done | bytes 1048608 | tf_op jit(solution)/shard_map/ppermute | solution.py:469
  165.7 0.4 sums.4
  166.1 1.2 collective-permute-start.29
  167.3 2.3 %collective-permute-start.30 = (bf16[64,4096]{1,0:T(8,128)(2,1)S(1)}, bf16[64,4096]{1,0:T(8,128)(2,1)S(1)}, u32[]{:S(2)}, u32[]{:S(2)}) collective-permute-start(bf16[64,4096]{1,0:T(8,128)(2,1)S(1)} %get-tuple-element.171), channel_id=1, source_target_pairs={{0,24},{16,0},{8,16},{24,8},{1,25},{17,1},{9,17},{25,9},{2,26},{18... | collective-permute-start | bytes 1572872 | tf_op jit(solution)/shard_map/ppermute | solution.py:469
  169.6 5.5 %collective-permute-done.32.refs_1_ = bf16[64,4096]{1,0:T(8,128)(2,1)S(1)} collective-permute-done((bf16[64,4096]{1,0:T(8,128)(2,1)S(1)}, bf16[64,4096]{1,0:T(8,128)(2,1)S(1)}, u32[]{:S(2)}, u32[]{:S(2)}) %collective-permute-start.32) | collective-permute-done | bytes 524320 | tf_op jit(solution)/shard_map/ppermute | solution.py:469
  175.5 1.2 collective-permute-start.34
  176.7 2.1 %collective-permute-start.35 = (bf16[64,8192]{1,0:T(8,128)(2,1)S(1)}, bf16[64,8192]{1,0:T(8,128)(2,1)S(1)}, u32[]{:S(2)}, u32[]{:S(2)}) collective-permute-start(bf16[64,8192]{1,0:T(8,128)(2,1)S(1)} %get-tuple-element.180), channel_id=1, source_target_pairs={{0,6},{2,0},{4,2},{6,4},{1,7},{3,1},{5,3},{7,5},{8,14},{10,8},{12,... | collective-permute-start | bytes 3145736 | tf_op jit(solution)/shard_map/ppermute | solution.py:469
  178.8 2.2 %collective-permute-start.28 = (bf16[1024,128]{1,0:T(8,128)(2,1)S(1)}, bf16[1024,128]{1,0:T(8,128)(2,1)S(1)}, u32[]{:S(2)}, u32[]{:S(2)}) collective-permute-start(bf16[1024,128]{1,0:T(8,128)(2,1)S(1)} %constant_dynamic-update-slice_fusion.refs_0_), channel_id=1, source_target_pairs={{0,96},{32,0},{64,32},{96,64},{1,97},{33,1},{65,33},{97,65},{2,98}... | collective-permute-start | bytes 786440 | tf_op jit(solution)/shard_map/ppermute | solution.py:469
  181.0 0.9 collective-permute-start.36
  181.9 2.3 %collective-permute-start.37 = (bf16[64,4096]{1,0:T(8,128)(2,1)S(1)}, bf16[64,4096]{1,0:T(8,128)(2,1)S(1)}, u32[]{:S(2)}, u32[]{:S(2)}) collective-permute-start(bf16[64,4096]{1,0:T(8,128)(2,1)S(1)} %collective-permute-done.30), channel_id=1, source_target_pairs={{0,24},{16,0},{8,16},{24,8},{1,25},{17,1},{9,17},{25,9},{2,26},{18... | collective-permute-start | bytes 1572872 | tf_op jit(solution)/shard_map/ppermute | solution.py:469
  184.2 0.9 collective-permute-done.28.refs_1_
  185.2 1.5 collective-permute-start.31
  186.7 6.3 %collective-permute-done.31.refs_3_ = bf16[1024,128]{1,0:T(8,128)(2,1)S(1)} collective-permute-done((bf16[1024,128]{1,0:T(8,128)(2,1)S(1)}, bf16[1024,128]{1,0:T(8,128)(2,1)S(1)}, u32[]{:S(2)}, u32[]{:S(2)}) %collective-permute-start.31) | collective-permute-done | bytes 262176 | tf_op jit(solution)/shard_map/ppermute | solution.py:469
  192.9 1.8 apply.1
  194.8 5.4 %collective-permute-done.34.refs_1_ = bf16[64,8192]{1,0:T(8,128)(2,1)S(1)} collective-permute-done((bf16[64,8192]{1,0:T(8,128)(2,1)S(1)}, bf16[64,8192]{1,0:T(8,128)(2,1)S(1)}, u32[]{:S(2)}, u32[]{:S(2)}) %collective-permute-start.34) | collective-permute-done | bytes 1048608 | tf_op jit(solution)/shard_map/ppermute | solution.py:469
  200.2 1.5 finish.1
  (103 shorter events, 2.3 us)
Async XLA Ops:
  0.6 12.1 %copy-start.7 = (bf16[1,512,1024]{2,1,0:T(8,128)(2,1)S(1)}, bf16[1,512,1024]{2,1,0:T(8,128)(2,1)}, u32[]{:S(2)}) copy-start(bf16[1,512,1024]{2,1,0:T(8,128)(2,1)} %param.14) | copy-start | bytes 3145732
  0.6 1.3 copy-start.8
  4.5 16.0 %collective-permute-start.2 = (bf16[8192,128]{1,0:T(8,128)(2,1)}, bf16[8192,128]{1,0:T(8,128)(2,1)}, u32[]{:S(2)}, u32[]{:S(2)}) collective-permute-start(bf16[8192,128]{1,0:T(8,128)(2,1)} %refs_4_.2), channel_id=1, source_target_pairs={{0,1},{1,0},{2,3},{3,2},{4,5},{5,4},{6,7},{7,6},{8,9},{9,8},{10,11... | collective-permute-start | bytes 6291464 | tf_op jit(solution)/shard_map/ppermute | solution.py:464
  4.5 16.0 %collective-permute-start = (bf16[32,8192]{1,0:T(8,128)(2,1)}, bf16[32,8192]{1,0:T(8,128)(2,1)}, u32[]{:S(2)}, u32[]{:S(2)}) collective-permute-start(bf16[32,8192]{1,0:T(8,128)(2,1)} %get-tuple-element.94), channel_id=1, source_target_pairs={{0,16},{16,8},{8,24},{24,0},{1,17},{17,9},{9,25},{25,1},{2,18},{18... | collective-permute-start | bytes 1572872 | tf_op jit(solution)/shard_map/ppermute | solution.py:469
  6.1 14.3 %collective-permute-start.1 = (bf16[32,8192]{1,0:T(8,128)(2,1)S(1)}, bf16[32,8192]{1,0:T(8,128)(2,1)}, u32[]{:S(2)}, u32[]{:S(2)}) collective-permute-start(bf16[32,8192]{1,0:T(8,128)(2,1)S(1)} %get-tuple-element.95), channel_id=1, source_target_pairs={{0,24},{16,0},{8,16},{24,8},{1,25},{17,1},{9,17},{25,9},{2,26},{18... | collective-permute-start | bytes 1572872 | tf_op jit(solution)/shard_map/ppermute | solution.py:469
  7.7 27.6 %collective-permute-start.5 = (bf16[64,8192]{1,0:T(8,128)(2,1)}, bf16[64,8192]{1,0:T(8,128)(2,1)S(1)}, u32[]{:S(2)}, u32[]{:S(2)}) collective-permute-start(bf16[64,8192]{1,0:T(8,128)(2,1)} %get-tuple-element.96.refs_0_), channel_id=1, source_target_pairs={{0,2},{2,4},{4,6},{6,0},{1,3},{3,5},{5,7},{7,1},{8,10},{10,12},{12... | collective-permute-start | bytes 3145736 | tf_op jit(solution)/shard_map/ppermute | solution.py:469
  9.7 25.7 %collective-permute-start.6 = (bf16[64,8192]{1,0:T(8,128)(2,1)}, bf16[64,8192]{1,0:T(8,128)(2,1)}, u32[]{:S(2)}, u32[]{:S(2)}) collective-permute-start(bf16[64,8192]{1,0:T(8,128)(2,1)} %get-tuple-element.96.refs_0_), channel_id=1, source_target_pairs={{0,6},{2,0},{4,2},{6,4},{1,7},{3,1},{5,3},{7,5},{8,14},{10,8},{12,... | collective-permute-start | bytes 3145736 | tf_op jit(solution)/shard_map/ppermute | solution.py:469
  13.9 21.4 %copy-start.16 = (bf16[1024,128]{1,0:T(8,128)(2,1)}, bf16[1024,128]{1,0:T(8,128)(2,1)S(1)}, u32[]{:S(2)}) copy-start(bf16[1024,128]{1,0:T(8,128)(2,1)S(1)} %get-tuple-element.127) | copy-start | bytes 786436
  14.0 21.4 %copy-start.19 = (bf16[1024,128]{1,0:T(8,128)(2,1)}, bf16[1024,128]{1,0:T(8,128)(2,1)S(1)}, u32[]{:S(2)}) copy-start(bf16[1024,128]{1,0:T(8,128)(2,1)S(1)} %get-tuple-element.120) | copy-start | bytes 786436
  14.0 21.4 %copy-start.21 = (bf16[1024,128]{1,0:T(8,128)(2,1)}, bf16[1024,128]{1,0:T(8,128)(2,1)S(1)}, u32[]{:S(2)}) copy-start(bf16[1024,128]{1,0:T(8,128)(2,1)S(1)} %get-tuple-element.119) | copy-start | bytes 786436
  20.5 34.1 %collective-permute-start.11 = (bf16[8192,512]{1,0:T(8,128)(2,1)}, bf16[8192,512]{1,0:T(8,128)(2,1)}, u32[]{:S(2)}, u32[]{:S(2)}) collective-permute-start(bf16[8192,512]{1,0:T(8,128)(2,1)} %refs_2_), channel_id=1, source_target_pairs={{0,1},{1,0},{2,3},{3,2},{4,5},{5,4},{6,7},{7,6},{8,9},{9,8},{10,11... | collective-permute-start | bytes 25165832 | tf_op jit(solution)/shard_map/ppermute | solution.py:464
  20.5 20.8 %collective-permute-start.4 = (bf16[32,8192]{1,0:T(8,128)(2,1)}, bf16[32,8192]{1,0:T(8,128)(2,1)S(1)}, u32[]{:S(2)}, u32[]{:S(2)}) collective-permute-start(bf16[32,8192]{1,0:T(8,128)(2,1)} %collective-permute-done.1), channel_id=1, source_target_pairs={{0,24},{16,0},{8,16},{24,8},{1,25},{17,1},{9,17},{25,9},{2,26},{18... | collective-permute-start | bytes 1572872 | tf_op jit(solution)/shard_map/ppermute | solution.py:469
  23.2 18.0 %collective-permute-start.3 = (bf16[32,8192]{1,0:T(8,128)(2,1)}, bf16[32,8192]{1,0:T(8,128)(2,1)S(1)}, u32[]{:S(2)}, u32[]{:S(2)}) collective-permute-start(bf16[32,8192]{1,0:T(8,128)(2,1)} %collective-permute-done), channel_id=1, source_target_pairs={{0,16},{16,8},{8,24},{24,0},{1,17},{17,9},{9,25},{25,1},{2,18},{18... | collective-permute-start | bytes 1572872 | tf_op jit(solution)/shard_map/ppermute | solution.py:469
  35.4 7.0 %copy-start.10 = (bf16[64,8192]{1,0:T(8,128)(2,1)}, bf16[64,8192]{1,0:T(8,128)(2,1)S(1)}, u32[]{:S(2)}) copy-start(bf16[64,8192]{1,0:T(8,128)(2,1)S(1)} %get-tuple-element.109.below_ref.refs_2_) | copy-start | bytes 3145732
  38.0 16.4 %collective-permute-start.9 = (bf16[32,8192]{1,0:T(8,128)(2,1)}, bf16[32,8192]{1,0:T(8,128)(2,1)}, u32[]{:S(2)}, u32[]{:S(2)}) collective-permute-start(bf16[32,8192]{1,0:T(8,128)(2,1)} %get-tuple-element.110), channel_id=1, source_target_pairs={{0,2},{2,4},{4,6},{6,0},{1,3},{3,5},{5,7},{7,1},{8,10},{10,12},{12... | collective-permute-start | bytes 1572872 | tf_op jit(solution)/shard_map/ppermute | solution.py:469
  39.4 15.2 %collective-permute-start.10 = (bf16[32,8192]{1,0:T(8,128)(2,1)}, bf16[32,8192]{1,0:T(8,128)(2,1)}, u32[]{:S(2)}, u32[]{:S(2)}) collective-permute-start(bf16[32,8192]{1,0:T(8,128)(2,1)} %get-tuple-element.111), channel_id=1, source_target_pairs={{0,6},{2,0},{4,2},{6,4},{1,7},{3,1},{5,3},{7,5},{8,14},{10,8},{12,... | collective-permute-start | bytes 1572872 | tf_op jit(solution)/shard_map/ppermute | solution.py:469
  42.3 32.2 %collective-permute-start.7 = (bf16[64,8192]{1,0:T(8,128)(2,1)}, bf16[64,8192]{1,0:T(8,128)(2,1)S(1)}, u32[]{:S(2)}, u32[]{:S(2)}) collective-permute-start(bf16[64,8192]{1,0:T(8,128)(2,1)} %pad_maximum_fusion.refs_0_), channel_id=1, source_target_pairs={{0,6},{2,0},{4,2},{6,4},{1,7},{3,1},{5,3},{7,5},{8,14},{10,8},{12,... | collective-permute-start | bytes 3145736 | tf_op jit(solution)/shard_map/ppermute | solution.py:469
  44.2 31.0 %collective-permute-start.8 = (bf16[64,8192]{1,0:T(8,128)(2,1)}, bf16[64,8192]{1,0:T(8,128)(2,1)S(1)}, u32[]{:S(2)}, u32[]{:S(2)}) collective-permute-start(bf16[64,8192]{1,0:T(8,128)(2,1)} %pad_maximum_fusion.refs_0_), channel_id=1, source_target_pairs={{0,2},{2,4},{4,6},{6,0},{1,3},{3,5},{5,7},{7,1},{8,10},{10,12},{12... | collective-permute-start | bytes 3145736 | tf_op jit(solution)/shard_map/ppermute | solution.py:469
  54.6 12.1 %copy-start.22 = (bf16[1024,128]{1,0:T(8,128)(2,1)S(1)}, bf16[1024,128]{1,0:T(8,128)(2,1)}, u32[]{:S(2)}) copy-start(bf16[1024,128]{1,0:T(8,128)(2,1)} %copy-done.21) | copy-start | bytes 786436
  54.6 13.7 %copy-start.20 = (bf16[1024,128]{1,0:T(8,128)(2,1)S(1)}, bf16[1024,128]{1,0:T(8,128)(2,1)}, u32[]{:S(2)}) copy-start(bf16[1024,128]{1,0:T(8,128)(2,1)} %copy-done.19) | copy-start | bytes 786436
  66.7 12.7 %copy-start.17 = (bf16[1024,128]{1,0:T(8,128)(2,1)S(1)}, bf16[1024,128]{1,0:T(8,128)(2,1)}, u32[]{:S(2)}) copy-start(bf16[1024,128]{1,0:T(8,128)(2,1)} %copy-done.16) | copy-start | bytes 786436
  66.7 14.3 %copy-start.27 = (bf16[256,256]{1,0:T(8,128)(2,1)S(1)}, bf16[256,256]{1,0:T(8,128)(2,1)}, u32[]{:S(2)}) copy-start(bf16[256,256]{1,0:T(8,128)(2,1)} %get-tuple-element.134.refs_3_) | copy-start | bytes 393220
  66.7 8.5 %collective-permute-start.12 = (bf16[1024,128]{1,0:T(8,128)(2,1)S(1)}, bf16[1024,128]{1,0:T(8,128)(2,1)S(1)}, u32[]{:S(2)}, u32[]{:S(2)}) collective-permute-start(bf16[1024,128]{1,0:T(8,128)(2,1)S(1)} %copy-done.22), channel_id=1, source_target_pairs={{0,32},{32,64},{64,96},{96,0},{1,33},{33,65},{65,97},{97,1},{2,34}... | collective-permute-start | bytes 786440 | tf_op jit(solution)/shard_map/ppermute | solution.py:469
  68.2 7.0 %collective-permute-start.13 = (bf16[1024,128]{1,0:T(8,128)(2,1)S(1)}, bf16[1024,128]{1,0:T(8,128)(2,1)S(1)}, u32[]{:S(2)}, u32[]{:S(2)}) collective-permute-start(bf16[1024,128]{1,0:T(8,128)(2,1)S(1)} %copy-done.20), channel_id=1, source_target_pairs={{0,96},{32,0},{64,32},{96,64},{1,97},{33,1},{65,33},{97,65},{2,98}... | collective-permute-start | bytes 786440 | tf_op jit(solution)/shard_map/ppermute | solution.py:469
  74.6 6.4 %copy-start = (bf16[64,8192]{1,0:T(8,128)(2,1)}, bf16[64,8192]{1,0:T(8,128)(2,1)S(1)}, u32[]{:S(2)}) copy-start(bf16[64,8192]{1,0:T(8,128)(2,1)S(1)} %collective-permute-done.7.above_ref.refs_1_) | copy-start | bytes 3145732
  75.2 5.8 %copy-start.1 = (bf16[64,8192]{1,0:T(8,128)(2,1)}, bf16[64,8192]{1,0:T(8,128)(2,1)S(1)}, u32[]{:S(2)}) copy-start(bf16[64,8192]{1,0:T(8,128)(2,1)S(1)} %collective-permute-done.8.below_ref.refs_2_) | copy-start | bytes 3145732
  76.0 28.6 %collective-permute-start.20 = (bf16[512,8192]{1,0:T(8,128)(2,1)}, bf16[512,8192]{1,0:T(8,128)(2,1)}, u32[]{:S(2)}, u32[]{:S(2)}) collective-permute-start(bf16[512,8192]{1,0:T(8,128)(2,1)} %refs_0_.1), channel_id=1, source_target_pairs={{0,1},{1,0},{2,3},{3,2},{4,5},{5,4},{6,7},{7,6},{8,9},{9,8},{10,11... | collective-permute-start | bytes 25165832 | tf_op jit(solution)/shard_map/ppermute | solution.py:464
  76.0 3.4 %copy-start.26 = (bf16[1024,128]{1,0:T(8,128)(2,1)S(1)}, bf16[1024,128]{1,0:T(8,128)(2,1)}, u32[]{:S(2)}) copy-start(bf16[1024,128]{1,0:T(8,128)(2,1)} %copy-done.25) | copy-start | bytes 786436
  76.1 16.2 %collective-permute-start.14 = (bf16[32,8192]{1,0:T(8,128)(2,1)S(1)}, bf16[32,8192]{1,0:T(8,128)(2,1)S(1)}, u32[]{:S(2)}, u32[]{:S(2)}) collective-permute-start(bf16[32,8192]{1,0:T(8,128)(2,1)S(1)} %get-tuple-element.125), channel_id=1, source_target_pairs={{0,2},{2,4},{4,6},{6,0},{1,3},{3,5},{5,7},{7,1},{8,10},{10,12},{12... | collective-permute-start | bytes 1572872 | tf_op jit(solution)/shard_map/ppermute | solution.py:469
  77.0 15.2 %collective-permute-start.15 = (bf16[32,8192]{1,0:T(8,128)(2,1)S(1)}, bf16[32,8192]{1,0:T(8,128)(2,1)S(1)}, u32[]{:S(2)}, u32[]{:S(2)}) collective-permute-start(bf16[32,8192]{1,0:T(8,128)(2,1)S(1)} %get-tuple-element.126), channel_id=1, source_target_pairs={{0,6},{2,0},{4,2},{6,4},{1,7},{3,1},{5,3},{7,5},{8,14},{10,8},{12,... | collective-permute-start | bytes 1572872 | tf_op jit(solution)/shard_map/ppermute | solution.py:469
  79.4 12.2 %collective-permute-start.16 = (bf16[1024,128]{1,0:T(8,128)(2,1)S(1)}, bf16[1024,128]{1,0:T(8,128)(2,1)S(1)}, u32[]{:S(2)}, u32[]{:S(2)}) collective-permute-start(bf16[1024,128]{1,0:T(8,128)(2,1)S(1)} %add_convert_fusion), channel_id=1, source_target_pairs={{0,32},{32,64},{64,96},{96,0},{1,33},{33,65},{65,97},{97,1},{2,34}... | collective-permute-start | bytes 786440 | tf_op jit(solution)/shard_map/ppermute | solution.py:469
  81.0 22.8 %collective-permute-start.17 = (bf16[256,256]{1,0:T(8,128)(2,1)S(1)}, bf16[256,256]{1,0:T(8,128)(2,1)}, u32[]{:S(2)}, u32[]{:S(2)}) collective-permute-start(bf16[256,256]{1,0:T(8,128)(2,1)S(1)} %copy-done.27), channel_id=1, source_target_pairs={{0,1},{1,0},{2,3},{3,2},{4,5},{5,4},{6,7},{7,6},{8,9},{9,8},{10,11... | collective-permute-start | bytes 393224 | tf_op jit(solution)/shard_map/ppermute | solution.py:464
  91.6 12.2 %collective-permute-start.18 = (bf16[192,256]{1,0:T(8,128)(2,1)}, bf16[192,256]{1,0:T(8,128)(2,1)S(1)}, u32[]{:S(2)}, u32[]{:S(2)}) collective-permute-start(bf16[192,256]{1,0:T(8,128)(2,1)} %get-tuple-element.135.refs_4_), channel_id=1, source_target_pairs={{0,1},{1,0},{2,3},{3,2},{4,5},{5,4},{6,7},{7,6},{8,9},{9,8},{10,11... | collective-permute-start | bytes 294920 | tf_op jit(solution)/shard_map/ppermute | solution.py:464
  102.9 1.7 collective-permute-start.19
  115.7 21.5 %collective-permute-start.21 = (bf16[64,4096]{1,0:T(8,128)(2,1)}, bf16[64,4096]{1,0:T(8,128)(2,1)S(1)}, u32[]{:S(2)}, u32[]{:S(2)}) collective-permute-start(bf16[64,4096]{1,0:T(8,128)(2,1)} %get-tuple-element.140), channel_id=1, source_target_pairs={{0,2},{2,4},{4,6},{6,0},{1,3},{3,5},{5,7},{7,1},{8,10},{10,12},{12... | collective-permute-start | bytes 1572872 | tf_op jit(solution)/shard_map/ppermute | solution.py:469
  123.2 14.4 %collective-permute-start.22 = (bf16[64,4096]{1,0:T(8,128)(2,1)}, bf16[64,4096]{1,0:T(8,128)(2,1)S(1)}, u32[]{:S(2)}, u32[]{:S(2)}) collective-permute-start(bf16[64,4096]{1,0:T(8,128)(2,1)} %get-tuple-element.142), channel_id=1, source_target_pairs={{0,6},{2,0},{4,2},{6,4},{1,7},{3,1},{5,3},{7,5},{8,14},{10,8},{12,... | collective-permute-start | bytes 1572872 | tf_op jit(solution)/shard_map/ppermute | solution.py:469
  126.1 11.5 %copy-start.11 = (bf16[64,4096]{1,0:T(8,128)(2,1)S(1)}, bf16[64,4096]{1,0:T(8,128)(2,1)}, u32[]{:S(2)}) copy-start(bf16[64,4096]{1,0:T(8,128)(2,1)} %get-tuple-element.150.refs_0_) | copy-start | bytes 1572868
  126.1 11.5 %copy-start.12 = (bf16[64,4096]{1,0:T(8,128)(2,1)S(1)}, bf16[64,4096]{1,0:T(8,128)(2,1)}, u32[]{:S(2)}) copy-start(bf16[64,4096]{1,0:T(8,128)(2,1)} %get-tuple-element.153.refs_3_) | copy-start | bytes 1572868
  126.2 11.5 %copy-start.13 = (bf16[64,4096]{1,0:T(8,128)(2,1)S(1)}, bf16[64,4096]{1,0:T(8,128)(2,1)}, u32[]{:S(2)}) copy-start(bf16[64,4096]{1,0:T(8,128)(2,1)} %get-tuple-element.151.refs_1_) | copy-start | bytes 1572868
  126.2 11.5 %copy-start.14 = (bf16[64,4096]{1,0:T(8,128)(2,1)S(1)}, bf16[64,4096]{1,0:T(8,128)(2,1)}, u32[]{:S(2)}) copy-start(bf16[64,4096]{1,0:T(8,128)(2,1)} %get-tuple-element.154.refs_4_) | copy-start | bytes 1572868
  126.2 11.8 %collective-permute-start.23 = (bf16[512,128]{1,0:T(8,128)(2,1)S(1)}, bf16[512,128]{1,0:T(8,128)(2,1)S(1)}, u32[]{:S(2)}, u32[]{:S(2)}) collective-permute-start(bf16[512,128]{1,0:T(8,128)(2,1)S(1)} %add_convert_fusion.1), channel_id=1, source_target_pairs={{0,16},{16,0},{1,17},{17,1},{2,18},{18,2},{3,19},{19,3},{4,20},{20... | collective-permute-start | bytes 393224 | tf_op jit(solution)/shard_map/ppermute | solution.py:464
  137.2 4.6 %copy-start.31 = (bf16[64,4096]{1,0:T(8,128)(2,1)S(1)}, bf16[64,4096]{1,0:T(8,128)(2,1)}, u32[]{:S(2)}) copy-start(bf16[64,4096]{1,0:T(8,128)(2,1)} %get-tuple-element.176) | copy-start | bytes 1572868
  137.2 4.7 %copy-start.30 = (bf16[64,4096]{1,0:T(8,128)(2,1)S(1)}, bf16[64,4096]{1,0:T(8,128)(2,1)}, u32[]{:S(2)}) copy-start(bf16[64,4096]{1,0:T(8,128)(2,1)} %get-tuple-element.178) | copy-start | bytes 1572868
  137.2 7.9 %copy-start.15 = (f32[512,128]{1,0:T(8,128)S(1)}, f32[512,128]{1,0:T(8,128)}, u32[]{:S(2)}) copy-start(f32[512,128]{1,0:T(8,128)} %refs_4_.3) | copy-start | bytes 786436
  137.6 28.1 %copy-start.2 = (bf16[64,4096]{1,0:T(8,128)(2,1)S(1)}, bf16[64,4096]{1,0:T(8,128)(2,1)}, u32[]{:S(2)}) copy-start(bf16[64,4096]{1,0:T(8,128)(2,1)} %get-tuple-element.166.refs_0_.refs_4_) | copy-start | bytes 1572868
  137.6 28.1 %copy-start.3 = (bf16[64,4096]{1,0:T(8,128)(2,1)S(1)}, bf16[64,4096]{1,0:T(8,128)(2,1)}, u32[]{:S(2)}) copy-start(bf16[64,4096]{1,0:T(8,128)(2,1)} %get-tuple-element.167.refs_1_.refs_5_) | copy-start | bytes 1572868
  138.0 27.7 %collective-permute-start.24 = (bf16[64,8192]{1,0:T(8,128)(2,1)S(1)}, bf16[64,8192]{1,0:T(8,128)(2,1)S(1)}, u32[]{:S(2)}, u32[]{:S(2)}) collective-permute-start(bf16[64,8192]{1,0:T(8,128)(2,1)S(1)} %get-tuple-element.161), channel_id=1, source_target_pairs={{0,2},{2,4},{4,6},{6,0},{1,3},{3,5},{5,7},{7,1},{8,10},{10,12},{12... | collective-permute-start | bytes 3145736 | tf_op jit(solution)/shard_map/ppermute | solution.py:469
  139.3 26.4 %collective-permute-start.25 = (bf16[64,8192]{1,0:T(8,128)(2,1)S(1)}, bf16[64,8192]{1,0:T(8,128)(2,1)S(1)}, u32[]{:S(2)}, u32[]{:S(2)}) collective-permute-start(bf16[64,8192]{1,0:T(8,128)(2,1)S(1)} %get-tuple-element.162), channel_id=1, source_target_pairs={{0,6},{2,0},{4,2},{6,4},{1,7},{3,1},{5,3},{7,5},{8,14},{10,8},{12,... | collective-permute-start | bytes 3145736 | tf_op jit(solution)/shard_map/ppermute | solution.py:469
  141.8 33.4 %collective-permute-start.32 = (bf16[64,4096]{1,0:T(8,128)(2,1)S(1)}, bf16[64,4096]{1,0:T(8,128)(2,1)S(1)}, u32[]{:S(2)}, u32[]{:S(2)}) collective-permute-start(bf16[64,4096]{1,0:T(8,128)(2,1)S(1)} %copy-done.31), channel_id=1, source_target_pairs={{0,2},{2,4},{4,6},{6,0},{1,3},{3,5},{5,7},{7,1},{8,10},{10,12},{12... | collective-permute-start | bytes 1572872 | tf_op jit(solution)/shard_map/ppermute | solution.py:469
  141.9 33.3 %collective-permute-start.33 = (bf16[64,4096]{1,0:T(8,128)(2,1)S(1)}, bf16[64,4096]{1,0:T(8,128)(2,1)S(1)}, u32[]{:S(2)}, u32[]{:S(2)}) collective-permute-start(bf16[64,4096]{1,0:T(8,128)(2,1)S(1)} %copy-done.30), channel_id=1, source_target_pairs={{0,6},{2,0},{4,2},{6,4},{1,7},{3,1},{5,3},{7,5},{8,14},{10,8},{12,... | collective-permute-start | bytes 1572872 | tf_op jit(solution)/shard_map/ppermute | solution.py:469
  146.6 5.0 %collective-permute-start.26 = (bf16[512,128]{1,0:T(8,128)(2,1)S(1)}, bf16[512,128]{1,0:T(8,128)(2,1)S(1)}, u32[]{:S(2)}, u32[]{:S(2)}) collective-permute-start(bf16[512,128]{1,0:T(8,128)(2,1)S(1)} %get-tuple-element.164), channel_id=1, source_target_pairs={{0,16},{16,0},{1,17},{17,1},{2,18},{18,2},{3,19},{19,3},{4,20},{20... | collective-permute-start | bytes 393224 | tf_op jit(solution)/shard_map/ppermute | solution.py:464
  151.6 7.7 %collective-permute-start.27 = (bf16[1024,128]{1,0:T(8,128)(2,1)S(1)}, bf16[1024,128]{1,0:T(8,128)(2,1)S(1)}, u32[]{:S(2)}, u32[]{:S(2)}) collective-permute-start(bf16[1024,128]{1,0:T(8,128)(2,1)S(1)} %constant_dynamic-update-slice_fusion.refs_0_), channel_id=1, source_target_pairs={{0,32},{32,64},{64,96},{96,0},{1,33},{33,65},{65,97},{97,1},{2,34}... | collective-permute-start | bytes 786440 | tf_op jit(solution)/shard_map/ppermute | solution.py:469
  165.7 9.5 %copy-start.5 = (bf16[64,8192]{1,0:T(8,128)(2,1)S(1)}, bf16[64,8192]{1,0:T(8,128)(2,1)}, u32[]{:S(2)}) copy-start(bf16[64,8192]{1,0:T(8,128)(2,1)} %get-tuple-element.175.refs_0_) | copy-start | bytes 3145732
  165.7 9.5 %copy-start.6 = (bf16[64,8192]{1,0:T(8,128)(2,1)S(1)}, bf16[64,8192]{1,0:T(8,128)(2,1)}, u32[]{:S(2)}) copy-start(bf16[64,8192]{1,0:T(8,128)(2,1)} %get-tuple-element.177.refs_2_) | copy-start | bytes 3145732
  166.1 26.8 %copy-start.9 = (bf16[512,1024]{1,0:T(8,128)(2,1)S(1)}, bf16[512,1024]{1,0:T(8,128)(2,1)}, u32[]{:S(2)}) copy-start(bf16[512,1024]{1,0:T(8,128)(2,1)} %params_ref.1) | copy-start | bytes 3145732
  166.1 14.9 %collective-permute-start.29 = (bf16[64,4096]{1,0:T(8,128)(2,1)S(1)}, bf16[64,4096]{1,0:T(8,128)(2,1)S(1)}, u32[]{:S(2)}, u32[]{:S(2)}) collective-permute-start(bf16[64,4096]{1,0:T(8,128)(2,1)S(1)} %get-tuple-element.170.refs_4_), channel_id=1, source_target_pairs={{0,16},{16,8},{8,24},{24,0},{1,17},{17,9},{9,25},{25,1},{2,18},{18... | collective-permute-start | bytes 1572872 | tf_op jit(solution)/shard_map/ppermute | solution.py:469
  167.3 13.7 %collective-permute-start.30 = (bf16[64,4096]{1,0:T(8,128)(2,1)S(1)}, bf16[64,4096]{1,0:T(8,128)(2,1)S(1)}, u32[]{:S(2)}, u32[]{:S(2)}) collective-permute-start(bf16[64,4096]{1,0:T(8,128)(2,1)S(1)} %get-tuple-element.171), channel_id=1, source_target_pairs={{0,24},{16,0},{8,16},{24,8},{1,25},{17,1},{9,17},{25,9},{2,26},{18... | collective-permute-start | bytes 1572872 | tf_op jit(solution)/shard_map/ppermute | solution.py:469
  175.5 24.7 %copy-start.4 = (bf16[64,8192]{1,0:T(8,128)(2,1)S(1)}, bf16[64,8192]{1,0:T(8,128)(2,1)}, u32[]{:S(2)}) copy-start(bf16[64,8192]{1,0:T(8,128)(2,1)} %get-tuple-element.174.refs_0_) | copy-start | bytes 3145732
  175.5 24.7 %collective-permute-start.34 = (bf16[64,8192]{1,0:T(8,128)(2,1)S(1)}, bf16[64,8192]{1,0:T(8,128)(2,1)S(1)}, u32[]{:S(2)}, u32[]{:S(2)}) collective-permute-start(bf16[64,8192]{1,0:T(8,128)(2,1)S(1)} %get-tuple-element.179), channel_id=1, source_target_pairs={{0,2},{2,4},{4,6},{6,0},{1,3},{3,5},{5,7},{7,1},{8,10},{10,12},{12... | collective-permute-start | bytes 3145736 | tf_op jit(solution)/shard_map/ppermute | solution.py:469
  176.7 23.5 %collective-permute-start.35 = (bf16[64,8192]{1,0:T(8,128)(2,1)S(1)}, bf16[64,8192]{1,0:T(8,128)(2,1)S(1)}, u32[]{:S(2)}, u32[]{:S(2)}) collective-permute-start(bf16[64,8192]{1,0:T(8,128)(2,1)S(1)} %get-tuple-element.180), channel_id=1, source_target_pairs={{0,6},{2,0},{4,2},{6,4},{1,7},{3,1},{5,3},{7,5},{8,14},{10,8},{12,... | collective-permute-start | bytes 3145736 | tf_op jit(solution)/shard_map/ppermute | solution.py:469
  178.8 6.4 %collective-permute-start.28 = (bf16[1024,128]{1,0:T(8,128)(2,1)S(1)}, bf16[1024,128]{1,0:T(8,128)(2,1)S(1)}, u32[]{:S(2)}, u32[]{:S(2)}) collective-permute-start(bf16[1024,128]{1,0:T(8,128)(2,1)S(1)} %constant_dynamic-update-slice_fusion.refs_0_), channel_id=1, source_target_pairs={{0,96},{32,0},{64,32},{96,64},{1,97},{33,1},{65,33},{97,65},{2,98}... | collective-permute-start | bytes 786440 | tf_op jit(solution)/shard_map/ppermute | solution.py:469
  181.0 19.2 %collective-permute-start.36 = (bf16[64,4096]{1,0:T(8,128)(2,1)S(1)}, bf16[64,4096]{1,0:T(8,128)(2,1)S(1)}, u32[]{:S(2)}, u32[]{:S(2)}) collective-permute-start(bf16[64,4096]{1,0:T(8,128)(2,1)S(1)} %collective-permute-done.29), channel_id=1, source_target_pairs={{0,16},{16,8},{8,24},{24,0},{1,17},{17,9},{9,25},{25,1},{2,18},{18... | collective-permute-start | bytes 1572872 | tf_op jit(solution)/shard_map/ppermute | solution.py:469
  181.9 18.3 %collective-permute-start.37 = (bf16[64,4096]{1,0:T(8,128)(2,1)S(1)}, bf16[64,4096]{1,0:T(8,128)(2,1)S(1)}, u32[]{:S(2)}, u32[]{:S(2)}) collective-permute-start(bf16[64,4096]{1,0:T(8,128)(2,1)S(1)} %collective-permute-done.30), channel_id=1, source_target_pairs={{0,24},{16,0},{8,16},{24,8},{1,25},{17,1},{9,17},{25,9},{2,26},{18... | collective-permute-start | bytes 1572872 | tf_op jit(solution)/shard_map/ppermute | solution.py:469
  185.2 7.8 %collective-permute-start.31 = (bf16[1024,128]{1,0:T(8,128)(2,1)S(1)}, bf16[1024,128]{1,0:T(8,128)(2,1)S(1)}, u32[]{:S(2)}, u32[]{:S(2)}) collective-permute-start(bf16[1024,128]{1,0:T(8,128)(2,1)S(1)} %collective-permute-done.27.refs_2_), channel_id=1, source_target_pairs={{0,32},{32,64},{64,96},{96,0},{1,33},{33,65},{65,97},{97,1},{2,34}... | collective-permute-start | bytes 786440 | tf_op jit(solution)/shard_map/ppermute | solution.py:469
  (6 other events, 4.6 us)
where the time goes:
time: 202 us
  Pallas kernels  71.9 us (36%)
  waiting for transfers between devices  70.1 us (35%)
  starting transfers between devices  51.3 us (25%)
  local copies, waits for them, and re-layouts  6.03 us (3%)
    ppermute x30, waiting for transfers between devices, hop(): lax.ppermute(block, axis, [(at[i], at[(i + way) % 4]) for i in range(4)])  65.2 us
    ppermute x30, starting transfers between devices, hop(): lax.ppermute(block, axis, [(at[i], at[(i + way) % 4]) for i in range(4)])  49.3 us
    pallas_call x3, Pallas kernels, project(): pl.pallas_call(project_body, in_specs=[pl.BlockSpec(memory_space=pltpu.SM...  32.3 us
    pallas_call x2, Pallas kernels, output(): pl.pallas_call(functools.partial(output_body, side, first, pieces), in_sp...  17.7 us
    pallas_call x1, Pallas kernels, attend(): pl.pallas_call(functools.partial(attend_body, order), in_specs=[pl.BlockS...  10.5 us
    unnamed x66, local copies, waits for them, and re-layouts  5.32 us
    ppermute x8, waiting for transfers between devices, swap(): return lax.ppermute(block, axis, [(0, 1), (1, 0)])  4.87 us
  transfers between devices with their start and end apart: 38, of which 15 were waited for; matrix products, arithmetic and copies ran while one was open for 1% of the time, Pallas kernels for 29%

commit v1 on v0

--- a/solution.py
+++ b/solution.py
@@ -17,6 +17,7 @@
 Y = ("ylo", "yhi")
 HALVES = 2
 TILE = 1024
+PIECES = (1, 1, 1, HALVES)
 MIB = 1024 * 1024
 
 
@@ -56,7 +57,7 @@
             jax.ShapeDtypeStruct((c, width), jnp.bfloat16)
             for c in [count] + [count // HALVES] * HALVES
         ],
-        compiler_params=params(12),
+        compiler_params=params(56),
         cost_estimate=cost(4 * rows.size, 6 * rows.size),
         name="normalize",
     )(rows, gain.reshape(1, width))
@@ -173,10 +174,9 @@
 
 
 def attend_body(order, core_ref, place_ref, *refs):
-    blocks = len(RING)
-    ins, refs = refs[: -8 - blocks], refs[-8 - blocks :]
-    weights, mixed_ref, out_refs = refs[:2], refs[2], refs[3 : 3 + blocks]
-    query_ref, own_ref, other_ref, held, arrived = refs[3 + blocks :]
+    ins, refs = refs[: -8 - sum(PIECES)], refs[-8 - sum(PIECES) :]
+    weights, mixed_ref, out_refs = refs[:2], refs[2], list(refs[3 : 3 + sum(PIECES)])
+    query_ref, own_ref, other_ref, held, arrived = refs[3 + sum(PIECES) :]
     fetch(weights, held, arrived, 0)
     core = core_ref[0]
     parts = len(ins) // 3
@@ -237,9 +237,8 @@
                 top = h * block + part * ROWS
                 mixed_ref[place, h * HEAD : (h + 1) * HEAD] = mixed[top : top + ROWS]
 
-    multiply(
-        lambda: mixed_ref[count // 2 :], weights, held, arrived, 0, [[ref] for ref in out_refs]
-    )
+    outs = [[out_refs.pop(0) for _ in range(piece)] for piece in PIECES]
+    multiply(lambda: mixed_ref[count // 2 :], weights, held, arrived, 0, outs)
 
 
 def attend(core, places, order, queries, own, other, weights):
@@ -253,13 +252,17 @@
         in_specs=[pl.BlockSpec(memory_space=pltpu.SMEM)] * 2
         + [vmem] * len(args)
         + [pl.BlockSpec(memory_space=pl.ANY)] * 2,
-        out_specs=[vmem] * (1 + len(RING)),
+        out_specs=[vmem] * (1 + sum(PIECES)),
         out_shape=[jax.ShapeDtypeStruct((count, qcols), jnp.bfloat16)]
-        + [jax.ShapeDtypeStruct((ROWS, width // HALVES), jnp.bfloat16)] * len(RING),
+        + [
+            jax.ShapeDtypeStruct((ROWS, width // piece), jnp.bfloat16)
+            for piece in PIECES
+            for _ in range(piece)
+        ],
         scratch_shapes=[pltpu.VMEM((count, cols), jnp.bfloat16) for cols in (qcols, kcols, kcols)]
         + [
-            pltpu.VMEM((2 * depth, width // HALVES), jnp.bfloat16),
-            pltpu.SemaphoreType.DMA((width // HALVES // TILE, 2)),
+            pltpu.VMEM((2 * depth, width), jnp.bfloat16),
+            pltpu.SemaphoreType.DMA((width // TILE, 2)),
         ],
         compiler_params=params(56),
         cost_estimate=cost(8 * count * count * qcols, 4 * count * qcols + 4 * depth * width),
@@ -267,23 +270,22 @@
     )(core, places, *args, *weights)
 
 
-def output_body(side, first, pieces, mixed_ref, *refs):
+def output_body(mixed_ref, *refs):
     weights, out_refs, (held, arrived) = refs[:2], list(refs[2:-2]), refs[-2:]
-    fetch(weights, held, arrived, first)
+    fetch(weights, held, arrived, 0)
     count = mixed_ref.shape[0] // 2
-    outs = [[out_refs.pop(0) for _ in range(piece)] for piece in pieces]
-    rows_of = lambda: mixed_ref[side * count : (side + 1) * count]
-    multiply(rows_of, weights, held, arrived, first, outs)
-
-
-def output(mixed, weights, side, first, width, pieces):
-    depth = weights[0].shape[0]
+    outs = [[out_refs.pop(0) for _ in range(piece)] for piece in PIECES]
+    multiply(lambda: mixed_ref[:count], weights, held, arrived, 0, outs)
+
+
+def output(mixed, weights):
+    depth, width = weights[0].shape
     count = mixed.shape[0] // 2
     vmem = pl.BlockSpec(memory_space=pltpu.VMEM)
-    widths = [width // piece for piece in pieces for _ in range(piece)]
-    result = list(
+    widths = [width // piece for piece in PIECES for _ in range(piece)]
+    return list(
         pl.pallas_call(
-            functools.partial(output_body, side, first, pieces),
+            output_body,
             in_specs=[vmem] + [pl.BlockSpec(memory_space=pl.ANY)] * 2,
             out_specs=[vmem] * len(widths),
             out_shape=[jax.ShapeDtypeStruct((ROWS, w), jnp.bfloat16) for w in widths],
@@ -298,7 +300,6 @@
             name="output",
         )(mixed, *weights)
     )
-    return [[result.pop(0) for _ in range(piece)] for piece in pieces]
 
 
 def mark_body(*refs):
@@ -340,7 +341,7 @@
     outs = refs[-len(shapes) :]
     first = 0
     for out_ref, (offset, starts) in zip(outs, shapes):
-        step = min(ref.shape[1] for ref in refs[first : first + len(starts)])
+        step = min(ref.shape[1] for ref in (out_ref, *refs[first : first + len(starts)]))
         for left in range(0, out_ref.shape[1], step):
             total = None
             for at, start in enumerate(starts):
@@ -532,7 +533,7 @@
     query_l, pair_l = project(core, [pfar1, pfar2], weights)
     other_l = swap(pair_l, "core")
     out_weights = (out_weight, out_theirs)
-    mixed, q0a, qupa, qdowna, qfara = attend(
+    mixed, q0, qup, qdown, far_a, far_b = attend(
         core,
         places,
         tuple(range(8)),
@@ -544,19 +545,16 @@
 
     full = out_weight.shape[1]
     half = full // HALVES
-    mixed, far_a = wait(mixed, qfara)
-    far_a = hop(far_a, "z", 1)
-    (q0b,), (qupb,), (qdownb,), (qfarb,) = output(mixed, out_weights, 1, half, half, (1, 1, 1, 1))
-    far_b = hop(qfarb, "z", -1)
+    mixed, far_a, far_b = wait(mixed, far_a, far_b)
+    far_a, far_b = hop(far_a, "z", 1), hop(far_b, "z", -1)
     mine = (at0, passed, x3)
     count = momentum.shape[0]
-    sent, q0b, mixed = wait(add(*(part[count:] for part in mine)), q0b, mixed)
+    sent, q0, mixed = wait(add(*(part[count:] for part in mine)), q0, mixed)
     theirs = swap(sent, "ylo")
-    (o0,), (oup,), (odown,), (ofara, ofarb) = output(mixed, out_weights, 0, 0, full, (1, 1, 1, 2))
+    o0, oup, odown, ofara, ofarb = output(mixed, out_weights)
     far_a, far_b, o0 = wait(far_a, far_b, o0)
     up, down = sums(
-        ((0, full), ((qupa, 0), (qupb, half), (far_a, 0))),
-        ((0, full), ((qdowna, 0), (qdownb, half), (far_b, half))),
+        ((0, full), ((qup, 0), (far_a, 0))), ((0, full), ((qdown, 0), (far_b, half)))
     )
     up, down, theirs, ofara, ofarb = wait(up, down, theirs, ofara, ofarb)
     up, down = hop(up, "z", 1), hop(down, "z", -1)
@@ -567,7 +565,7 @@
     before = hop(both, "x", 1)
     up, down, before, both = wait(up, down, before, both)
     s1, s2 = sums(
-        *(((at, half), ((q0a, 0), (q0b, half), (up, 0), (down, 0))) for at in (0, half))
+        *(((at, half), ((q0, 0), (up, 0), (down, 0))) for at in (0, half))
     )
     oup, odown = sums(
         ((0, full), ((oup, 0), (ofara, 0))),

time: 202 us -> 198 us (0.980)
    pallas_call x2 -> x1, Pallas kernels: 17.7 us -> 10.8 us  [output(): pl.pallas_call(output_body, in_specs=[vmem] + [pl.BlockSpec(memory_space=...]
    pallas_call x1, Pallas kernels: 10.5 us -> 14.3 us  [attend(): pl.pallas_call(functools.partial(attend_body, order), in_specs=[pl.BlockS...]
    unnamed x66 -> x56, local copies, waits for them, and re-layouts: 5.32 us -> 3.24 us
  transfers between devices with their start and end apart: 38 -> 38, of which waited for: 15 -> 16; matrix products, arithmetic and copies ran while one was open for 1% -> 1% of each run, Pallas kernels for 29% -> 26%
where the time goes in v1:
time: 198 us
  waiting for transfers between devices  70.6 us (36%)
  Pallas kernels  70.1 us (35%)
  starting transfers between devices  50.9 us (26%)
  local copies, waits for them, and re-layouts  4.04 us (2%)
    ppermute x30, waiting for transfers between devices, hop(): lax.ppermute(block, axis, [(at[i], at[(i + way) % 4]) for i in range(4)])  65.7 us
    ppermute x30, starting transfers between devices, hop(): lax.ppermute(block, axis, [(at[i], at[(i + way) % 4]) for i in range(4)])  49 us
    pallas_call x3, Pallas kernels, project(): pl.pallas_call(project_body, in_specs=[pl.BlockSpec(memory_space=pltpu.SM...  32.3 us
    pallas_call x1, Pallas kernels, attend(): pl.pallas_call(functools.partial(attend_body, order), in_specs=[pl.BlockS...  14.3 us
    pallas_call x1, Pallas kernels, output(): pl.pallas_call(output_body, in_specs=[vmem] + [pl.BlockSpec(memory_space=...  10.8 us
    ppermute x8, waiting for transfers between devices, swap(): return lax.ppermute(block, axis, [(0, 1), (1, 0)])  4.93 us
  transfers between devices with their start and end apart: 38, of which 16 were waited for; matrix products, arithmetic and copies ran while one was open for 1% of the time, Pallas kernels for 26%

profile of v1, /device:TPU:0, one launch (start us, length us, event | category | flops | bytes accessed | tf_op | source)
XLA Modules:
  0.0 198.0 jit_solution(11356123512198165937)
XLA Ops:
  0.6 3.1 %normalize.1 = (bf16[64,8192]{1,0:T(8,128)(2,1)}, bf16[32,8192]{1,0:T(8,128)(2,1)}, bf16[32,8192]{1,0:T(8,128)(2,1)}) custom-call(bf16[64,8192]{1,0:T(8,128)(2,1)} %rows_ref.1, f32[1,8192]{1,0:T(1,128)} %bitcast.22), custom_call_target="tpu_custom_call" | custom-call | flops 2097152 | bytes 3145728 | tf_op jit(solution)/shard_map/normalize/pallas_call | solution.py:54
  3.8 1.7 collective-permute-start
  5.4 1.6 collective-permute-start.1
  7.0 2.0 %collective-permute-start.5 = (bf16[64,8192]{1,0:T(8,128)(2,1)}, bf16[64,8192]{1,0:T(8,128)(2,1)S(1)}, u32[]{:S(2)}, u32[]{:S(2)}) collective-permute-start(bf16[64,8192]{1,0:T(8,128)(2,1)} %get-tuple-element.94.refs_0_), channel_id=1, source_target_pairs={{0,2},{2,4},{4,6},{6,0},{1,3},{3,5},{5,7},{7,1},{8,10},{10,12},{12... | collective-permute-start | bytes 3145736 | tf_op jit(solution)/shard_map/ppermute | solution.py:470
  9.0 2.1 %collective-permute-start.6 = (bf16[64,8192]{1,0:T(8,128)(2,1)}, bf16[64,8192]{1,0:T(8,128)(2,1)}, u32[]{:S(2)}, u32[]{:S(2)}) collective-permute-start(bf16[64,8192]{1,0:T(8,128)(2,1)} %get-tuple-element.94.refs_0_), channel_id=1, source_target_pairs={{0,6},{2,0},{4,2},{6,4},{1,7},{3,1},{5,3},{7,5},{8,14},{10,8},{12,... | collective-permute-start | bytes 3145736 | tf_op jit(solution)/shard_map/ppermute | solution.py:470
  11.1 0.8 copy.14
  12.1 1.2 terms.1
  13.3 6.4 %collective-permute-done = bf16[32,8192]{1,0:T(8,128)(2,1)S(1)} collective-permute-done((bf16[32,8192]{1,0:T(8,128)(2,1)}, bf16[32,8192]{1,0:T(8,128)(2,1)S(1)}, u32[]{:S(2)}, u32[]{:S(2)}) %collective-permute-start) | collective-permute-done | bytes 524320 | tf_op jit(solution)/shard_map/ppermute | solution.py:470
  19.8 2.9 %collective-permute-start.4 = (bf16[32,8192]{1,0:T(8,128)(2,1)}, bf16[32,8192]{1,0:T(8,128)(2,1)S(1)}, u32[]{:S(2)}, u32[]{:S(2)}) collective-permute-start(bf16[32,8192]{1,0:T(8,128)(2,1)} %collective-permute-done.1), channel_id=1, source_target_pairs={{0,24},{16,0},{8,16},{24,8},{1,25},{17,1},{9,17},{25,9},{2,26},{18... | collective-permute-start | bytes 1572872 | tf_op jit(solution)/shard_map/ppermute | solution.py:470
  22.7 11.9 %collective-permute-done.5.refs_0_ = bf16[64,8192]{1,0:T(8,128)(2,1)S(1)} collective-permute-done((bf16[64,8192]{1,0:T(8,128)(2,1)}, bf16[64,8192]{1,0:T(8,128)(2,1)S(1)}, u32[]{:S(2)}, u32[]{:S(2)}) %collective-permute-start.5) | collective-permute-done | bytes 1048608 | tf_op jit(solution)/shard_map/ppermute | solution.py:470
  34.7 2.6 %pick.2 = (bf16[32,8192]{1,0:T(8,128)(2,1)}, bf16[32,8192]{1,0:T(8,128)(2,1)}) custom-call(bf16[64,8192]{1,0:T(8,128)(2,1)S(1)} %get-tuple-element.107.below_ref.refs_2_, bf16[64,8192]{1,0:T(8,128)(2,1)} %get-tuple-element.106.above_ref.refs_1_), custom_call_target="tpu_custom_call" | custom-call | flops 100000000 | bytes 2097152 | tf_op jit(solution)/shard_map/pick/pallas_call | solution.py:331
  37.3 1.4 collective-permute-start.9
  38.7 1.9 collective-permute-start.10
  40.6 1.1 pad_maximum_fusion.refs_0_
  41.6 1.8 collective-permute-start.7
  43.7 10.0 %collective-permute-done.9.refs_3_ = bf16[32,8192]{1,0:T(8,128)(2,1)} collective-permute-done((bf16[32,8192]{1,0:T(8,128)(2,1)}, bf16[32,8192]{1,0:T(8,128)(2,1)}, u32[]{:S(2)}, u32[]{:S(2)}) %collective-permute-start.9) | collective-permute-done | bytes 524320 | tf_op jit(solution)/shard_map/ppermute | solution.py:470
  53.9 12.1 %project.3 = (bf16[256,1024]{1,0:T(8,128)(2,1)}, bf16[256,256]{1,0:T(8,128)(2,1)}) custom-call(s32[1]{0:T(128)} %bitcast.core_ref, bf16[64,8192]{1,0:T(8,128)(2,1)} %get-tuple-element.94.refs_0_, bf16[64,8192]{1,0:T(8,128)(2,1)} %get-tuple-element.106.above_ref.refs_1_, bf16[64,8192]{1,0:T(8,128)(2,1)} %copy-done.10, ...), custom_call_target="tpu_custom_call" | custom-call | flops 8053063680 | bytes 25165824 | tf_op jit(solution)/shard_map/project/pallas_call | solution.py:114
  66.0 1.6 collective-permute-start.12
  67.5 1.7 collective-permute-start.13
  69.3 4.6 %collective-permute-done.7.above_ref.refs_1_ = bf16[64,8192]{1,0:T(8,128)(2,1)S(1)} collective-permute-done((bf16[64,8192]{1,0:T(8,128)(2,1)}, bf16[64,8192]{1,0:T(8,128)(2,1)S(1)}, u32[]{:S(2)}, u32[]{:S(2)}) %collective-permute-start.7) | collective-permute-done | bytes 1048608 | tf_op jit(solution)/shard_map/ppermute | solution.py:470
  73.9 0.6 collective-permute-done.8.below_ref.refs_2_
  74.5 0.7 copy-done.20
  75.4 1.0 collective-permute-start.14
  76.3 2.3 %collective-permute-start.15 = (bf16[32,8192]{1,0:T(8,128)(2,1)S(1)}, bf16[32,8192]{1,0:T(8,128)(2,1)S(1)}, u32[]{:S(2)}, u32[]{:S(2)}) collective-permute-start(bf16[32,8192]{1,0:T(8,128)(2,1)S(1)} %get-tuple-element.124), channel_id=1, source_target_pairs={{0,6},{2,0},{4,2},{6,4},{1,7},{3,1},{5,3},{7,5},{8,14},{10,8},{12,... | collective-permute-start | bytes 1572872 | tf_op jit(solution)/shard_map/ppermute | solution.py:470
  78.7 1.6 collective-permute-start.16
  80.3 10.6 %project.4 = (bf16[192,1024]{1,0:T(8,128)(2,1)}, bf16[192,256]{1,0:T(8,128)(2,1)}) custom-call(s32[1]{0:T(128)} %bitcast.core_ref, bf16[64,8192]{1,0:T(8,128)(2,1)} %pad_maximum_fusion.refs_0_, bf16[64,8192]{1,0:T(8,128)(2,1)} %copy-done.1, bf16[64,8192]{1,0:T(8,128)(2,1)} %copy-done.2, bf16[8192,512]{1,0:T(8,128)(2,1)} %refs_2_, ...), custom_call_target="tpu_custom_call" | custom-call | flops 6039797760 | bytes 24117248 | tf_op jit(solution)/shard_map/project/pallas_call | solution.py:114
  91.0 0.6 collective-permute-start.18
  91.6 0.8 copy-done.18
  92.5 9.6 %project.5 = (bf16[64,1024]{1,0:T(8,128)(2,1)}, bf16[64,256]{1,0:T(8,128)(2,1)}) custom-call(s32[1]{0:T(128)} %bitcast.core_ref, bf16[32,8192]{1,0:T(8,128)(2,1)} %copy-done.18, bf16[32,8192]{1,0:T(8,128)(2,1)} %copy-done.19, bf16[8192,512]{1,0:T(8,128)(2,1)} %refs_2_, bf16[8192,512]{1,0:T(8,128)(2,1)} %collective-permute-done.11.refs_6_.refs_4_.refs_3_, ...), custom_call_target="tpu_custom_call" | custom-call | flops 2013265920 | bytes 22020096 | tf_op jit(solution)/shard_map/project/pallas_call | solution.py:114
  102.2 0.3 collective-permute-start.19
  102.5 0.7 concatenate.9.place_ref
  103.2 0.6 collective-permute-done.19.refs_8_
  103.8 0.6 copy-done.24
  104.4 14.3 %attend.1 = (bf16[512,1024]{1,0:T(8,128)(2,1)}, bf16[64,8192]{1,0:T(8,128)(2,1)}, bf16[64,8192]{1,0:T(8,128)(2,1)}, bf16[64,8192]{1,0:T(8,128)(2,1)}, bf16[64,40...) custom-call(s32[1]{0:T(128)} %bitcast.core_ref, s32[16]{0:T(128)} %concatenate.9.place_ref, ...), custom_call_target="tpu_custom_call" | custom-call | flops 2147483648 | bytes 18874368 | tf_op jit(solution)/shard_map/attend/pallas_call | solution.py:250
  118.8 0.5 collective-permute-start.21
  119.3 2.8 %collective-permute-start.22 = (bf16[64,4096]{1,0:T(8,128)(2,1)}, bf16[64,4096]{1,0:T(8,128)(2,1)S(1)}, u32[]{:S(2)}, u32[]{:S(2)}) collective-permute-start(bf16[64,4096]{1,0:T(8,128)(2,1)} %get-tuple-element.140), channel_id=1, source_target_pairs={{0,6},{2,0},{4,2},{6,4},{1,7},{3,1},{5,3},{7,5},{8,14},{10,8},{12,... | collective-permute-start | bytes 1572872 | tf_op jit(solution)/shard_map/ppermute | solution.py:470
  122.2 0.3 collective-permute-start.23
  122.5 10.8 %output.1 = (bf16[64,8192]{1,0:T(8,128)(2,1)}, bf16[64,8192]{1,0:T(8,128)(2,1)}, bf16[64,8192]{1,0:T(8,128)(2,1)}, bf16[64,4096]{1,0:T(8,128)(2,1)}, bf16[64,4096]{1,0:T(8,128)(2,1)}) custom-call(bf16[512,1024]{1,0:T(8,128)(2,1)} %get-tuple-element.146.mixed_ref, bf16[512,8192]{1,0:T(8,128)(2,1)} %refs_0_, ...), custom_call_target="tpu_custom_call" | custom-call | flops 4294967296 | bytes 20971520 | tf_op jit(solution)/shard_map/output/pallas_call | solution.py:287
  133.3 1.0 collective-permute-done.21.refs_1_
  134.6 0.7 collective-permute-start.24
  135.3 2.6 %collective-permute-start.25 = (bf16[64,8192]{1,0:T(8,128)(2,1)S(1)}, bf16[64,8192]{1,0:T(8,128)(2,1)S(1)}, u32[]{:S(2)}, u32[]{:S(2)}) collective-permute-start(bf16[64,8192]{1,0:T(8,128)(2,1)S(1)} %get-tuple-element.159), channel_id=1, source_target_pairs={{0,6},{2,0},{4,2},{6,4},{1,7},{3,1},{5,3},{7,5},{8,14},{10,8},{12,... | collective-permute-start | bytes 3145736 | tf_op jit(solution)/shard_map/ppermute | solution.py:470
  138.1 3.2 %collective-permute-start.33 = (bf16[64,4096]{1,0:T(8,128)(2,1)S(1)}, bf16[64,4096]{1,0:T(8,128)(2,1)S(1)}, u32[]{:S(2)}, u32[]{:S(2)}) collective-permute-start(bf16[64,4096]{1,0:T(8,128)(2,1)S(1)} %copy-done.25), channel_id=1, source_target_pairs={{0,6},{2,0},{4,2},{6,4},{1,7},{3,1},{5,3},{7,5},{8,14},{10,8},{12,... | collective-permute-start | bytes 1572872 | tf_op jit(solution)/shard_map/ppermute | solution.py:470
  141.3 1.5 outer.1
  142.7 0.7 collective-permute-start.26
  143.5 4.3 %collective-permute-done.26 = bf16[512,128]{1,0:T(8,128)(2,1)S(1)} collective-permute-done((bf16[512,128]{1,0:T(8,128)(2,1)S(1)}, bf16[512,128]{1,0:T(8,128)(2,1)S(1)}, u32[]{:S(2)}, u32[]{:S(2)}) %collective-permute-start.26) | collective-permute-done | bytes 131104 | tf_op jit(solution)/shard_map/ppermute | solution.py:465
  147.8 1.6 collective-permute-start.27
  149.4 6.1 %collective-permute-done.27.refs_2_ = bf16[1024,128]{1,0:T(8,128)(2,1)S(1)} collective-permute-done((bf16[1024,128]{1,0:T(8,128)(2,1)S(1)}, bf16[1024,128]{1,0:T(8,128)(2,1)S(1)}, u32[]{:S(2)}, u32[]{:S(2)}) %collective-permute-start.27) | collective-permute-done | bytes 262176 | tf_op jit(solution)/shard_map/ppermute | solution.py:470
  155.5 6.5 %collective-permute-done.24.refs_1_.refs_4_ = bf16[64,8192]{1,0:T(8,128)(2,1)S(1)} collective-permute-done((bf16[64,8192]{1,0:T(8,128)(2,1)S(1)}, bf16[64,8192]{1,0:T(8,128)(2,1)S(1)}, u32[]{:S(2)}, u32[]{:S(2)}) %collective-permute-start.24) | collective-permute-done | bytes 1048608 | tf_op jit(solution)/shard_map/ppermute | solution.py:470
  162.0 0.4 sums.4
  162.3 1.0 collective-permute-start.29
  163.3 2.6 %collective-permute-start.30 = (bf16[64,4096]{1,0:T(8,128)(2,1)S(1)}, bf16[64,4096]{1,0:T(8,128)(2,1)S(1)}, u32[]{:S(2)}, u32[]{:S(2)}) collective-permute-start(bf16[64,4096]{1,0:T(8,128)(2,1)S(1)} %get-tuple-element.167), channel_id=1, source_target_pairs={{0,24},{16,0},{8,16},{24,8},{1,25},{17,1},{9,17},{25,9},{2,26},{18... | collective-permute-start | bytes 1572872 | tf_op jit(solution)/shard_map/ppermute | solution.py:470
  165.9 5.6 %collective-permute-done.32.refs_1_ = bf16[64,4096]{1,0:T(8,128)(2,1)S(1)} collective-permute-done((bf16[64,4096]{1,0:T(8,128)(2,1)S(1)}, bf16[64,4096]{1,0:T(8,128)(2,1)S(1)}, u32[]{:S(2)}, u32[]{:S(2)}) %collective-permute-start.32) | collective-permute-done | bytes 524320 | tf_op jit(solution)/shard_map/ppermute | solution.py:470
  171.5 0.3 sums.5
  171.8 0.9 collective-permute-start.34
  172.7 2.4 %collective-permute-start.35 = (bf16[64,8192]{1,0:T(8,128)(2,1)S(1)}, bf16[64,8192]{1,0:T(8,128)(2,1)S(1)}, u32[]{:S(2)}, u32[]{:S(2)}) collective-permute-start(bf16[64,8192]{1,0:T(8,128)(2,1)S(1)} %get-tuple-element.176), channel_id=1, source_target_pairs={{0,6},{2,0},{4,2},{6,4},{1,7},{3,1},{5,3},{7,5},{8,14},{10,8},{12,... | collective-permute-start | bytes 3145736 | tf_op jit(solution)/shard_map/ppermute | solution.py:470
  175.1 2.2 %collective-permute-start.28 = (bf16[1024,128]{1,0:T(8,128)(2,1)S(1)}, bf16[1024,128]{1,0:T(8,128)(2,1)S(1)}, u32[]{:S(2)}, u32[]{:S(2)}) collective-permute-start(bf16[1024,128]{1,0:T(8,128)(2,1)S(1)} %constant_dynamic-update-slice_fusion.refs_0_), channel_id=1, source_target_pairs={{0,96},{32,0},{64,32},{96,64},{1,97},{33,1},{65,33},{97,65},{2,98}... | collective-permute-start | bytes 786440 | tf_op jit(solution)/shard_map/ppermute | solution.py:470
  177.3 0.7 collective-permute-start.36
  178.0 2.6 %collective-permute-start.37 = (bf16[64,4096]{1,0:T(8,128)(2,1)S(1)}, bf16[64,4096]{1,0:T(8,128)(2,1)S(1)}, u32[]{:S(2)}, u32[]{:S(2)}) collective-permute-start(bf16[64,4096]{1,0:T(8,128)(2,1)S(1)} %collective-permute-done.30), channel_id=1, source_target_pairs={{0,24},{16,0},{8,16},{24,8},{1,25},{17,1},{9,17},{25,9},{2,26},{18... | collective-permute-start | bytes 1572872 | tf_op jit(solution)/shard_map/ppermute | solution.py:470
  180.5 0.9 collective-permute-done.28.refs_1_
  181.5 1.5 collective-permute-start.31
  183.0 6.2 %collective-permute-done.31.refs_3_ = bf16[1024,128]{1,0:T(8,128)(2,1)S(1)} collective-permute-done((bf16[1024,128]{1,0:T(8,128)(2,1)S(1)}, bf16[1024,128]{1,0:T(8,128)(2,1)S(1)}, u32[]{:S(2)}, u32[]{:S(2)}) %collective-permute-start.31) | collective-permute-done | bytes 262176 | tf_op jit(solution)/shard_map/ppermute | solution.py:470
  189.2 1.8 apply.1
  191.1 5.5 %collective-permute-done.34.refs_1_ = bf16[64,8192]{1,0:T(8,128)(2,1)S(1)} collective-permute-done((bf16[64,8192]{1,0:T(8,128)(2,1)S(1)}, bf16[64,8192]{1,0:T(8,128)(2,1)S(1)}, u32[]{:S(2)}, u32[]{:S(2)}) %collective-permute-start.34) | collective-permute-done | bytes 1048608 | tf_op jit(solution)/shard_map/ppermute | solution.py:470
  196.6 1.5 finish.1
  (92 shorter events, 1.6 us)
Async XLA Ops:
  0.6 11.4 %copy-start.8 = (bf16[1,512,1024]{2,1,0:T(8,128)(2,1)S(1)}, bf16[1,512,1024]{2,1,0:T(8,128)(2,1)}, u32[]{:S(2)}) copy-start(bf16[1,512,1024]{2,1,0:T(8,128)(2,1)} %param.14) | copy-start | bytes 3145732
  3.8 16.0 %collective-permute-start.2 = (bf16[8192,128]{1,0:T(8,128)(2,1)}, bf16[8192,128]{1,0:T(8,128)(2,1)}, u32[]{:S(2)}, u32[]{:S(2)}) collective-permute-start(bf16[8192,128]{1,0:T(8,128)(2,1)} %refs_4_.2), channel_id=1, source_target_pairs={{0,1},{1,0},{2,3},{3,2},{4,5},{5,4},{6,7},{7,6},{8,9},{9,8},{10,11... | collective-permute-start | bytes 6291464 | tf_op jit(solution)/shard_map/ppermute | solution.py:465
  3.8 15.9 %collective-permute-start = (bf16[32,8192]{1,0:T(8,128)(2,1)}, bf16[32,8192]{1,0:T(8,128)(2,1)S(1)}, u32[]{:S(2)}, u32[]{:S(2)}) collective-permute-start(bf16[32,8192]{1,0:T(8,128)(2,1)} %get-tuple-element.92), channel_id=1, source_target_pairs={{0,16},{16,8},{8,24},{24,0},{1,17},{17,9},{9,25},{25,1},{2,18},{18... | collective-permute-start | bytes 1572872 | tf_op jit(solution)/shard_map/ppermute | solution.py:470
  5.4 14.4 %collective-permute-start.1 = (bf16[32,8192]{1,0:T(8,128)(2,1)}, bf16[32,8192]{1,0:T(8,128)(2,1)}, u32[]{:S(2)}, u32[]{:S(2)}) collective-permute-start(bf16[32,8192]{1,0:T(8,128)(2,1)} %get-tuple-element.93), channel_id=1, source_target_pairs={{0,24},{16,0},{8,16},{24,8},{1,25},{17,1},{9,17},{25,9},{2,26},{18... | collective-permute-start | bytes 1572872 | tf_op jit(solution)/shard_map/ppermute | solution.py:470
  7.0 27.6 %collective-permute-start.5 = (bf16[64,8192]{1,0:T(8,128)(2,1)}, bf16[64,8192]{1,0:T(8,128)(2,1)S(1)}, u32[]{:S(2)}, u32[]{:S(2)}) collective-permute-start(bf16[64,8192]{1,0:T(8,128)(2,1)} %get-tuple-element.94.refs_0_), channel_id=1, source_target_pairs={{0,2},{2,4},{4,6},{6,0},{1,3},{3,5},{5,7},{7,1},{8,10},{10,12},{12... | collective-permute-start | bytes 3145736 | tf_op jit(solution)/shard_map/ppermute | solution.py:470
  9.0 25.7 %collective-permute-start.6 = (bf16[64,8192]{1,0:T(8,128)(2,1)}, bf16[64,8192]{1,0:T(8,128)(2,1)}, u32[]{:S(2)}, u32[]{:S(2)}) collective-permute-start(bf16[64,8192]{1,0:T(8,128)(2,1)} %get-tuple-element.94.refs_0_), channel_id=1, source_target_pairs={{0,6},{2,0},{4,2},{6,4},{1,7},{3,1},{5,3},{7,5},{8,14},{10,8},{12,... | collective-permute-start | bytes 3145736 | tf_op jit(solution)/shard_map/ppermute | solution.py:470
  13.2 21.4 %copy-start.12 = (bf16[1024,128]{1,0:T(8,128)(2,1)}, bf16[1024,128]{1,0:T(8,128)(2,1)S(1)}, u32[]{:S(2)}) copy-start(bf16[1024,128]{1,0:T(8,128)(2,1)S(1)} %get-tuple-element.125) | copy-start | bytes 786436
  13.2 21.4 %copy-start.14 = (bf16[1024,128]{1,0:T(8,128)(2,1)}, bf16[1024,128]{1,0:T(8,128)(2,1)S(1)}, u32[]{:S(2)}) copy-start(bf16[1024,128]{1,0:T(8,128)(2,1)S(1)} %get-tuple-element.118) | copy-start | bytes 786436
  13.3 21.4 %copy-start.16 = (bf16[1024,128]{1,0:T(8,128)(2,1)}, bf16[1024,128]{1,0:T(8,128)(2,1)S(1)}, u32[]{:S(2)}) copy-start(bf16[1024,128]{1,0:T(8,128)(2,1)S(1)} %get-tuple-element.117) | copy-start | bytes 786436
  19.8 34.1 %collective-permute-start.11 = (bf16[8192,512]{1,0:T(8,128)(2,1)}, bf16[8192,512]{1,0:T(8,128)(2,1)}, u32[]{:S(2)}, u32[]{:S(2)}) collective-permute-start(bf16[8192,512]{1,0:T(8,128)(2,1)} %refs_2_), channel_id=1, source_target_pairs={{0,1},{1,0},{2,3},{3,2},{4,5},{5,4},{6,7},{7,6},{8,9},{9,8},{10,11... | collective-permute-start | bytes 25165832 | tf_op jit(solution)/shard_map/ppermute | solution.py:465
  19.8 20.8 %collective-permute-start.4 = (bf16[32,8192]{1,0:T(8,128)(2,1)}, bf16[32,8192]{1,0:T(8,128)(2,1)S(1)}, u32[]{:S(2)}, u32[]{:S(2)}) collective-permute-start(bf16[32,8192]{1,0:T(8,128)(2,1)} %collective-permute-done.1), channel_id=1, source_target_pairs={{0,24},{16,0},{8,16},{24,8},{1,25},{17,1},{9,17},{25,9},{2,26},{18... | collective-permute-start | bytes 1572872 | tf_op jit(solution)/shard_map/ppermute | solution.py:470
  22.7 17.8 %collective-permute-start.3 = (bf16[32,8192]{1,0:T(8,128)(2,1)S(1)}, bf16[32,8192]{1,0:T(8,128)(2,1)S(1)}, u32[]{:S(2)}, u32[]{:S(2)}) collective-permute-start(bf16[32,8192]{1,0:T(8,128)(2,1)S(1)} %collective-permute-done), channel_id=1, source_target_pairs={{0,16},{16,8},{8,24},{24,0},{1,17},{17,9},{9,25},{25,1},{2,18},{18... | collective-permute-start | bytes 1572872 | tf_op jit(solution)/shard_map/ppermute | solution.py:470
  34.7 6.9 %copy-start.10 = (bf16[64,8192]{1,0:T(8,128)(2,1)}, bf16[64,8192]{1,0:T(8,128)(2,1)S(1)}, u32[]{:S(2)}) copy-start(bf16[64,8192]{1,0:T(8,128)(2,1)S(1)} %get-tuple-element.107.below_ref.refs_2_) | copy-start | bytes 3145732
  37.3 16.4 %collective-permute-start.9 = (bf16[32,8192]{1,0:T(8,128)(2,1)}, bf16[32,8192]{1,0:T(8,128)(2,1)}, u32[]{:S(2)}, u32[]{:S(2)}) collective-permute-start(bf16[32,8192]{1,0:T(8,128)(2,1)} %get-tuple-element.108), channel_id=1, source_target_pairs={{0,2},{2,4},{4,6},{6,0},{1,3},{3,5},{5,7},{7,1},{8,10},{10,12},{12... | collective-permute-start | bytes 1572872 | tf_op jit(solution)/shard_map/ppermute | solution.py:470
  38.7 15.2 %collective-permute-start.10 = (bf16[32,8192]{1,0:T(8,128)(2,1)}, bf16[32,8192]{1,0:T(8,128)(2,1)}, u32[]{:S(2)}, u32[]{:S(2)}) collective-permute-start(bf16[32,8192]{1,0:T(8,128)(2,1)} %get-tuple-element.109), channel_id=1, source_target_pairs={{0,6},{2,0},{4,2},{6,4},{1,7},{3,1},{5,3},{7,5},{8,14},{10,8},{12,... | collective-permute-start | bytes 1572872 | tf_op jit(solution)/shard_map/ppermute | solution.py:470
  41.6 32.3 %collective-permute-start.7 = (bf16[64,8192]{1,0:T(8,128)(2,1)}, bf16[64,8192]{1,0:T(8,128)(2,1)S(1)}, u32[]{:S(2)}, u32[]{:S(2)}) collective-permute-start(bf16[64,8192]{1,0:T(8,128)(2,1)} %pad_maximum_fusion.refs_0_), channel_id=1, source_target_pairs={{0,6},{2,0},{4,2},{6,4},{1,7},{3,1},{5,3},{7,5},{8,14},{10,8},{12,... | collective-permute-start | bytes 3145736 | tf_op jit(solution)/shard_map/ppermute | solution.py:470
  43.5 31.0 %collective-permute-start.8 = (bf16[64,8192]{1,0:T(8,128)(2,1)}, bf16[64,8192]{1,0:T(8,128)(2,1)S(1)}, u32[]{:S(2)}, u32[]{:S(2)}) collective-permute-start(bf16[64,8192]{1,0:T(8,128)(2,1)} %pad_maximum_fusion.refs_0_), channel_id=1, source_target_pairs={{0,2},{2,4},{4,6},{6,0},{1,3},{3,5},{5,7},{7,1},{8,10},{10,12},{12... | collective-permute-start | bytes 3145736 | tf_op jit(solution)/shard_map/ppermute | solution.py:470
  53.9 12.1 %copy-start.17 = (bf16[1024,128]{1,0:T(8,128)(2,1)S(1)}, bf16[1024,128]{1,0:T(8,128)(2,1)}, u32[]{:S(2)}) copy-start(bf16[1024,128]{1,0:T(8,128)(2,1)} %copy-done.16) | copy-start | bytes 786436
  53.9 13.7 %copy-start.15 = (bf16[1024,128]{1,0:T(8,128)(2,1)S(1)}, bf16[1024,128]{1,0:T(8,128)(2,1)}, u32[]{:S(2)}) copy-start(bf16[1024,128]{1,0:T(8,128)(2,1)} %copy-done.14) | copy-start | bytes 786436
  66.0 12.7 %copy-start.13 = (bf16[1024,128]{1,0:T(8,128)(2,1)S(1)}, bf16[1024,128]{1,0:T(8,128)(2,1)}, u32[]{:S(2)}) copy-start(bf16[1024,128]{1,0:T(8,128)(2,1)} %copy-done.12) | copy-start | bytes 786436
  66.0 14.3 %copy-start.22 = (bf16[256,256]{1,0:T(8,128)(2,1)S(1)}, bf16[256,256]{1,0:T(8,128)(2,1)}, u32[]{:S(2)}) copy-start(bf16[256,256]{1,0:T(8,128)(2,1)} %get-tuple-element.132.refs_3_) | copy-start | bytes 393220
  66.0 8.5 %collective-permute-start.12 = (bf16[1024,128]{1,0:T(8,128)(2,1)S(1)}, bf16[1024,128]{1,0:T(8,128)(2,1)S(1)}, u32[]{:S(2)}, u32[]{:S(2)}) collective-permute-start(bf16[1024,128]{1,0:T(8,128)(2,1)S(1)} %copy-done.17), channel_id=1, source_target_pairs={{0,32},{32,64},{64,96},{96,0},{1,33},{33,65},{65,97},{97,1},{2,34}... | collective-permute-start | bytes 786440 | tf_op jit(solution)/shard_map/ppermute | solution.py:470
  67.5 7.0 %collective-permute-start.13 = (bf16[1024,128]{1,0:T(8,128)(2,1)S(1)}, bf16[1024,128]{1,0:T(8,128)(2,1)S(1)}, u32[]{:S(2)}, u32[]{:S(2)}) collective-permute-start(bf16[1024,128]{1,0:T(8,128)(2,1)S(1)} %copy-done.15), channel_id=1, source_target_pairs={{0,96},{32,0},{64,32},{96,64},{1,97},{33,1},{65,33},{97,65},{2,98}... | collective-permute-start | bytes 786440 | tf_op jit(solution)/shard_map/ppermute | solution.py:470
  73.9 6.4 %copy-start.1 = (bf16[64,8192]{1,0:T(8,128)(2,1)}, bf16[64,8192]{1,0:T(8,128)(2,1)S(1)}, u32[]{:S(2)}) copy-start(bf16[64,8192]{1,0:T(8,128)(2,1)S(1)} %collective-permute-done.7.above_ref.refs_1_) | copy-start | bytes 3145732
  74.5 5.8 %copy-start.2 = (bf16[64,8192]{1,0:T(8,128)(2,1)}, bf16[64,8192]{1,0:T(8,128)(2,1)S(1)}, u32[]{:S(2)}) copy-start(bf16[64,8192]{1,0:T(8,128)(2,1)S(1)} %collective-permute-done.8.below_ref.refs_2_) | copy-start | bytes 3145732
  74.5 0.8 copy-start.20
  75.3 28.6 %collective-permute-start.20 = (bf16[512,8192]{1,0:T(8,128)(2,1)}, bf16[512,8192]{1,0:T(8,128)(2,1)}, u32[]{:S(2)}, u32[]{:S(2)}) collective-permute-start(bf16[512,8192]{1,0:T(8,128)(2,1)} %refs_0_), channel_id=1, source_target_pairs={{0,1},{1,0},{2,3},{3,2},{4,5},{5,4},{6,7},{7,6},{8,9},{9,8},{10,11... | collective-permute-start | bytes 25165832 | tf_op jit(solution)/shard_map/ppermute | solution.py:465
  75.3 3.4 %copy-start.21 = (bf16[1024,128]{1,0:T(8,128)(2,1)S(1)}, bf16[1024,128]{1,0:T(8,128)(2,1)}, u32[]{:S(2)}) copy-start(bf16[1024,128]{1,0:T(8,128)(2,1)} %copy-done.20) | copy-start | bytes 786436
  75.4 16.2 %collective-permute-start.14 = (bf16[32,8192]{1,0:T(8,128)(2,1)S(1)}, bf16[32,8192]{1,0:T(8,128)(2,1)S(1)}, u32[]{:S(2)}, u32[]{:S(2)}) collective-permute-start(bf16[32,8192]{1,0:T(8,128)(2,1)S(1)} %get-tuple-element.123), channel_id=1, source_target_pairs={{0,2},{2,4},{4,6},{6,0},{1,3},{3,5},{5,7},{7,1},{8,10},{10,12},{12... | collective-permute-start | bytes 1572872 | tf_op jit(solution)/shard_map/ppermute | solution.py:470
  76.3 15.2 %collective-permute-start.15 = (bf16[32,8192]{1,0:T(8,128)(2,1)S(1)}, bf16[32,8192]{1,0:T(8,128)(2,1)S(1)}, u32[]{:S(2)}, u32[]{:S(2)}) collective-permute-start(bf16[32,8192]{1,0:T(8,128)(2,1)S(1)} %get-tuple-element.124), channel_id=1, source_target_pairs={{0,6},{2,0},{4,2},{6,4},{1,7},{3,1},{5,3},{7,5},{8,14},{10,8},{12,... | collective-permute-start | bytes 1572872 | tf_op jit(solution)/shard_map/ppermute | solution.py:470
  78.7 12.2 %collective-permute-start.16 = (bf16[1024,128]{1,0:T(8,128)(2,1)S(1)}, bf16[1024,128]{1,0:T(8,128)(2,1)S(1)}, u32[]{:S(2)}, u32[]{:S(2)}) collective-permute-start(bf16[1024,128]{1,0:T(8,128)(2,1)S(1)} %add_convert_fusion), channel_id=1, source_target_pairs={{0,32},{32,64},{64,96},{96,0},{1,33},{33,65},{65,97},{97,1},{2,34}... | collective-permute-start | bytes 786440 | tf_op jit(solution)/shard_map/ppermute | solution.py:470
  80.3 22.9 %collective-permute-start.17 = (bf16[256,256]{1,0:T(8,128)(2,1)S(1)}, bf16[256,256]{1,0:T(8,128)(2,1)}, u32[]{:S(2)}, u32[]{:S(2)}) collective-permute-start(bf16[256,256]{1,0:T(8,128)(2,1)S(1)} %copy-done.22), channel_id=1, source_target_pairs={{0,1},{1,0},{2,3},{3,2},{4,5},{5,4},{6,7},{7,6},{8,9},{9,8},{10,11... | collective-permute-start | bytes 393224 | tf_op jit(solution)/shard_map/ppermute | solution.py:465
  91.0 12.2 %collective-permute-start.18 = (bf16[192,256]{1,0:T(8,128)(2,1)}, bf16[192,256]{1,0:T(8,128)(2,1)S(1)}, u32[]{:S(2)}, u32[]{:S(2)}) collective-permute-start(bf16[192,256]{1,0:T(8,128)(2,1)} %get-tuple-element.133.refs_4_), channel_id=1, source_target_pairs={{0,1},{1,0},{2,3},{3,2},{4,5},{5,4},{6,7},{7,6},{8,9},{9,8},{10,11... | collective-permute-start | bytes 294920 | tf_op jit(solution)/shard_map/ppermute | solution.py:465
  91.5 0.8 copy-start.18
  91.5 1.0 copy-start.19
  102.2 1.7 collective-permute-start.19
  103.2 0.6 copy-start.23
  118.8 15.5 %collective-permute-start.21 = (bf16[64,4096]{1,0:T(8,128)(2,1)}, bf16[64,4096]{1,0:T(8,128)(2,1)S(1)}, u32[]{:S(2)}, u32[]{:S(2)}) collective-permute-start(bf16[64,4096]{1,0:T(8,128)(2,1)} %get-tuple-element.139), channel_id=1, source_target_pairs={{0,2},{2,4},{4,6},{6,0},{1,3},{3,5},{5,7},{7,1},{8,10},{10,12},{12... | collective-permute-start | bytes 1572872 | tf_op jit(solution)/shard_map/ppermute | solution.py:470
  119.3 15.0 %collective-permute-start.22 = (bf16[64,4096]{1,0:T(8,128)(2,1)}, bf16[64,4096]{1,0:T(8,128)(2,1)S(1)}, u32[]{:S(2)}, u32[]{:S(2)}) collective-permute-start(bf16[64,4096]{1,0:T(8,128)(2,1)} %get-tuple-element.140), channel_id=1, source_target_pairs={{0,6},{2,0},{4,2},{6,4},{1,7},{3,1},{5,3},{7,5},{8,14},{10,8},{12,... | collective-permute-start | bytes 1572872 | tf_op jit(solution)/shard_map/ppermute | solution.py:470
  122.1 12.1 %copy-start.6 = (bf16[64,8192]{1,0:T(8,128)(2,1)S(1)}, bf16[64,8192]{1,0:T(8,128)(2,1)}, u32[]{:S(2)}) copy-start(bf16[64,8192]{1,0:T(8,128)(2,1)} %get-tuple-element.149.refs_0_) | copy-start | bytes 3145732
  122.1 12.1 %copy-start.7 = (bf16[64,8192]{1,0:T(8,128)(2,1)S(1)}, bf16[64,8192]{1,0:T(8,128)(2,1)}, u32[]{:S(2)}) copy-start(bf16[64,8192]{1,0:T(8,128)(2,1)} %get-tuple-element.151.refs_2_) | copy-start | bytes 3145732
  122.2 12.4 %collective-permute-start.23 = (bf16[512,128]{1,0:T(8,128)(2,1)S(1)}, bf16[512,128]{1,0:T(8,128)(2,1)S(1)}, u32[]{:S(2)}, u32[]{:S(2)}) collective-permute-start(bf16[512,128]{1,0:T(8,128)(2,1)S(1)} %add_convert_fusion.1), channel_id=1, source_target_pairs={{0,16},{16,0},{1,17},{17,1},{2,18},{18,2},{3,19},{19,3},{4,20},{20... | collective-permute-start | bytes 393224 | tf_op jit(solution)/shard_map/ppermute | solution.py:465
  133.2 4.7 %copy-start.26 = (bf16[64,4096]{1,0:T(8,128)(2,1)S(1)}, bf16[64,4096]{1,0:T(8,128)(2,1)}, u32[]{:S(2)}) copy-start(bf16[64,4096]{1,0:T(8,128)(2,1)} %get-tuple-element.172) | copy-start | bytes 1572868
  133.3 4.8 %copy-start.25 = (bf16[64,4096]{1,0:T(8,128)(2,1)S(1)}, bf16[64,4096]{1,0:T(8,128)(2,1)}, u32[]{:S(2)}) copy-start(bf16[64,4096]{1,0:T(8,128)(2,1)} %get-tuple-element.174) | copy-start | bytes 1572868
  133.3 8.0 %copy-start.11 = (f32[512,128]{1,0:T(8,128)S(1)}, f32[512,128]{1,0:T(8,128)}, u32[]{:S(2)}) copy-start(f32[512,128]{1,0:T(8,128)} %refs_4_.3) | copy-start | bytes 786436
  134.3 27.7 %copy-start = (bf16[64,8192]{1,0:T(8,128)(2,1)S(1)}, bf16[64,8192]{1,0:T(8,128)(2,1)}, u32[]{:S(2)}) copy-start(bf16[64,8192]{1,0:T(8,128)(2,1)} %get-tuple-element.163.refs_0_.refs_3_) | copy-start | bytes 3145732
  134.6 27.4 %collective-permute-start.24 = (bf16[64,8192]{1,0:T(8,128)(2,1)S(1)}, bf16[64,8192]{1,0:T(8,128)(2,1)S(1)}, u32[]{:S(2)}, u32[]{:S(2)}) collective-permute-start(bf16[64,8192]{1,0:T(8,128)(2,1)S(1)} %get-tuple-element.158), channel_id=1, source_target_pairs={{0,2},{2,4},{4,6},{6,0},{1,3},{3,5},{5,7},{7,1},{8,10},{10,12},{12... | collective-permute-start | bytes 3145736 | tf_op jit(solution)/shard_map/ppermute | solution.py:470
  135.3 26.7 %collective-permute-start.25 = (bf16[64,8192]{1,0:T(8,128)(2,1)S(1)}, bf16[64,8192]{1,0:T(8,128)(2,1)S(1)}, u32[]{:S(2)}, u32[]{:S(2)}) collective-permute-start(bf16[64,8192]{1,0:T(8,128)(2,1)S(1)} %get-tuple-element.159), channel_id=1, source_target_pairs={{0,6},{2,0},{4,2},{6,4},{1,7},{3,1},{5,3},{7,5},{8,14},{10,8},{12,... | collective-permute-start | bytes 3145736 | tf_op jit(solution)/shard_map/ppermute | solution.py:470
  138.0 33.5 %collective-permute-start.32 = (bf16[64,4096]{1,0:T(8,128)(2,1)S(1)}, bf16[64,4096]{1,0:T(8,128)(2,1)S(1)}, u32[]{:S(2)}, u32[]{:S(2)}) collective-permute-start(bf16[64,4096]{1,0:T(8,128)(2,1)S(1)} %copy-done.26), channel_id=1, source_target_pairs={{0,2},{2,4},{4,6},{6,0},{1,3},{3,5},{5,7},{7,1},{8,10},{10,12},{12... | collective-permute-start | bytes 1572872 | tf_op jit(solution)/shard_map/ppermute | solution.py:470
  138.1 33.4 %collective-permute-start.33 = (bf16[64,4096]{1,0:T(8,128)(2,1)S(1)}, bf16[64,4096]{1,0:T(8,128)(2,1)S(1)}, u32[]{:S(2)}, u32[]{:S(2)}) collective-permute-start(bf16[64,4096]{1,0:T(8,128)(2,1)S(1)} %copy-done.25), channel_id=1, source_target_pairs={{0,6},{2,0},{4,2},{6,4},{1,7},{3,1},{5,3},{7,5},{8,14},{10,8},{12,... | collective-permute-start | bytes 1572872 | tf_op jit(solution)/shard_map/ppermute | solution.py:470
  142.7 5.0 %collective-permute-start.26 = (bf16[512,128]{1,0:T(8,128)(2,1)S(1)}, bf16[512,128]{1,0:T(8,128)(2,1)S(1)}, u32[]{:S(2)}, u32[]{:S(2)}) collective-permute-start(bf16[512,128]{1,0:T(8,128)(2,1)S(1)} %get-tuple-element.161), channel_id=1, source_target_pairs={{0,16},{16,0},{1,17},{17,1},{2,18},{18,2},{3,19},{19,3},{4,20},{20... | collective-permute-start | bytes 393224 | tf_op jit(solution)/shard_map/ppermute | solution.py:465
  147.8 23.7 %copy-start.4 = (bf16[64,8192]{1,0:T(8,128)(2,1)S(1)}, bf16[64,8192]{1,0:T(8,128)(2,1)}, u32[]{:S(2)}) copy-start(bf16[64,8192]{1,0:T(8,128)(2,1)} %get-tuple-element.171.refs_0_) | copy-start | bytes 3145732
  147.8 23.7 %copy-start.5 = (bf16[64,8192]{1,0:T(8,128)(2,1)S(1)}, bf16[64,8192]{1,0:T(8,128)(2,1)}, u32[]{:S(2)}) copy-start(bf16[64,8192]{1,0:T(8,128)(2,1)} %get-tuple-element.173.refs_2_) | copy-start | bytes 3145732
  147.8 7.7 %collective-permute-start.27 = (bf16[1024,128]{1,0:T(8,128)(2,1)S(1)}, bf16[1024,128]{1,0:T(8,128)(2,1)S(1)}, u32[]{:S(2)}, u32[]{:S(2)}) collective-permute-start(bf16[1024,128]{1,0:T(8,128)(2,1)S(1)} %constant_dynamic-update-slice_fusion.refs_0_), channel_id=1, source_target_pairs={{0,32},{32,64},{64,96},{96,0},{1,33},{33,65},{65,97},{97,1},{2,34}... | collective-permute-start | bytes 786440 | tf_op jit(solution)/shard_map/ppermute | solution.py:470
  162.3 26.9 %copy-start.9 = (bf16[512,1024]{1,0:T(8,128)(2,1)S(1)}, bf16[512,1024]{1,0:T(8,128)(2,1)}, u32[]{:S(2)}) copy-start(bf16[512,1024]{1,0:T(8,128)(2,1)} %params_ref.1) | copy-start | bytes 3145732
  162.3 14.9 %collective-permute-start.29 = (bf16[64,4096]{1,0:T(8,128)(2,1)S(1)}, bf16[64,4096]{1,0:T(8,128)(2,1)S(1)}, u32[]{:S(2)}, u32[]{:S(2)}) collective-permute-start(bf16[64,4096]{1,0:T(8,128)(2,1)S(1)} %get-tuple-element.166.refs_4_), channel_id=1, source_target_pairs={{0,16},{16,8},{8,24},{24,0},{1,17},{17,9},{9,25},{25,1},{2,18},{18... | collective-permute-start | bytes 1572872 | tf_op jit(solution)/shard_map/ppermute | solution.py:470
  163.3 14.0 %collective-permute-start.30 = (bf16[64,4096]{1,0:T(8,128)(2,1)S(1)}, bf16[64,4096]{1,0:T(8,128)(2,1)S(1)}, u32[]{:S(2)}, u32[]{:S(2)}) collective-permute-start(bf16[64,4096]{1,0:T(8,128)(2,1)S(1)} %get-tuple-element.167), channel_id=1, source_target_pairs={{0,24},{16,0},{8,16},{24,8},{1,25},{17,1},{9,17},{25,9},{2,26},{18... | collective-permute-start | bytes 1572872 | tf_op jit(solution)/shard_map/ppermute | solution.py:470
  171.8 24.8 %copy-start.3 = (bf16[64,8192]{1,0:T(8,128)(2,1)S(1)}, bf16[64,8192]{1,0:T(8,128)(2,1)}, u32[]{:S(2)}) copy-start(bf16[64,8192]{1,0:T(8,128)(2,1)} %get-tuple-element.170.refs_0_) | copy-start | bytes 3145732
  171.8 24.8 %collective-permute-start.34 = (bf16[64,8192]{1,0:T(8,128)(2,1)S(1)}, bf16[64,8192]{1,0:T(8,128)(2,1)S(1)}, u32[]{:S(2)}, u32[]{:S(2)}) collective-permute-start(bf16[64,8192]{1,0:T(8,128)(2,1)S(1)} %get-tuple-element.175), channel_id=1, source_target_pairs={{0,2},{2,4},{4,6},{6,0},{1,3},{3,5},{5,7},{7,1},{8,10},{10,12},{12... | collective-permute-start | bytes 3145736 | tf_op jit(solution)/shard_map/ppermute | solution.py:470
  172.7 23.9 %collective-permute-start.35 = (bf16[64,8192]{1,0:T(8,128)(2,1)S(1)}, bf16[64,8192]{1,0:T(8,128)(2,1)S(1)}, u32[]{:S(2)}, u32[]{:S(2)}) collective-permute-start(bf16[64,8192]{1,0:T(8,128)(2,1)S(1)} %get-tuple-element.176), channel_id=1, source_target_pairs={{0,6},{2,0},{4,2},{6,4},{1,7},{3,1},{5,3},{7,5},{8,14},{10,8},{12,... | collective-permute-start | bytes 3145736 | tf_op jit(solution)/shard_map/ppermute | solution.py:470
  175.1 6.4 %collective-permute-start.28 = (bf16[1024,128]{1,0:T(8,128)(2,1)S(1)}, bf16[1024,128]{1,0:T(8,128)(2,1)S(1)}, u32[]{:S(2)}, u32[]{:S(2)}) collective-permute-start(bf16[1024,128]{1,0:T(8,128)(2,1)S(1)} %constant_dynamic-update-slice_fusion.refs_0_), channel_id=1, source_target_pairs={{0,96},{32,0},{64,32},{96,64},{1,97},{33,1},{65,33},{97,65},{2,98}... | collective-permute-start | bytes 786440 | tf_op jit(solution)/shard_map/ppermute | solution.py:470
  177.3 19.3 %collective-permute-start.36 = (bf16[64,4096]{1,0:T(8,128)(2,1)S(1)}, bf16[64,4096]{1,0:T(8,128)(2,1)S(1)}, u32[]{:S(2)}, u32[]{:S(2)}) collective-permute-start(bf16[64,4096]{1,0:T(8,128)(2,1)S(1)} %collective-permute-done.29), channel_id=1, source_target_pairs={{0,16},{16,8},{8,24},{24,0},{1,17},{17,9},{9,25},{25,1},{2,18},{18... | collective-permute-start | bytes 1572872 | tf_op jit(solution)/shard_map/ppermute | solution.py:470
  178.0 18.6 %collective-permute-start.37 = (bf16[64,4096]{1,0:T(8,128)(2,1)S(1)}, bf16[64,4096]{1,0:T(8,128)(2,1)S(1)}, u32[]{:S(2)}, u32[]{:S(2)}) collective-permute-start(bf16[64,4096]{1,0:T(8,128)(2,1)S(1)} %collective-permute-done.30), channel_id=1, source_target_pairs={{0,24},{16,0},{8,16},{24,8},{1,25},{17,1},{9,17},{25,9},{2,26},{18... | collective-permute-start | bytes 1572872 | tf_op jit(solution)/shard_map/ppermute | solution.py:470
  181.5 7.8 %collective-permute-start.31 = (bf16[1024,128]{1,0:T(8,128)(2,1)S(1)}, bf16[1024,128]{1,0:T(8,128)(2,1)S(1)}, u32[]{:S(2)}, u32[]{:S(2)}) collective-permute-start(bf16[1024,128]{1,0:T(8,128)(2,1)S(1)} %collective-permute-done.27.refs_2_), channel_id=1, source_target_pairs={{0,32},{32,64},{64,96},{96,0},{1,33},{33,65},{65,97},{97,1},{2,34}... | collective-permute-start | bytes 786440 | tf_op jit(solution)/shard_map/ppermute | solution.py:470
  (1 other events, 0.6 us)

commit v2 on v1

--- a/solution.py
+++ b/solution.py
@@ -321,15 +321,17 @@
 
 
 def pick_body(below_ref, above_ref, first_ref, second_ref):
-    count = first_ref.shape[0]
-    first_ref[...] = below_ref[:count]
-    second_ref[...] = above_ref[count:]
+    first_ref[...] = below_ref[...]
+    second_ref[...] = above_ref[...]
 
 
 def pick(below, above):
     shape = jax.ShapeDtypeStruct((below.shape[0] // HALVES, below.shape[1]), below.dtype)
     return pl.pallas_call(
         pick_body,
+        grid=(1,),
+        in_specs=[pl.BlockSpec(shape.shape, lambda i, at=at: (at, 0)) for at in range(HALVES)],
+        out_specs=[pl.BlockSpec(shape.shape, lambda i: (0, 0))] * HALVES,
         out_shape=[shape, shape],
         compiler_params=params(),
         cost_estimate=cost(1e8, 4 * below.size),
@@ -517,29 +519,28 @@
     far1, far2 = hop(far1, "z", 1), hop(far2, "z", -1)
     pbelow, pabove = hop(partner, "z", 1), hop(partner, "z", -1)
     weights = [query_weight, query_theirs, kv_weight, kv_theirs]
-    query_a, pair_a = project(core, [block, above, below, far1, far2], weights)
+    query_a, pair_a = project(core, [block, above, below, far1, far2, partner], weights)
     query_a, far1, far2, at2, at3 = wait(query_a, far1, far2, at2, at3)
     x2, x3 = hop(at2, "x", 1), hop(at3, "x", -1)
-    pabove, pbelow, query_a, pair_a, x2, x3, at1, out_weight = wait(
-        pabove, pbelow, query_a, pair_a, x2, x3, at1, out_weight
+    pabove, pbelow, query_a, pair_a, x2, x3, at1, out_weight, places = wait(
+        pabove, pbelow, query_a, pair_a, x2, x3, at1, out_weight, places
     )
     pfar1, pfar2 = pick(pbelow, pabove)
     pfar1, pfar2 = hop(pfar1, "z", 1), hop(pfar2, "z", -1)
     out_theirs = swap(out_weight, "core")
-    query_m, pair_m = project(core, [partner, pabove, pbelow], weights)
     passed = hop(add(at1, x2), "x", 1)
-    other_a, other_m = swap(pair_a, "core"), swap(pair_m, "core")
-    pfar1, pfar2, passed, query_m = wait(pfar1, pfar2, passed, query_m)
-    query_l, pair_l = project(core, [pfar1, pfar2], weights)
+    other_a = swap(pair_a, "core")
+    pfar1, pfar2, passed, other_a = wait(pfar1, pfar2, passed, other_a)
+    query_l, pair_l = project(core, [pabove, pbelow, pfar1, pfar2], weights)
     other_l = swap(pair_l, "core")
     out_weights = (out_weight, out_theirs)
     mixed, q0, qup, qdown, far_a, far_b = attend(
         core,
         places,
         tuple(range(8)),
-        (query_a, query_m, query_l),
-        (pair_a, pair_m, pair_l),
-        (other_a, other_m, other_l),
+        (query_a, query_l),
+        (pair_a, pair_l),
+        (other_a, other_l),
         out_weights,
     )
 

time: 198 us -> 199 us (level)
  Pallas kernels: 70.1 us -> 60.8 us
  waiting for transfers between devices: 70.6 us -> 78.7 us
    ppermute x8 -> x7, waiting for transfers between devices: 4.93 us -> 13.2 us  [swap(): return lax.ppermute(block, axis, [(0, 1), (1, 0)])]
    pallas_call x3 -> x2, Pallas kernels: 32.3 us -> 24.4 us  [project(): pl.pallas_call(project_body, in_specs=[pl.BlockSpec(memory_space=pltpu.SM...]
  transfers between devices with their start and end apart: 38 -> 37, of which waited for: 16 -> 20; matrix products, arithmetic and copies ran while one was open for 1% -> 2% of each run, Pallas kernels for 26% -> 21%
where the time goes in v2:
time: 199 us
  waiting for transfers between devices  78.7 us (40%)
  Pallas kernels  60.8 us (31%)
  starting transfers between devices  51.4 us (26%)
  local copies, waits for them, and re-layouts  4.74 us (2%)
  other arithmetic  2.24 us (1%)
    ppermute x30, waiting for transfers between devices, hop(): lax.ppermute(block, axis, [(at[i], at[(i + way) % 4]) for i in range(4)])  65.5 us
    ppermute x30, starting transfers between devices, hop(): lax.ppermute(block, axis, [(at[i], at[(i + way) % 4]) for i in range(4)])  50.1 us
    pallas_call x2, Pallas kernels, project(): pl.pallas_call(project_body, in_specs=[pl.BlockSpec(memory_space=pltpu.SM...  24.4 us
    pallas_call x1, Pallas kernels, attend(): pl.pallas_call(functools.partial(attend_body, order), in_specs=[pl.BlockS...  14.2 us
    ppermute x7, waiting for transfers between devices, swap(): return lax.ppermute(block, axis, [(0, 1), (1, 0)])  13.2 us
    pallas_call x1, Pallas kernels, output(): pl.pallas_call(output_body, in_specs=[vmem] + [pl.BlockSpec(memory_space=...  10.7 us
    unnamed x56, local copies, waits for them, and re-layouts  4 us
  transfers between devices with their start and end apart: 37, of which 20 were waited for; matrix products, arithmetic and copies ran while one was open for 2% of the time, Pallas kernels for 21%

profile of v2, /device:TPU:0, one launch (start us, length us, event | category | flops | bytes accessed | tf_op | source)
XLA Modules:
  0.0 198.9 jit_solution(8258946797658478333)
XLA Ops:
  0.6 3.1 %normalize.1 = (bf16[64,8192]{1,0:T(8,128)(2,1)}, bf16[32,8192]{1,0:T(8,128)(2,1)}, bf16[32,8192]{1,0:T(8,128)(2,1)}) custom-call(bf16[64,8192]{1,0:T(8,128)(2,1)} %rows_ref.1, f32[1,8192]{1,0:T(1,128)} %bitcast.22), custom_call_target="tpu_custom_call" | custom-call | flops 2097152 | bytes 3145728 | tf_op jit(solution)/shard_map/normalize/pallas_call | solution.py:54
  3.8 1.7 collective-permute-start
  5.4 1.6 collective-permute-start.1
  7.0 2.0 collective-permute-start.5
  9.0 2.1 %collective-permute-start.6 = (bf16[64,8192]{1,0:T(8,128)(2,1)}, bf16[64,8192]{1,0:T(8,128)(2,1)}, u32[]{:S(2)}, u32[]{:S(2)}) collective-permute-start(bf16[64,8192]{1,0:T(8,128)(2,1)} %get-tuple-element.93.refs_0_), channel_id=1, source_target_pairs={{0,6},{2,0},{4,2},{6,4},{1,7},{3,1},{5,3},{7,5},{8,14},{10,8},{12,... | collective-permute-start | bytes 3145736 | tf_op jit(solution)/shard_map/ppermute | solution.py:472
  11.1 0.8 copy.14
  12.1 1.2 terms.1
  13.3 6.5 %collective-permute-done = bf16[32,8192]{1,0:T(8,128)(2,1)} collective-permute-done((bf16[32,8192]{1,0:T(8,128)(2,1)}, bf16[32,8192]{1,0:T(8,128)(2,1)}, u32[]{:S(2)}, u32[]{:S(2)}) %collective-permute-start) | collective-permute-done | bytes 524320 | tf_op jit(solution)/shard_map/ppermute | solution.py:472
  19.8 2.9 %collective-permute-start.4 = (bf16[32,8192]{1,0:T(8,128)(2,1)}, bf16[32,8192]{1,0:T(8,128)(2,1)S(1)}, u32[]{:S(2)}, u32[]{:S(2)}) collective-permute-start(bf16[32,8192]{1,0:T(8,128)(2,1)} %collective-permute-done.1), channel_id=1, source_target_pairs={{0,24},{16,0},{8,16},{24,8},{1,25},{17,1},{9,17},{25,9},{2,26},{18... | collective-permute-start | bytes 1572872 | tf_op jit(solution)/shard_map/ppermute | solution.py:472
  22.7 11.9 %collective-permute-done.5.refs_0_ = bf16[64,8192]{1,0:T(8,128)(2,1)S(1)} collective-permute-done((bf16[64,8192]{1,0:T(8,128)(2,1)}, bf16[64,8192]{1,0:T(8,128)(2,1)S(1)}, u32[]{:S(2)}, u32[]{:S(2)}) %collective-permute-start.5) | collective-permute-done | bytes 1048608 | tf_op jit(solution)/shard_map/ppermute | solution.py:472
  34.7 1.5 pick.2
  36.2 1.4 collective-permute-start.9
  37.6 1.9 collective-permute-start.10
  39.5 1.1 pad_maximum_fusion.refs_5_
  40.6 2.7 %collective-permute-start.7 = (bf16[64,8192]{1,0:T(8,128)(2,1)}, bf16[64,8192]{1,0:T(8,128)(2,1)S(1)}, u32[]{:S(2)}, u32[]{:S(2)}) collective-permute-start(bf16[64,8192]{1,0:T(8,128)(2,1)} %pad_maximum_fusion.refs_5_), channel_id=1, source_target_pairs={{0,6},{2,0},{4,2},{6,4},{1,7},{3,1},{5,3},{7,5},{8,14},{10,8},{12,... | collective-permute-start | bytes 3145736 | tf_op jit(solution)/shard_map/ppermute | solution.py:472
  43.3 9.0 %collective-permute-done.9.refs_3_ = bf16[32,8192]{1,0:T(8,128)(2,1)S(1)} collective-permute-done((bf16[32,8192]{1,0:T(8,128)(2,1)S(1)}, bf16[32,8192]{1,0:T(8,128)(2,1)S(1)}, u32[]{:S(2)}, u32[]{:S(2)}) %collective-permute-start.9) | collective-permute-done | bytes 524320 | tf_op jit(solution)/shard_map/ppermute | solution.py:472
  52.5 0.6 copy-done.25
  53.3 13.9 %project.2 = (bf16[320,1024]{1,0:T(8,128)(2,1)}, bf16[320,256]{1,0:T(8,128)(2,1)}) custom-call(s32[1]{0:T(128)} %bitcast.core_ref, bf16[64,8192]{1,0:T(8,128)(2,1)} %get-tuple-element.93.refs_0_, bf16[64,8192]{1,0:T(8,128)(2,1)} %get-tuple-element.105.above_ref.refs_1_, bf16[64,8192]{1,0:T(8,128)(2,1)} %copy-done.10, bf16[32,8192]{1,0:T(8,128)(2,1)} %copy-done.25, ...), custom_call_target="tpu_custom_call" | custom-call | flops 10066329600 | bytes 26214400 | tf_op jit(solution)/shard_map/project/pallas_call | solution.py:114
  67.2 1.6 collective-permute-start.12
  68.8 1.7 collective-permute-start.13
  70.5 0.6 concatenate.10.place_ref
  71.2 1.4 collective-permute-done.7.above_ref.refs_0_
  72.6 0.6 collective-permute-done.8.below_ref.refs_1_
  73.2 1.7 collective-permute-done.12
  75.2 1.6 collective-permute-start.14
  76.9 1.7 collective-permute-start.15
  78.5 1.0 add_convert_fusion
  79.6 1.6 collective-permute-start.16
  81.2 7.4 %collective-permute-done.17.refs_4_ = bf16[320,256]{1,0:T(8,128)(2,1)S(1)} collective-permute-done((bf16[320,256]{1,0:T(8,128)(2,1)S(1)}, bf16[320,256]{1,0:T(8,128)(2,1)S(1)}, u32[]{:S(2)}, u32[]{:S(2)}) %collective-permute-start.17) | collective-permute-done | bytes 163872 | tf_op jit(solution)/shard_map/ppermute | solution.py:467
  88.5 0.7 collective-permute-done.16.refs_1_
  89.2 1.7 collective-permute-done.14.refs_2_
  91.0 0.8 copy-done.18
  91.7 0.8 copy-done.19
  92.5 10.6 %project.3 = (bf16[192,1024]{1,0:T(8,128)(2,1)}, bf16[192,256]{1,0:T(8,128)(2,1)}) custom-call(s32[1]{0:T(128)} %bitcast.core_ref, bf16[64,8192]{1,0:T(8,128)(2,1)} %copy-done.1, bf16[64,8192]{1,0:T(8,128)(2,1)} %copy-done.2, bf16[32,8192]{1,0:T(8,128)(2,1)} %copy-done.18, bf16[32,8192]{1,0:T(8,128)(2,1)} %copy-done.19, bf16[8192,512]{1,0:T(8,128)(2,1)} %refs_4_.1, ...), custom_call_target="tpu_custom_call" | custom-call | flops 6039797760 | bytes 24117248 | tf_op jit(solution)/shard_map/project/pallas_call | solution.py:114
  103.4 1.5 collective-permute-done.18.refs_5_
  104.9 0.6 copy-done.22
  105.5 14.2 %attend.1 = (bf16[512,1024]{1,0:T(8,128)(2,1)}, bf16[64,8192]{1,0:T(8,128)(2,1)}, bf16[64,8192]{1,0:T(8,128)(2,1)}, bf16[64,8192]{1,0:T(8,128)(2,1)}, bf16[64,40...) custom-call(s32[1]{0:T(128)} %bitcast.core_ref, s32[16]{0:T(128)} %concatenate.10.place_ref, ...), custom_call_target="tpu_custom_call" | custom-call | flops 2147483648 | bytes 18874368 | tf_op jit(solution)/shard_map/attend/pallas_call | solution.py:250
  119.7 0.8 collective-permute-start.20
  120.5 2.5 %collective-permute-start.21 = (bf16[64,4096]{1,0:T(8,128)(2,1)}, bf16[64,4096]{1,0:T(8,128)(2,1)S(1)}, u32[]{:S(2)}, u32[]{:S(2)}) collective-permute-start(bf16[64,4096]{1,0:T(8,128)(2,1)} %get-tuple-element.138), channel_id=1, source_target_pairs={{0,6},{2,0},{4,2},{6,4},{1,7},{3,1},{5,3},{7,5},{8,14},{10,8},{12,... | collective-permute-start | bytes 1572872 | tf_op jit(solution)/shard_map/ppermute | solution.py:472
  123.5 10.7 %output.1 = (bf16[64,8192]{1,0:T(8,128)(2,1)}, bf16[64,8192]{1,0:T(8,128)(2,1)}, bf16[64,8192]{1,0:T(8,128)(2,1)}, bf16[64,4096]{1,0:T(8,128)(2,1)}, bf16[64,4096]{1,0:T(8,128)(2,1)}) custom-call(bf16[512,1024]{1,0:T(8,128)(2,1)} %get-tuple-element.144.mixed_ref, bf16[512,8192]{1,0:T(8,128)(2,1)} %refs_0_, ...), custom_call_target="tpu_custom_call" | custom-call | flops 4294967296 | bytes 20971520 | tf_op jit(solution)/shard_map/output/pallas_call | solution.py:287
  134.2 1.0 collective-permute-done.20.refs_1_
  135.5 0.7 collective-permute-start.23
  136.1 2.6 %collective-permute-start.24 = (bf16[64,8192]{1,0:T(8,128)(2,1)S(1)}, bf16[64,8192]{1,0:T(8,128)(2,1)S(1)}, u32[]{:S(2)}, u32[]{:S(2)}) collective-permute-start(bf16[64,8192]{1,0:T(8,128)(2,1)S(1)} %get-tuple-element.157), channel_id=1, source_target_pairs={{0,6},{2,0},{4,2},{6,4},{1,7},{3,1},{5,3},{7,5},{8,14},{10,8},{12,... | collective-permute-start | bytes 3145736 | tf_op jit(solution)/shard_map/ppermute | solution.py:472
  139.0 3.2 %collective-permute-start.32 = (bf16[64,4096]{1,0:T(8,128)(2,1)S(1)}, bf16[64,4096]{1,0:T(8,128)(2,1)S(1)}, u32[]{:S(2)}, u32[]{:S(2)}) collective-permute-start(bf16[64,4096]{1,0:T(8,128)(2,1)S(1)} %copy-done.23), channel_id=1, source_target_pairs={{0,6},{2,0},{4,2},{6,4},{1,7},{3,1},{5,3},{7,5},{8,14},{10,8},{12,... | collective-permute-start | bytes 1572872 | tf_op jit(solution)/shard_map/ppermute | solution.py:472
  142.2 1.5 outer.1
  143.6 0.7 collective-permute-start.25
  144.3 4.4 %collective-permute-done.25 = bf16[512,128]{1,0:T(8,128)(2,1)S(1)} collective-permute-done((bf16[512,128]{1,0:T(8,128)(2,1)S(1)}, bf16[512,128]{1,0:T(8,128)(2,1)S(1)}, u32[]{:S(2)}, u32[]{:S(2)}) %collective-permute-start.25) | collective-permute-done | bytes 131104 | tf_op jit(solution)/shard_map/ppermute | solution.py:467
  148.7 1.6 collective-permute-start.26
  150.3 6.1 %collective-permute-done.26.refs_2_ = bf16[1024,128]{1,0:T(8,128)(2,1)S(1)} collective-permute-done((bf16[1024,128]{1,0:T(8,128)(2,1)S(1)}, bf16[1024,128]{1,0:T(8,128)(2,1)S(1)}, u32[]{:S(2)}, u32[]{:S(2)}) %collective-permute-start.26) | collective-permute-done | bytes 262176 | tf_op jit(solution)/shard_map/ppermute | solution.py:472
  156.4 6.5 %collective-permute-done.23.refs_1_.refs_4_ = bf16[64,8192]{1,0:T(8,128)(2,1)S(1)} collective-permute-done((bf16[64,8192]{1,0:T(8,128)(2,1)S(1)}, bf16[64,8192]{1,0:T(8,128)(2,1)S(1)}, u32[]{:S(2)}, u32[]{:S(2)}) %collective-permute-start.23) | collective-permute-done | bytes 1048608 | tf_op jit(solution)/shard_map/ppermute | solution.py:472
  163.3 0.9 collective-permute-start.28
  164.1 2.6 %collective-permute-start.29 = (bf16[64,4096]{1,0:T(8,128)(2,1)S(1)}, bf16[64,4096]{1,0:T(8,128)(2,1)S(1)}, u32[]{:S(2)}, u32[]{:S(2)}) collective-permute-start(bf16[64,4096]{1,0:T(8,128)(2,1)S(1)} %get-tuple-element.165), channel_id=1, source_target_pairs={{0,24},{16,0},{8,16},{24,8},{1,25},{17,1},{9,17},{25,9},{2,26},{18... | collective-permute-start | bytes 1572872 | tf_op jit(solution)/shard_map/ppermute | solution.py:472
  166.8 5.6 %collective-permute-done.31.refs_1_ = bf16[64,4096]{1,0:T(8,128)(2,1)S(1)} collective-permute-done((bf16[64,4096]{1,0:T(8,128)(2,1)S(1)}, bf16[64,4096]{1,0:T(8,128)(2,1)S(1)}, u32[]{:S(2)}, u32[]{:S(2)}) %collective-permute-start.31) | collective-permute-done | bytes 524320 | tf_op jit(solution)/shard_map/ppermute | solution.py:472
  172.7 0.9 collective-permute-start.33
  173.5 2.4 %collective-permute-start.34 = (bf16[64,8192]{1,0:T(8,128)(2,1)S(1)}, bf16[64,8192]{1,0:T(8,128)(2,1)S(1)}, u32[]{:S(2)}, u32[]{:S(2)}) collective-permute-start(bf16[64,8192]{1,0:T(8,128)(2,1)S(1)} %get-tuple-element.174), channel_id=1, source_target_pairs={{0,6},{2,0},{4,2},{6,4},{1,7},{3,1},{5,3},{7,5},{8,14},{10,8},{12,... | collective-permute-start | bytes 3145736 | tf_op jit(solution)/shard_map/ppermute | solution.py:472
  176.0 3.0 %collective-permute-start.27 = (bf16[1024,128]{1,0:T(8,128)(2,1)S(1)}, bf16[1024,128]{1,0:T(8,128)(2,1)S(1)}, u32[]{:S(2)}, u32[]{:S(2)}) collective-permute-start(bf16[1024,128]{1,0:T(8,128)(2,1)S(1)} %constant_dynamic-update-slice_fusion.refs_0_), channel_id=1, source_target_pairs={{0,96},{32,0},{64,32},{96,64},{1,97},{33,1},{65,33},{97,65},{2,98}... | collective-permute-start | bytes 786440 | tf_op jit(solution)/shard_map/ppermute | solution.py:472
  179.0 0.6 collective-permute-start.35
  179.5 2.7 %collective-permute-start.36 = (bf16[64,4096]{1,0:T(8,128)(2,1)S(1)}, bf16[64,4096]{1,0:T(8,128)(2,1)S(1)}, u32[]{:S(2)}, u32[]{:S(2)}) collective-permute-start(bf16[64,4096]{1,0:T(8,128)(2,1)S(1)} %collective-permute-done.29), channel_id=1, source_target_pairs={{0,24},{16,0},{8,16},{24,8},{1,25},{17,1},{9,17},{25,9},{2,26},{18... | collective-permute-start | bytes 1572872 | tf_op jit(solution)/shard_map/ppermute | solution.py:472
  182.2 0.6 collective-permute-done.27.refs_1_
  182.9 1.0 collective-permute-start.30
  183.9 7.0 %collective-permute-done.30.refs_3_ = bf16[1024,128]{1,0:T(8,128)(2,1)S(1)} collective-permute-done((bf16[1024,128]{1,0:T(8,128)(2,1)S(1)}, bf16[1024,128]{1,0:T(8,128)(2,1)S(1)}, u32[]{:S(2)}, u32[]{:S(2)}) %collective-permute-start.30) | collective-permute-done | bytes 262176 | tf_op jit(solution)/shard_map/ppermute | solution.py:472
  190.9 1.8 apply.1
  192.7 4.7 %collective-permute-done.33.refs_1_ = bf16[64,8192]{1,0:T(8,128)(2,1)S(1)} collective-permute-done((bf16[64,8192]{1,0:T(8,128)(2,1)S(1)}, bf16[64,8192]{1,0:T(8,128)(2,1)S(1)}, u32[]{:S(2)}, u32[]{:S(2)}) %collective-permute-start.33) | collective-permute-done | bytes 1048608 | tf_op jit(solution)/shard_map/ppermute | solution.py:472
  197.4 1.5 finish.1
  (89 shorter events, 2.7 us)
Async XLA Ops:
  0.6 11.4 %copy-start.8 = (bf16[1,512,1024]{2,1,0:T(8,128)(2,1)S(1)}, bf16[1,512,1024]{2,1,0:T(8,128)(2,1)}, u32[]{:S(2)}) copy-start(bf16[1,512,1024]{2,1,0:T(8,128)(2,1)} %param.14) | copy-start | bytes 3145732
  3.8 16.0 %collective-permute-start.2 = (bf16[8192,128]{1,0:T(8,128)(2,1)}, bf16[8192,128]{1,0:T(8,128)(2,1)}, u32[]{:S(2)}, u32[]{:S(2)}) collective-permute-start(bf16[8192,128]{1,0:T(8,128)(2,1)} %refs_6_.2), channel_id=1, source_target_pairs={{0,1},{1,0},{2,3},{3,2},{4,5},{5,4},{6,7},{7,6},{8,9},{9,8},{10,11... | collective-permute-start | bytes 6291464 | tf_op jit(solution)/shard_map/ppermute | solution.py:467
  3.8 16.0 %collective-permute-start = (bf16[32,8192]{1,0:T(8,128)(2,1)}, bf16[32,8192]{1,0:T(8,128)(2,1)}, u32[]{:S(2)}, u32[]{:S(2)}) collective-permute-start(bf16[32,8192]{1,0:T(8,128)(2,1)} %get-tuple-element.91), channel_id=1, source_target_pairs={{0,16},{16,8},{8,24},{24,0},{1,17},{17,9},{9,25},{25,1},{2,18},{18... | collective-permute-start | bytes 1572872 | tf_op jit(solution)/shard_map/ppermute | solution.py:472
  5.4 14.4 %collective-permute-start.1 = (bf16[32,8192]{1,0:T(8,128)(2,1)}, bf16[32,8192]{1,0:T(8,128)(2,1)}, u32[]{:S(2)}, u32[]{:S(2)}) collective-permute-start(bf16[32,8192]{1,0:T(8,128)(2,1)} %get-tuple-element.92), channel_id=1, source_target_pairs={{0,24},{16,0},{8,16},{24,8},{1,25},{17,1},{9,17},{25,9},{2,26},{18... | collective-permute-start | bytes 1572872 | tf_op jit(solution)/shard_map/ppermute | solution.py:472
  7.0 27.6 %collective-permute-start.5 = (bf16[64,8192]{1,0:T(8,128)(2,1)}, bf16[64,8192]{1,0:T(8,128)(2,1)S(1)}, u32[]{:S(2)}, u32[]{:S(2)}) collective-permute-start(bf16[64,8192]{1,0:T(8,128)(2,1)} %get-tuple-element.93.refs_0_), channel_id=1, source_target_pairs={{0,2},{2,4},{4,6},{6,0},{1,3},{3,5},{5,7},{7,1},{8,10},{10,12},{12... | collective-permute-start | bytes 3145736 | tf_op jit(solution)/shard_map/ppermute | solution.py:472
  9.0 25.7 %collective-permute-start.6 = (bf16[64,8192]{1,0:T(8,128)(2,1)}, bf16[64,8192]{1,0:T(8,128)(2,1)}, u32[]{:S(2)}, u32[]{:S(2)}) collective-permute-start(bf16[64,8192]{1,0:T(8,128)(2,1)} %get-tuple-element.93.refs_0_), channel_id=1, source_target_pairs={{0,6},{2,0},{4,2},{6,4},{1,7},{3,1},{5,3},{7,5},{8,14},{10,8},{12,... | collective-permute-start | bytes 3145736 | tf_op jit(solution)/shard_map/ppermute | solution.py:472
  13.2 21.4 %copy-start.12 = (bf16[1024,128]{1,0:T(8,128)(2,1)}, bf16[1024,128]{1,0:T(8,128)(2,1)S(1)}, u32[]{:S(2)}) copy-start(bf16[1024,128]{1,0:T(8,128)(2,1)S(1)} %get-tuple-element.125) | copy-start | bytes 786436
  13.2 21.4 %copy-start.14 = (bf16[1024,128]{1,0:T(8,128)(2,1)}, bf16[1024,128]{1,0:T(8,128)(2,1)S(1)}, u32[]{:S(2)}) copy-start(bf16[1024,128]{1,0:T(8,128)(2,1)S(1)} %get-tuple-element.117) | copy-start | bytes 786436
  13.2 21.4 %copy-start.16 = (bf16[1024,128]{1,0:T(8,128)(2,1)}, bf16[1024,128]{1,0:T(8,128)(2,1)S(1)}, u32[]{:S(2)}) copy-start(bf16[1024,128]{1,0:T(8,128)(2,1)S(1)} %get-tuple-element.116) | copy-start | bytes 786436
  19.8 32.7 %collective-permute-start.11 = (bf16[8192,512]{1,0:T(8,128)(2,1)}, bf16[8192,512]{1,0:T(8,128)(2,1)}, u32[]{:S(2)}, u32[]{:S(2)}) collective-permute-start(bf16[8192,512]{1,0:T(8,128)(2,1)} %refs_4_.1), channel_id=1, source_target_pairs={{0,1},{1,0},{2,3},{3,2},{4,5},{5,4},{6,7},{7,6},{8,9},{9,8},{10,11... | collective-permute-start | bytes 25165832 | tf_op jit(solution)/shard_map/ppermute | solution.py:467
  19.8 19.7 %collective-permute-start.4 = (bf16[32,8192]{1,0:T(8,128)(2,1)}, bf16[32,8192]{1,0:T(8,128)(2,1)S(1)}, u32[]{:S(2)}, u32[]{:S(2)}) collective-permute-start(bf16[32,8192]{1,0:T(8,128)(2,1)} %collective-permute-done.1), channel_id=1, source_target_pairs={{0,24},{16,0},{8,16},{24,8},{1,25},{17,1},{9,17},{25,9},{2,26},{18... | collective-permute-start | bytes 1572872 | tf_op jit(solution)/shard_map/ppermute | solution.py:472
  22.7 16.8 %collective-permute-start.3 = (bf16[32,8192]{1,0:T(8,128)(2,1)}, bf16[32,8192]{1,0:T(8,128)(2,1)S(1)}, u32[]{:S(2)}, u32[]{:S(2)}) collective-permute-start(bf16[32,8192]{1,0:T(8,128)(2,1)} %collective-permute-done), channel_id=1, source_target_pairs={{0,16},{16,8},{8,24},{24,0},{1,17},{17,9},{9,25},{25,1},{2,18},{18... | collective-permute-start | bytes 1572872 | tf_op jit(solution)/shard_map/ppermute | solution.py:472
  34.7 5.9 %copy-start.10 = (bf16[64,8192]{1,0:T(8,128)(2,1)}, bf16[64,8192]{1,0:T(8,128)(2,1)S(1)}, u32[]{:S(2)}) copy-start(bf16[64,8192]{1,0:T(8,128)(2,1)S(1)} %get-tuple-element.106.below_ref.refs_2_) | copy-start | bytes 3145732
  36.2 16.1 %collective-permute-start.9 = (bf16[32,8192]{1,0:T(8,128)(2,1)S(1)}, bf16[32,8192]{1,0:T(8,128)(2,1)S(1)}, u32[]{:S(2)}, u32[]{:S(2)}) collective-permute-start(bf16[32,8192]{1,0:T(8,128)(2,1)S(1)} %get-tuple-element.107), channel_id=1, source_target_pairs={{0,2},{2,4},{4,6},{6,0},{1,3},{3,5},{5,7},{7,1},{8,10},{10,12},{12... | collective-permute-start | bytes 1572872 | tf_op jit(solution)/shard_map/ppermute | solution.py:472
  37.6 14.9 %collective-permute-start.10 = (bf16[32,8192]{1,0:T(8,128)(2,1)S(1)}, bf16[32,8192]{1,0:T(8,128)(2,1)S(1)}, u32[]{:S(2)}, u32[]{:S(2)}) collective-permute-start(bf16[32,8192]{1,0:T(8,128)(2,1)S(1)} %get-tuple-element.108), channel_id=1, source_target_pairs={{0,6},{2,0},{4,2},{6,4},{1,7},{3,1},{5,3},{7,5},{8,14},{10,8},{12,... | collective-permute-start | bytes 1572872 | tf_op jit(solution)/shard_map/ppermute | solution.py:472
  40.6 32.0 %collective-permute-start.7 = (bf16[64,8192]{1,0:T(8,128)(2,1)}, bf16[64,8192]{1,0:T(8,128)(2,1)S(1)}, u32[]{:S(2)}, u32[]{:S(2)}) collective-permute-start(bf16[64,8192]{1,0:T(8,128)(2,1)} %pad_maximum_fusion.refs_5_), channel_id=1, source_target_pairs={{0,6},{2,0},{4,2},{6,4},{1,7},{3,1},{5,3},{7,5},{8,14},{10,8},{12,... | collective-permute-start | bytes 3145736 | tf_op jit(solution)/shard_map/ppermute | solution.py:472
  43.3 29.9 %collective-permute-start.8 = (bf16[64,8192]{1,0:T(8,128)(2,1)}, bf16[64,8192]{1,0:T(8,128)(2,1)S(1)}, u32[]{:S(2)}, u32[]{:S(2)}) collective-permute-start(bf16[64,8192]{1,0:T(8,128)(2,1)} %pad_maximum_fusion.refs_5_), channel_id=1, source_target_pairs={{0,2},{2,4},{4,6},{6,0},{1,3},{3,5},{5,7},{7,1},{8,10},{10,12},{12... | collective-permute-start | bytes 3145736 | tf_op jit(solution)/shard_map/ppermute | solution.py:472
  52.3 0.8 copy-start.25
  52.5 0.8 copy-start.26
  53.3 13.9 %copy-start.17 = (bf16[1024,128]{1,0:T(8,128)(2,1)S(1)}, bf16[1024,128]{1,0:T(8,128)(2,1)}, u32[]{:S(2)}) copy-start(bf16[1024,128]{1,0:T(8,128)(2,1)} %copy-done.16) | copy-start | bytes 786436
  53.3 15.5 %copy-start.15 = (bf16[1024,128]{1,0:T(8,128)(2,1)S(1)}, bf16[1024,128]{1,0:T(8,128)(2,1)}, u32[]{:S(2)}) copy-start(bf16[1024,128]{1,0:T(8,128)(2,1)} %copy-done.14) | copy-start | bytes 786436
  67.2 11.3 %copy-start.13 = (bf16[1024,128]{1,0:T(8,128)(2,1)S(1)}, bf16[1024,128]{1,0:T(8,128)(2,1)}, u32[]{:S(2)}) copy-start(bf16[1024,128]{1,0:T(8,128)(2,1)} %copy-done.12) | copy-start | bytes 786436
  67.2 7.8 %collective-permute-start.12 = (bf16[1024,128]{1,0:T(8,128)(2,1)S(1)}, bf16[1024,128]{1,0:T(8,128)(2,1)}, u32[]{:S(2)}, u32[]{:S(2)}) collective-permute-start(bf16[1024,128]{1,0:T(8,128)(2,1)S(1)} %copy-done.17), channel_id=1, source_target_pairs={{0,32},{32,64},{64,96},{96,0},{1,33},{33,65},{65,97},{97,1},{2,34}... | collective-permute-start | bytes 786440 | tf_op jit(solution)/shard_map/ppermute | solution.py:472
  68.8 6.4 %collective-permute-start.13 = (bf16[1024,128]{1,0:T(8,128)(2,1)S(1)}, bf16[1024,128]{1,0:T(8,128)(2,1)S(1)}, u32[]{:S(2)}, u32[]{:S(2)}) collective-permute-start(bf16[1024,128]{1,0:T(8,128)(2,1)S(1)} %copy-done.15), channel_id=1, source_target_pairs={{0,96},{32,0},{64,32},{96,64},{1,97},{33,1},{65,33},{97,65},{2,98}... | collective-permute-start | bytes 786440 | tf_op jit(solution)/shard_map/ppermute | solution.py:472
  71.2 10.0 %copy-start.20 = (bf16[320,256]{1,0:T(8,128)(2,1)S(1)}, bf16[320,256]{1,0:T(8,128)(2,1)}, u32[]{:S(2)}) copy-start(bf16[320,256]{1,0:T(8,128)(2,1)} %get-tuple-element.127.refs_2_) | copy-start | bytes 491524
  72.6 18.3 %copy-start.1 = (bf16[64,8192]{1,0:T(8,128)(2,1)}, bf16[64,8192]{1,0:T(8,128)(2,1)S(1)}, u32[]{:S(2)}) copy-start(bf16[64,8192]{1,0:T(8,128)(2,1)S(1)} %collective-permute-done.7.above_ref.refs_0_) | copy-start | bytes 3145732
  73.2 17.7 %copy-start.2 = (bf16[64,8192]{1,0:T(8,128)(2,1)}, bf16[64,8192]{1,0:T(8,128)(2,1)S(1)}, u32[]{:S(2)}) copy-start(bf16[64,8192]{1,0:T(8,128)(2,1)S(1)} %collective-permute-done.8.below_ref.refs_1_) | copy-start | bytes 3145732
  75.1 29.7 %collective-permute-start.19 = (bf16[512,8192]{1,0:T(8,128)(2,1)}, bf16[512,8192]{1,0:T(8,128)(2,1)}, u32[]{:S(2)}, u32[]{:S(2)}) collective-permute-start(bf16[512,8192]{1,0:T(8,128)(2,1)} %refs_0_), channel_id=1, source_target_pairs={{0,1},{1,0},{2,3},{3,2},{4,5},{5,4},{6,7},{7,6},{8,9},{9,8},{10,11... | collective-permute-start | bytes 25165832 | tf_op jit(solution)/shard_map/ppermute | solution.py:467
  75.2 15.7 %collective-permute-start.14 = (bf16[32,8192]{1,0:T(8,128)(2,1)S(1)}, bf16[32,8192]{1,0:T(8,128)(2,1)S(1)}, u32[]{:S(2)}, u32[]{:S(2)}) collective-permute-start(bf16[32,8192]{1,0:T(8,128)(2,1)S(1)} %get-tuple-element.123), channel_id=1, source_target_pairs={{0,2},{2,4},{4,6},{6,0},{1,3},{3,5},{5,7},{7,1},{8,10},{10,12},{12... | collective-permute-start | bytes 1572872 | tf_op jit(solution)/shard_map/ppermute | solution.py:472
  76.9 14.1 %collective-permute-start.15 = (bf16[32,8192]{1,0:T(8,128)(2,1)S(1)}, bf16[32,8192]{1,0:T(8,128)(2,1)S(1)}, u32[]{:S(2)}, u32[]{:S(2)}) collective-permute-start(bf16[32,8192]{1,0:T(8,128)(2,1)S(1)} %get-tuple-element.124), channel_id=1, source_target_pairs={{0,6},{2,0},{4,2},{6,4},{1,7},{3,1},{5,3},{7,5},{8,14},{10,8},{12,... | collective-permute-start | bytes 1572872 | tf_op jit(solution)/shard_map/ppermute | solution.py:472
  79.6 9.6 %collective-permute-start.16 = (bf16[1024,128]{1,0:T(8,128)(2,1)S(1)}, bf16[1024,128]{1,0:T(8,128)(2,1)S(1)}, u32[]{:S(2)}, u32[]{:S(2)}) collective-permute-start(bf16[1024,128]{1,0:T(8,128)(2,1)S(1)} %add_convert_fusion), channel_id=1, source_target_pairs={{0,32},{32,64},{64,96},{96,0},{1,33},{33,65},{65,97},{97,1},{2,34}... | collective-permute-start | bytes 786440 | tf_op jit(solution)/shard_map/ppermute | solution.py:472
  81.2 7.4 %collective-permute-start.17 = (bf16[320,256]{1,0:T(8,128)(2,1)S(1)}, bf16[320,256]{1,0:T(8,128)(2,1)S(1)}, u32[]{:S(2)}, u32[]{:S(2)}) collective-permute-start(bf16[320,256]{1,0:T(8,128)(2,1)S(1)} %copy-done.20), channel_id=1, source_target_pairs={{0,1},{1,0},{2,3},{3,2},{4,5},{5,4},{6,7},{7,6},{8,9},{9,8},{10,11... | collective-permute-start | bytes 491528 | tf_op jit(solution)/shard_map/ppermute | solution.py:467
  88.5 14.6 %copy-start.21 = (bf16[320,256]{1,0:T(8,128)(2,1)}, bf16[320,256]{1,0:T(8,128)(2,1)S(1)}, u32[]{:S(2)}) copy-start(bf16[320,256]{1,0:T(8,128)(2,1)S(1)} %collective-permute-done.17.refs_4_) | copy-start | bytes 491524
  90.9 0.8 copy-start.18
  91.7 0.8 copy-start.19
  103.1 1.8 collective-permute-start.18
  104.9 0.6 copy-start.22
  119.7 15.5 %collective-permute-start.20 = (bf16[64,4096]{1,0:T(8,128)(2,1)}, bf16[64,4096]{1,0:T(8,128)(2,1)S(1)}, u32[]{:S(2)}, u32[]{:S(2)}) collective-permute-start(bf16[64,4096]{1,0:T(8,128)(2,1)} %get-tuple-element.137), channel_id=1, source_target_pairs={{0,2},{2,4},{4,6},{6,0},{1,3},{3,5},{5,7},{7,1},{8,10},{10,12},{12... | collective-permute-start | bytes 1572872 | tf_op jit(solution)/shard_map/ppermute | solution.py:472
  120.5 14.7 %collective-permute-start.21 = (bf16[64,4096]{1,0:T(8,128)(2,1)}, bf16[64,4096]{1,0:T(8,128)(2,1)S(1)}, u32[]{:S(2)}, u32[]{:S(2)}) collective-permute-start(bf16[64,4096]{1,0:T(8,128)(2,1)} %get-tuple-element.138), channel_id=1, source_target_pairs={{0,6},{2,0},{4,2},{6,4},{1,7},{3,1},{5,3},{7,5},{8,14},{10,8},{12,... | collective-permute-start | bytes 1572872 | tf_op jit(solution)/shard_map/ppermute | solution.py:472
  123.1 12.1 %copy-start.6 = (bf16[64,8192]{1,0:T(8,128)(2,1)S(1)}, bf16[64,8192]{1,0:T(8,128)(2,1)}, u32[]{:S(2)}) copy-start(bf16[64,8192]{1,0:T(8,128)(2,1)} %get-tuple-element.147.refs_0_) | copy-start | bytes 3145732
  123.1 12.1 %copy-start.7 = (bf16[64,8192]{1,0:T(8,128)(2,1)S(1)}, bf16[64,8192]{1,0:T(8,128)(2,1)}, u32[]{:S(2)}) copy-start(bf16[64,8192]{1,0:T(8,128)(2,1)} %get-tuple-element.149.refs_2_) | copy-start | bytes 3145732
  123.1 12.4 %collective-permute-start.22 = (bf16[512,128]{1,0:T(8,128)(2,1)S(1)}, bf16[512,128]{1,0:T(8,128)(2,1)S(1)}, u32[]{:S(2)}, u32[]{:S(2)}) collective-permute-start(bf16[512,128]{1,0:T(8,128)(2,1)S(1)} %add_convert_fusion.1), channel_id=1, source_target_pairs={{0,16},{16,0},{1,17},{17,1},{2,18},{18,2},{3,19},{19,3},{4,20},{20... | collective-permute-start | bytes 393224 | tf_op jit(solution)/shard_map/ppermute | solution.py:467
  134.2 4.7 %copy-start.24 = (bf16[64,4096]{1,0:T(8,128)(2,1)S(1)}, bf16[64,4096]{1,0:T(8,128)(2,1)}, u32[]{:S(2)}) copy-start(bf16[64,4096]{1,0:T(8,128)(2,1)} %get-tuple-element.170) | copy-start | bytes 1572868
  134.2 4.8 %copy-start.23 = (bf16[64,4096]{1,0:T(8,128)(2,1)S(1)}, bf16[64,4096]{1,0:T(8,128)(2,1)}, u32[]{:S(2)}) copy-start(bf16[64,4096]{1,0:T(8,128)(2,1)} %get-tuple-element.172) | copy-start | bytes 1572868
  134.2 8.0 %copy-start.11 = (f32[512,128]{1,0:T(8,128)S(1)}, f32[512,128]{1,0:T(8,128)}, u32[]{:S(2)}) copy-start(f32[512,128]{1,0:T(8,128)} %refs_4_.2) | copy-start | bytes 786436
  135.2 27.7 %copy-start = (bf16[64,8192]{1,0:T(8,128)(2,1)S(1)}, bf16[64,8192]{1,0:T(8,128)(2,1)}, u32[]{:S(2)}) copy-start(bf16[64,8192]{1,0:T(8,128)(2,1)} %get-tuple-element.161.refs_0_.refs_3_) | copy-start | bytes 3145732
  135.5 27.4 %collective-permute-start.23 = (bf16[64,8192]{1,0:T(8,128)(2,1)S(1)}, bf16[64,8192]{1,0:T(8,128)(2,1)S(1)}, u32[]{:S(2)}, u32[]{:S(2)}) collective-permute-start(bf16[64,8192]{1,0:T(8,128)(2,1)S(1)} %get-tuple-element.156), channel_id=1, source_target_pairs={{0,2},{2,4},{4,6},{6,0},{1,3},{3,5},{5,7},{7,1},{8,10},{10,12},{12... | collective-permute-start | bytes 3145736 | tf_op jit(solution)/shard_map/ppermute | solution.py:472
  136.1 26.7 %collective-permute-start.24 = (bf16[64,8192]{1,0:T(8,128)(2,1)S(1)}, bf16[64,8192]{1,0:T(8,128)(2,1)S(1)}, u32[]{:S(2)}, u32[]{:S(2)}) collective-permute-start(bf16[64,8192]{1,0:T(8,128)(2,1)S(1)} %get-tuple-element.157), channel_id=1, source_target_pairs={{0,6},{2,0},{4,2},{6,4},{1,7},{3,1},{5,3},{7,5},{8,14},{10,8},{12,... | collective-permute-start | bytes 3145736 | tf_op jit(solution)/shard_map/ppermute | solution.py:472
  138.9 33.5 %collective-permute-start.31 = (bf16[64,4096]{1,0:T(8,128)(2,1)S(1)}, bf16[64,4096]{1,0:T(8,128)(2,1)S(1)}, u32[]{:S(2)}, u32[]{:S(2)}) collective-permute-start(bf16[64,4096]{1,0:T(8,128)(2,1)S(1)} %copy-done.24), channel_id=1, source_target_pairs={{0,2},{2,4},{4,6},{6,0},{1,3},{3,5},{5,7},{7,1},{8,10},{10,12},{12... | collective-permute-start | bytes 1572872 | tf_op jit(solution)/shard_map/ppermute | solution.py:472
  139.0 33.4 %collective-permute-start.32 = (bf16[64,4096]{1,0:T(8,128)(2,1)S(1)}, bf16[64,4096]{1,0:T(8,128)(2,1)S(1)}, u32[]{:S(2)}, u32[]{:S(2)}) collective-permute-start(bf16[64,4096]{1,0:T(8,128)(2,1)S(1)} %copy-done.23), channel_id=1, source_target_pairs={{0,6},{2,0},{4,2},{6,4},{1,7},{3,1},{5,3},{7,5},{8,14},{10,8},{12,... | collective-permute-start | bytes 1572872 | tf_op jit(solution)/shard_map/ppermute | solution.py:472
  143.6 5.0 %collective-permute-start.25 = (bf16[512,128]{1,0:T(8,128)(2,1)S(1)}, bf16[512,128]{1,0:T(8,128)(2,1)S(1)}, u32[]{:S(2)}, u32[]{:S(2)}) collective-permute-start(bf16[512,128]{1,0:T(8,128)(2,1)S(1)} %get-tuple-element.159), channel_id=1, source_target_pairs={{0,16},{16,0},{1,17},{17,1},{2,18},{18,2},{3,19},{19,3},{4,20},{20... | collective-permute-start | bytes 393224 | tf_op jit(solution)/shard_map/ppermute | solution.py:467
  148.7 23.7 %copy-start.4 = (bf16[64,8192]{1,0:T(8,128)(2,1)S(1)}, bf16[64,8192]{1,0:T(8,128)(2,1)}, u32[]{:S(2)}) copy-start(bf16[64,8192]{1,0:T(8,128)(2,1)} %get-tuple-element.169.refs_0_) | copy-start | bytes 3145732
  148.7 23.7 %copy-start.5 = (bf16[64,8192]{1,0:T(8,128)(2,1)S(1)}, bf16[64,8192]{1,0:T(8,128)(2,1)}, u32[]{:S(2)}) copy-start(bf16[64,8192]{1,0:T(8,128)(2,1)} %get-tuple-element.171.refs_2_) | copy-start | bytes 3145732
  148.7 7.7 %collective-permute-start.26 = (bf16[1024,128]{1,0:T(8,128)(2,1)S(1)}, bf16[1024,128]{1,0:T(8,128)(2,1)S(1)}, u32[]{:S(2)}, u32[]{:S(2)}) collective-permute-start(bf16[1024,128]{1,0:T(8,128)(2,1)S(1)} %constant_dynamic-update-slice_fusion.refs_0_), channel_id=1, source_target_pairs={{0,32},{32,64},{64,96},{96,0},{1,33},{33,65},{65,97},{97,1},{2,34}... | collective-permute-start | bytes 786440 | tf_op jit(solution)/shard_map/ppermute | solution.py:472
  163.2 27.7 %copy-start.9 = (bf16[512,1024]{1,0:T(8,128)(2,1)S(1)}, bf16[512,1024]{1,0:T(8,128)(2,1)}, u32[]{:S(2)}) copy-start(bf16[512,1024]{1,0:T(8,128)(2,1)} %params_ref.1) | copy-start | bytes 3145732
  163.3 15.7 %collective-permute-start.28 = (bf16[64,4096]{1,0:T(8,128)(2,1)S(1)}, bf16[64,4096]{1,0:T(8,128)(2,1)S(1)}, u32[]{:S(2)}, u32[]{:S(2)}) collective-permute-start(bf16[64,4096]{1,0:T(8,128)(2,1)S(1)} %get-tuple-element.164.refs_4_), channel_id=1, source_target_pairs={{0,16},{16,8},{8,24},{24,0},{1,17},{17,9},{9,25},{25,1},{2,18},{18... | collective-permute-start | bytes 1572872 | tf_op jit(solution)/shard_map/ppermute | solution.py:472
  164.1 14.8 %collective-permute-start.29 = (bf16[64,4096]{1,0:T(8,128)(2,1)S(1)}, bf16[64,4096]{1,0:T(8,128)(2,1)S(1)}, u32[]{:S(2)}, u32[]{:S(2)}) collective-permute-start(bf16[64,4096]{1,0:T(8,128)(2,1)S(1)} %get-tuple-element.165), channel_id=1, source_target_pairs={{0,24},{16,0},{8,16},{24,8},{1,25},{17,1},{9,17},{25,9},{2,26},{18... | collective-permute-start | bytes 1572872 | tf_op jit(solution)/shard_map/ppermute | solution.py:472
  172.7 24.8 %copy-start.3 = (bf16[64,8192]{1,0:T(8,128)(2,1)S(1)}, bf16[64,8192]{1,0:T(8,128)(2,1)}, u32[]{:S(2)}) copy-start(bf16[64,8192]{1,0:T(8,128)(2,1)} %get-tuple-element.168.refs_0_) | copy-start | bytes 3145732
  172.7 24.7 %collective-permute-start.33 = (bf16[64,8192]{1,0:T(8,128)(2,1)S(1)}, bf16[64,8192]{1,0:T(8,128)(2,1)S(1)}, u32[]{:S(2)}, u32[]{:S(2)}) collective-permute-start(bf16[64,8192]{1,0:T(8,128)(2,1)S(1)} %get-tuple-element.173), channel_id=1, source_target_pairs={{0,2},{2,4},{4,6},{6,0},{1,3},{3,5},{5,7},{7,1},{8,10},{10,12},{12... | collective-permute-start | bytes 3145736 | tf_op jit(solution)/shard_map/ppermute | solution.py:472
  173.5 23.9 %collective-permute-start.34 = (bf16[64,8192]{1,0:T(8,128)(2,1)S(1)}, bf16[64,8192]{1,0:T(8,128)(2,1)S(1)}, u32[]{:S(2)}, u32[]{:S(2)}) collective-permute-start(bf16[64,8192]{1,0:T(8,128)(2,1)S(1)} %get-tuple-element.174), channel_id=1, source_target_pairs={{0,6},{2,0},{4,2},{6,4},{1,7},{3,1},{5,3},{7,5},{8,14},{10,8},{12,... | collective-permute-start | bytes 3145736 | tf_op jit(solution)/shard_map/ppermute | solution.py:472
  176.0 6.9 %collective-permute-start.27 = (bf16[1024,128]{1,0:T(8,128)(2,1)S(1)}, bf16[1024,128]{1,0:T(8,128)(2,1)S(1)}, u32[]{:S(2)}, u32[]{:S(2)}) collective-permute-start(bf16[1024,128]{1,0:T(8,128)(2,1)S(1)} %constant_dynamic-update-slice_fusion.refs_0_), channel_id=1, source_target_pairs={{0,96},{32,0},{64,32},{96,64},{1,97},{33,1},{65,33},{97,65},{2,98}... | collective-permute-start | bytes 786440 | tf_op jit(solution)/shard_map/ppermute | solution.py:472
  179.0 18.5 %collective-permute-start.35 = (bf16[64,4096]{1,0:T(8,128)(2,1)S(1)}, bf16[64,4096]{1,0:T(8,128)(2,1)S(1)}, u32[]{:S(2)}, u32[]{:S(2)}) collective-permute-start(bf16[64,4096]{1,0:T(8,128)(2,1)S(1)} %collective-permute-done.28), channel_id=1, source_target_pairs={{0,16},{16,8},{8,24},{24,0},{1,17},{17,9},{9,25},{25,1},{2,18},{18... | collective-permute-start | bytes 1572872 | tf_op jit(solution)/shard_map/ppermute | solution.py:472
  179.5 17.9 %collective-permute-start.36 = (bf16[64,4096]{1,0:T(8,128)(2,1)S(1)}, bf16[64,4096]{1,0:T(8,128)(2,1)S(1)}, u32[]{:S(2)}, u32[]{:S(2)}) collective-permute-start(bf16[64,4096]{1,0:T(8,128)(2,1)S(1)} %collective-permute-done.29), channel_id=1, source_target_pairs={{0,24},{16,0},{8,16},{24,8},{1,25},{17,1},{9,17},{25,9},{2,26},{18... | collective-permute-start | bytes 1572872 | tf_op jit(solution)/shard_map/ppermute | solution.py:472
  182.9 8.0 %collective-permute-start.30 = (bf16[1024,128]{1,0:T(8,128)(2,1)S(1)}, bf16[1024,128]{1,0:T(8,128)(2,1)S(1)}, u32[]{:S(2)}, u32[]{:S(2)}) collective-permute-start(bf16[1024,128]{1,0:T(8,128)(2,1)S(1)} %collective-permute-done.26.refs_2_), channel_id=1, source_target_pairs={{0,32},{32,64},{64,96},{96,0},{1,33},{33,65},{65,97},{97,1},{2,34}... | collective-permute-start | bytes 786440 | tf_op jit(solution)/shard_map/ppermute | solution.py:472

commit v3 on v1

--- a/solution.py
+++ b/solution.py
@@ -321,15 +321,17 @@
 
 
 def pick_body(below_ref, above_ref, first_ref, second_ref):
-    count = first_ref.shape[0]
-    first_ref[...] = below_ref[:count]
-    second_ref[...] = above_ref[count:]
+    first_ref[...] = below_ref[...]
+    second_ref[...] = above_ref[...]
 
 
 def pick(below, above):
     shape = jax.ShapeDtypeStruct((below.shape[0] // HALVES, below.shape[1]), below.dtype)
     return pl.pallas_call(
         pick_body,
+        grid=(1,),
+        in_specs=[pl.BlockSpec(shape.shape, lambda i, at=at: (at, 0)) for at in range(HALVES)],
+        out_specs=[pl.BlockSpec(shape.shape, lambda i: (0, 0))] * HALVES,
         out_shape=[shape, shape],
         compiler_params=params(),
         cost_estimate=cost(1e8, 4 * below.size),
@@ -520,17 +522,19 @@
     query_a, pair_a = project(core, [block, above, below, far1, far2], weights)
     query_a, far1, far2, at2, at3 = wait(query_a, far1, far2, at2, at3)
     x2, x3 = hop(at2, "x", 1), hop(at3, "x", -1)
-    pabove, pbelow, query_a, pair_a, x2, x3, at1, out_weight = wait(
-        pabove, pbelow, query_a, pair_a, x2, x3, at1, out_weight
+    pabove, pbelow, query_a, pair_a, x2, x3, at1, out_weight, places = wait(
+        pabove, pbelow, query_a, pair_a, x2, x3, at1, out_weight, places
     )
     pfar1, pfar2 = pick(pbelow, pabove)
     pfar1, pfar2 = hop(pfar1, "z", 1), hop(pfar2, "z", -1)
     out_theirs = swap(out_weight, "core")
     query_m, pair_m = project(core, [partner, pabove, pbelow], weights)
+    query_m, pair_m, x2, at1 = wait(query_m, pair_m, x2, at1)
     passed = hop(add(at1, x2), "x", 1)
     other_a, other_m = swap(pair_a, "core"), swap(pair_m, "core")
-    pfar1, pfar2, passed, query_m = wait(pfar1, pfar2, passed, query_m)
+    pfar1, pfar2, query_m = wait(pfar1, pfar2, query_m)
     query_l, pair_l = project(core, [pfar1, pfar2], weights)
+    query_l, pair_l, passed = wait(query_l, pair_l, passed)
     other_l = swap(pair_l, "core")
     out_weights = (out_weight, out_theirs)
     mixed, q0, qup, qdown, far_a, far_b = attend(

time: 198 us -> 201 us (1.015)
  transfers between devices with their start and end apart: 38 -> 38, of which waited for: 16 -> 16; matrix products, arithmetic and copies ran while one was open for 1% -> 1% of each run, Pallas kernels for 26% -> 25%
where the time goes in v3:
time: 201 us
  waiting for transfers between devices  72.4 us (36%)
  Pallas kernels  69.9 us (35%)
  starting transfers between devices  52.5 us (26%)
  local copies, waits for them, and re-layouts  3.33 us (2%)
    ppermute x30, waiting for transfers between devices, hop(): lax.ppermute(block, axis, [(at[i], at[(i + way) % 4]) for i in range(4)])  66.9 us
    ppermute x30, starting transfers between devices, hop(): lax.ppermute(block, axis, [(at[i], at[(i + way) % 4]) for i in range(4)])  50.2 us
    pallas_call x3, Pallas kernels, project(): pl.pallas_call(project_body, in_specs=[pl.BlockSpec(memory_space=pltpu.SM...  32.4 us
    pallas_call x1, Pallas kernels, attend(): pl.pallas_call(functools.partial(attend_body, order), in_specs=[pl.BlockS...  14.3 us
    pallas_call x1, Pallas kernels, output(): pl.pallas_call(output_body, in_specs=[vmem] + [pl.BlockSpec(memory_space=...  10.7 us
    ppermute x8, waiting for transfers between devices, swap(): return lax.ppermute(block, axis, [(0, 1), (1, 0)])  5.56 us
  transfers between devices with their start and end apart: 38, of which 16 were waited for; matrix products, arithmetic and copies ran while one was open for 1% of the time, Pallas kernels for 25%

profile of v3, /device:TPU:0, one launch (start us, length us, event | category | flops | bytes accessed | tf_op | source)
XLA Modules:
  0.0 200.5 jit_solution(10909423945038599794)
XLA Ops:
  0.6 3.1 %normalize.1 = (bf16[64,8192]{1,0:T(8,128)(2,1)}, bf16[32,8192]{1,0:T(8,128)(2,1)}, bf16[32,8192]{1,0:T(8,128)(2,1)}) custom-call(bf16[64,8192]{1,0:T(8,128)(2,1)} %rows_ref.1, f32[1,8192]{1,0:T(1,128)} %bitcast.22), custom_call_target="tpu_custom_call" | custom-call | flops 2097152 | bytes 3145728 | tf_op jit(solution)/shard_map/normalize/pallas_call | solution.py:54
  3.8 1.7 collective-permute-start
  5.4 1.6 collective-permute-start.1
  7.0 2.0 collective-permute-start.5
  9.0 2.1 %collective-permute-start.6 = (bf16[64,8192]{1,0:T(8,128)(2,1)}, bf16[64,8192]{1,0:T(8,128)(2,1)}, u32[]{:S(2)}, u32[]{:S(2)}) collective-permute-start(bf16[64,8192]{1,0:T(8,128)(2,1)} %get-tuple-element.101.refs_0_), channel_id=1, source_target_pairs={{0,6},{2,0},{4,2},{6,4},{1,7},{3,1},{5,3},{7,5},{8,14},{10,8},{12,... | collective-permute-start | bytes 3145736 | tf_op jit(solution)/shard_map/ppermute | solution.py:472
  11.1 0.8 copy.14
  12.1 1.2 terms.1
  13.3 6.4 %collective-permute-done = bf16[32,8192]{1,0:T(8,128)(2,1)S(1)} collective-permute-done((bf16[32,8192]{1,0:T(8,128)(2,1)}, bf16[32,8192]{1,0:T(8,128)(2,1)S(1)}, u32[]{:S(2)}, u32[]{:S(2)}) %collective-permute-start) | collective-permute-done | bytes 524320 | tf_op jit(solution)/shard_map/ppermute | solution.py:472
  19.7 0.1 collective-permute-done.1
  19.8 1.6 collective-permute-start.3
  21.4 1.7 collective-permute-start.4
  23.0 11.6 %collective-permute-done.5.refs_0_ = bf16[64,8192]{1,0:T(8,128)(2,1)S(1)} collective-permute-done((bf16[64,8192]{1,0:T(8,128)(2,1)}, bf16[64,8192]{1,0:T(8,128)(2,1)S(1)}, u32[]{:S(2)}, u32[]{:S(2)}) %collective-permute-start.5) | collective-permute-done | bytes 1048608 | tf_op jit(solution)/shard_map/ppermute | solution.py:472
  34.7 2.5 %pick.2 = (bf16[32,8192]{1,0:T(8,128)(2,1)}, bf16[32,8192]{1,0:T(8,128)(2,1)}) custom-call(bf16[64,8192]{1,0:T(8,128)(2,1)S(1)} %get-tuple-element.114.below_ref.refs_2_, bf16[64,8192]{1,0:T(8,128)(2,1)} %get-tuple-element.113.above_ref.refs_1_), custom_call_target="tpu_custom_call" | custom-call | flops 100000000 | bytes 2097152 | tf_op jit(solution)/shard_map/pick/pallas_call | solution.py:330
  37.2 3.1 %collective-permute-start.10 = (bf16[32,8192]{1,0:T(8,128)(2,1)}, bf16[32,8192]{1,0:T(8,128)(2,1)}, u32[]{:S(2)}, u32[]{:S(2)}) collective-permute-start(bf16[32,8192]{1,0:T(8,128)(2,1)} %get-tuple-element.116), channel_id=1, source_target_pairs={{0,6},{2,0},{4,2},{6,4},{1,7},{3,1},{5,3},{7,5},{8,14},{10,8},{12,... | collective-permute-start | bytes 1572872 | tf_op jit(solution)/shard_map/ppermute | solution.py:472
  40.2 1.1 pad_maximum_fusion.refs_0_
  41.3 3.2 %collective-permute-start.7 = (bf16[64,8192]{1,0:T(8,128)(2,1)}, bf16[64,8192]{1,0:T(8,128)(2,1)S(1)}, u32[]{:S(2)}, u32[]{:S(2)}) collective-permute-start(bf16[64,8192]{1,0:T(8,128)(2,1)} %pad_maximum_fusion.refs_0_), channel_id=1, source_target_pairs={{0,6},{2,0},{4,2},{6,4},{1,7},{3,1},{5,3},{7,5},{8,14},{10,8},{12,... | collective-permute-start | bytes 3145736 | tf_op jit(solution)/shard_map/ppermute | solution.py:472
  44.5 8.4 %collective-permute-done.10.refs_4_ = bf16[32,8192]{1,0:T(8,128)(2,1)} collective-permute-done((bf16[32,8192]{1,0:T(8,128)(2,1)}, bf16[32,8192]{1,0:T(8,128)(2,1)}, u32[]{:S(2)}, u32[]{:S(2)}) %collective-permute-start.10) | collective-permute-done | bytes 524320 | tf_op jit(solution)/shard_map/ppermute | solution.py:472
  52.9 3.7 %collective-permute-done.9.refs_3_ = bf16[32,8192]{1,0:T(8,128)(2,1)} collective-permute-done((bf16[32,8192]{1,0:T(8,128)(2,1)}, bf16[32,8192]{1,0:T(8,128)(2,1)}, u32[]{:S(2)}, u32[]{:S(2)}) %collective-permute-start.9) | collective-permute-done | bytes 524320 | tf_op jit(solution)/shard_map/ppermute | solution.py:472
  56.6 12.1 %project.3 = (bf16[256,1024]{1,0:T(8,128)(2,1)}, bf16[256,256]{1,0:T(8,128)(2,1)}) custom-call(s32[1]{0:T(128)} %bitcast.core_ref, bf16[64,8192]{1,0:T(8,128)(2,1)} %get-tuple-element.101.refs_0_, bf16[64,8192]{1,0:T(8,128)(2,1)} %get-tuple-element.113.above_ref.refs_1_, bf16[64,8192]{1,0:T(8,128)(2,1)} %copy-done.10, ...), custom_call_target="tpu_custom_call" | custom-call | flops 8053063680 | bytes 25165824 | tf_op jit(solution)/shard_map/project/pallas_call | solution.py:114
  68.7 1.6 collective-permute-start.12
  70.3 1.7 collective-permute-start.13
  72.0 0.7 concatenate.10.place_ref
  72.7 0.8 collective-permute-done.7.above_ref.refs_1_
  73.5 3.3 %collective-permute-done.8.below_ref.refs_2_ = bf16[64,8192]{1,0:T(8,128)(2,1)S(1)} collective-permute-done((bf16[64,8192]{1,0:T(8,128)(2,1)}, bf16[64,8192]{1,0:T(8,128)(2,1)S(1)}, u32[]{:S(2)}, u32[]{:S(2)}) %collective-permute-start.8) | collective-permute-done | bytes 1048608 | tf_op jit(solution)/shard_map/ppermute | solution.py:472
  77.1 3.2 %collective-permute-start.15 = (bf16[32,8192]{1,0:T(8,128)(2,1)S(1)}, bf16[32,8192]{1,0:T(8,128)(2,1)S(1)}, u32[]{:S(2)}, u32[]{:S(2)}) collective-permute-start(bf16[32,8192]{1,0:T(8,128)(2,1)S(1)} %get-tuple-element.132), channel_id=1, source_target_pairs={{0,6},{2,0},{4,2},{6,4},{1,7},{3,1},{5,3},{7,5},{8,14},{10,8},{12,... | collective-permute-start | bytes 1572872 | tf_op jit(solution)/shard_map/ppermute | solution.py:472
  80.3 10.6 %project.4 = (bf16[192,1024]{1,0:T(8,128)(2,1)}, bf16[192,256]{1,0:T(8,128)(2,1)}) custom-call(s32[1]{0:T(128)} %bitcast.core_ref, bf16[64,8192]{1,0:T(8,128)(2,1)} %pad_maximum_fusion.refs_0_, bf16[64,8192]{1,0:T(8,128)(2,1)} %copy-done.1, bf16[64,8192]{1,0:T(8,128)(2,1)} %copy-done.2, bf16[8192,512]{1,0:T(8,128)(2,1)} %refs_2_, ...), custom_call_target="tpu_custom_call" | custom-call | flops 6039797760 | bytes 24117248 | tf_op jit(solution)/shard_map/project/pallas_call | solution.py:114
  91.0 1.6 collective-permute-start.16
  92.6 0.6 collective-permute-start.17
  93.2 0.2 copy-done.18
  93.4 0.8 copy-done.19
  94.2 9.7 %project.5 = (bf16[64,1024]{1,0:T(8,128)(2,1)}, bf16[64,256]{1,0:T(8,128)(2,1)}) custom-call(s32[1]{0:T(128)} %bitcast.core_ref, bf16[32,8192]{1,0:T(8,128)(2,1)} %copy-done.18, bf16[32,8192]{1,0:T(8,128)(2,1)} %copy-done.19, bf16[8192,512]{1,0:T(8,128)(2,1)} %refs_2_, bf16[8192,512]{1,0:T(8,128)(2,1)} %collective-permute-done.11.refs_6_.refs_4_.refs_3_, ...), custom_call_target="tpu_custom_call" | custom-call | flops 2013265920 | bytes 22020096 | tf_op jit(solution)/shard_map/project/pallas_call | solution.py:114
  103.9 0.8 collective-permute-start.19
  104.7 1.0 collective-permute-done.19.refs_8_
  105.7 0.6 copy-done.23
  106.3 14.3 %attend.1 = (bf16[512,1024]{1,0:T(8,128)(2,1)}, bf16[64,8192]{1,0:T(8,128)(2,1)}, bf16[64,8192]{1,0:T(8,128)(2,1)}, bf16[64,8192]{1,0:T(8,128)(2,1)}, bf16[64,40...) custom-call(s32[1]{0:T(128)} %bitcast.core_ref, s32[16]{0:T(128)} %concatenate.10.place_ref, ...), custom_call_target="tpu_custom_call" | custom-call | flops 2147483648 | bytes 18874368 | tf_op jit(solution)/shard_map/attend/pallas_call | solution.py:250
  120.7 3.2 %collective-permute-start.22 = (bf16[64,4096]{1,0:T(8,128)(2,1)}, bf16[64,4096]{1,0:T(8,128)(2,1)S(1)}, u32[]{:S(2)}, u32[]{:S(2)}) collective-permute-start(bf16[64,4096]{1,0:T(8,128)(2,1)} %get-tuple-element.154), channel_id=1, source_target_pairs={{0,6},{2,0},{4,2},{6,4},{1,7},{3,1},{5,3},{7,5},{8,14},{10,8},{12,... | collective-permute-start | bytes 1572872 | tf_op jit(solution)/shard_map/ppermute | solution.py:472
  124.0 0.3 collective-permute-start.23
  124.3 10.7 %output.1 = (bf16[64,8192]{1,0:T(8,128)(2,1)}, bf16[64,8192]{1,0:T(8,128)(2,1)}, bf16[64,8192]{1,0:T(8,128)(2,1)}, bf16[64,4096]{1,0:T(8,128)(2,1)}, bf16[64,4096]{1,0:T(8,128)(2,1)}) custom-call(bf16[512,1024]{1,0:T(8,128)(2,1)} %get-tuple-element.160.mixed_ref, bf16[512,8192]{1,0:T(8,128)(2,1)} %refs_0_, ...), custom_call_target="tpu_custom_call" | custom-call | flops 4294967296 | bytes 20971520 | tf_op jit(solution)/shard_map/output/pallas_call | solution.py:287
  135.1 1.2 collective-permute-done.21.refs_1_
  136.3 0.3 sums.3
  136.7 3.2 %collective-permute-start.25 = (bf16[64,8192]{1,0:T(8,128)(2,1)S(1)}, bf16[64,8192]{1,0:T(8,128)(2,1)S(1)}, u32[]{:S(2)}, u32[]{:S(2)}) collective-permute-start(bf16[64,8192]{1,0:T(8,128)(2,1)S(1)} %get-tuple-element.173), channel_id=1, source_target_pairs={{0,6},{2,0},{4,2},{6,4},{1,7},{3,1},{5,3},{7,5},{8,14},{10,8},{12,... | collective-permute-start | bytes 3145736 | tf_op jit(solution)/shard_map/ppermute | solution.py:472
  140.1 3.2 %collective-permute-start.33 = (bf16[64,4096]{1,0:T(8,128)(2,1)S(1)}, bf16[64,4096]{1,0:T(8,128)(2,1)S(1)}, u32[]{:S(2)}, u32[]{:S(2)}) collective-permute-start(bf16[64,4096]{1,0:T(8,128)(2,1)S(1)} %copy-done.24), channel_id=1, source_target_pairs={{0,6},{2,0},{4,2},{6,4},{1,7},{3,1},{5,3},{7,5},{8,14},{10,8},{12,... | collective-permute-start | bytes 1572872 | tf_op jit(solution)/shard_map/ppermute | solution.py:472
  143.3 1.5 outer.1
  144.8 0.5 collective-permute-start.26
  145.3 4.5 %collective-permute-done.26 = bf16[512,128]{1,0:T(8,128)(2,1)S(1)} collective-permute-done((bf16[512,128]{1,0:T(8,128)(2,1)S(1)}, bf16[512,128]{1,0:T(8,128)(2,1)S(1)}, u32[]{:S(2)}, u32[]{:S(2)}) %collective-permute-start.26) | collective-permute-done | bytes 131104 | tf_op jit(solution)/shard_map/ppermute | solution.py:467
  149.9 1.6 collective-permute-start.27
  151.4 6.1 %collective-permute-done.27.refs_2_ = bf16[1024,128]{1,0:T(8,128)(2,1)S(1)} collective-permute-done((bf16[1024,128]{1,0:T(8,128)(2,1)S(1)}, bf16[1024,128]{1,0:T(8,128)(2,1)S(1)}, u32[]{:S(2)}, u32[]{:S(2)}) %collective-permute-start.27) | collective-permute-done | bytes 262176 | tf_op jit(solution)/shard_map/ppermute | solution.py:472
  157.5 6.5 %collective-permute-done.24.refs_1_.refs_4_ = bf16[64,8192]{1,0:T(8,128)(2,1)S(1)} collective-permute-done((bf16[64,8192]{1,0:T(8,128)(2,1)S(1)}, bf16[64,8192]{1,0:T(8,128)(2,1)S(1)}, u32[]{:S(2)}, u32[]{:S(2)}) %collective-permute-start.24) | collective-permute-done | bytes 1048608 | tf_op jit(solution)/shard_map/ppermute | solution.py:472
  164.0 0.4 sums.4
  164.4 0.8 collective-permute-start.29
  165.1 2.8 %collective-permute-start.30 = (bf16[64,4096]{1,0:T(8,128)(2,1)S(1)}, bf16[64,4096]{1,0:T(8,128)(2,1)S(1)}, u32[]{:S(2)}, u32[]{:S(2)}) collective-permute-start(bf16[64,4096]{1,0:T(8,128)(2,1)S(1)} %get-tuple-element.181), channel_id=1, source_target_pairs={{0,24},{16,0},{8,16},{24,8},{1,25},{17,1},{9,17},{25,9},{2,26},{18... | collective-permute-start | bytes 1572872 | tf_op jit(solution)/shard_map/ppermute | solution.py:472
  167.9 5.8 %collective-permute-done.32.refs_1_ = bf16[64,4096]{1,0:T(8,128)(2,1)S(1)} collective-permute-done((bf16[64,4096]{1,0:T(8,128)(2,1)S(1)}, bf16[64,4096]{1,0:T(8,128)(2,1)S(1)}, u32[]{:S(2)}, u32[]{:S(2)}) %collective-permute-start.32) | collective-permute-done | bytes 524320 | tf_op jit(solution)/shard_map/ppermute | solution.py:472
  173.8 0.3 sums.5
  174.1 0.9 collective-permute-start.34
  174.9 2.4 %collective-permute-start.35 = (bf16[64,8192]{1,0:T(8,128)(2,1)S(1)}, bf16[64,8192]{1,0:T(8,128)(2,1)S(1)}, u32[]{:S(2)}, u32[]{:S(2)}) collective-permute-start(bf16[64,8192]{1,0:T(8,128)(2,1)S(1)} %get-tuple-element.190), channel_id=1, source_target_pairs={{0,6},{2,0},{4,2},{6,4},{1,7},{3,1},{5,3},{7,5},{8,14},{10,8},{12,... | collective-permute-start | bytes 3145736 | tf_op jit(solution)/shard_map/ppermute | solution.py:472
  177.4 2.2 %collective-permute-start.28 = (bf16[1024,128]{1,0:T(8,128)(2,1)S(1)}, bf16[1024,128]{1,0:T(8,128)(2,1)S(1)}, u32[]{:S(2)}, u32[]{:S(2)}) collective-permute-start(bf16[1024,128]{1,0:T(8,128)(2,1)S(1)} %constant_dynamic-update-slice_fusion.refs_0_), channel_id=1, source_target_pairs={{0,96},{32,0},{64,32},{96,64},{1,97},{33,1},{65,33},{97,65},{2,98}... | collective-permute-start | bytes 786440 | tf_op jit(solution)/shard_map/ppermute | solution.py:472
  179.5 0.6 collective-permute-start.36
  180.2 2.6 %collective-permute-start.37 = (bf16[64,4096]{1,0:T(8,128)(2,1)S(1)}, bf16[64,4096]{1,0:T(8,128)(2,1)S(1)}, u32[]{:S(2)}, u32[]{:S(2)}) collective-permute-start(bf16[64,4096]{1,0:T(8,128)(2,1)S(1)} %collective-permute-done.30), channel_id=1, source_target_pairs={{0,24},{16,0},{8,16},{24,8},{1,25},{17,1},{9,17},{25,9},{2,26},{18... | collective-permute-start | bytes 1572872 | tf_op jit(solution)/shard_map/ppermute | solution.py:472
  182.8 1.0 collective-permute-done.28.refs_1_
  183.7 1.5 collective-permute-start.31
  185.2 6.3 %collective-permute-done.31.refs_3_ = bf16[1024,128]{1,0:T(8,128)(2,1)S(1)} collective-permute-done((bf16[1024,128]{1,0:T(8,128)(2,1)S(1)}, bf16[1024,128]{1,0:T(8,128)(2,1)S(1)}, u32[]{:S(2)}, u32[]{:S(2)}) %collective-permute-start.31) | collective-permute-done | bytes 262176 | tf_op jit(solution)/shard_map/ppermute | solution.py:472
  191.5 1.8 apply.1
  193.3 5.7 %collective-permute-done.34.refs_1_ = bf16[64,8192]{1,0:T(8,128)(2,1)S(1)} collective-permute-done((bf16[64,8192]{1,0:T(8,128)(2,1)S(1)}, bf16[64,8192]{1,0:T(8,128)(2,1)S(1)}, u32[]{:S(2)}, u32[]{:S(2)}) %collective-permute-start.34) | collective-permute-done | bytes 1048608 | tf_op jit(solution)/shard_map/ppermute | solution.py:472
  199.1 1.5 finish.1
  (90 shorter events, 1.0 us)
Async XLA Ops:
  0.6 11.4 %copy-start.8 = (bf16[1,512,1024]{2,1,0:T(8,128)(2,1)S(1)}, bf16[1,512,1024]{2,1,0:T(8,128)(2,1)}, u32[]{:S(2)}) copy-start(bf16[1,512,1024]{2,1,0:T(8,128)(2,1)} %param.14) | copy-start | bytes 3145732
  3.8 16.0 %collective-permute-start.2 = (bf16[8192,128]{1,0:T(8,128)(2,1)}, bf16[8192,128]{1,0:T(8,128)(2,1)}, u32[]{:S(2)}, u32[]{:S(2)}) collective-permute-start(bf16[8192,128]{1,0:T(8,128)(2,1)} %refs_4_.2), channel_id=1, source_target_pairs={{0,1},{1,0},{2,3},{3,2},{4,5},{5,4},{6,7},{7,6},{8,9},{9,8},{10,11... | collective-permute-start | bytes 6291464 | tf_op jit(solution)/shard_map/ppermute | solution.py:467
  3.8 15.9 %collective-permute-start = (bf16[32,8192]{1,0:T(8,128)(2,1)}, bf16[32,8192]{1,0:T(8,128)(2,1)S(1)}, u32[]{:S(2)}, u32[]{:S(2)}) collective-permute-start(bf16[32,8192]{1,0:T(8,128)(2,1)} %get-tuple-element.99), channel_id=1, source_target_pairs={{0,16},{16,8},{8,24},{24,0},{1,17},{17,9},{9,25},{25,1},{2,18},{18... | collective-permute-start | bytes 1572872 | tf_op jit(solution)/shard_map/ppermute | solution.py:472
  5.4 14.4 %collective-permute-start.1 = (bf16[32,8192]{1,0:T(8,128)(2,1)}, bf16[32,8192]{1,0:T(8,128)(2,1)}, u32[]{:S(2)}, u32[]{:S(2)}) collective-permute-start(bf16[32,8192]{1,0:T(8,128)(2,1)} %get-tuple-element.100), channel_id=1, source_target_pairs={{0,24},{16,0},{8,16},{24,8},{1,25},{17,1},{9,17},{25,9},{2,26},{18... | collective-permute-start | bytes 1572872 | tf_op jit(solution)/shard_map/ppermute | solution.py:472
  7.0 27.6 %collective-permute-start.5 = (bf16[64,8192]{1,0:T(8,128)(2,1)}, bf16[64,8192]{1,0:T(8,128)(2,1)S(1)}, u32[]{:S(2)}, u32[]{:S(2)}) collective-permute-start(bf16[64,8192]{1,0:T(8,128)(2,1)} %get-tuple-element.101.refs_0_), channel_id=1, source_target_pairs={{0,2},{2,4},{4,6},{6,0},{1,3},{3,5},{5,7},{7,1},{8,10},{10,12},{12... | collective-permute-start | bytes 3145736 | tf_op jit(solution)/shard_map/ppermute | solution.py:472
  9.0 25.7 %collective-permute-start.6 = (bf16[64,8192]{1,0:T(8,128)(2,1)}, bf16[64,8192]{1,0:T(8,128)(2,1)}, u32[]{:S(2)}, u32[]{:S(2)}) collective-permute-start(bf16[64,8192]{1,0:T(8,128)(2,1)} %get-tuple-element.101.refs_0_), channel_id=1, source_target_pairs={{0,6},{2,0},{4,2},{6,4},{1,7},{3,1},{5,3},{7,5},{8,14},{10,8},{12,... | collective-permute-start | bytes 3145736 | tf_op jit(solution)/shard_map/ppermute | solution.py:472
  13.2 21.4 %copy-start.12 = (bf16[1024,128]{1,0:T(8,128)(2,1)}, bf16[1024,128]{1,0:T(8,128)(2,1)S(1)}, u32[]{:S(2)}) copy-start(bf16[1024,128]{1,0:T(8,128)(2,1)S(1)} %get-tuple-element.143) | copy-start | bytes 786436
  13.2 21.4 %copy-start.14 = (bf16[1024,128]{1,0:T(8,128)(2,1)}, bf16[1024,128]{1,0:T(8,128)(2,1)S(1)}, u32[]{:S(2)}) copy-start(bf16[1024,128]{1,0:T(8,128)(2,1)S(1)} %get-tuple-element.125) | copy-start | bytes 786436
  13.2 21.4 %copy-start.16 = (bf16[1024,128]{1,0:T(8,128)(2,1)}, bf16[1024,128]{1,0:T(8,128)(2,1)S(1)}, u32[]{:S(2)}) copy-start(bf16[1024,128]{1,0:T(8,128)(2,1)S(1)} %get-tuple-element.124) | copy-start | bytes 786436
  19.8 36.8 %collective-permute-start.11 = (bf16[8192,512]{1,0:T(8,128)(2,1)}, bf16[8192,512]{1,0:T(8,128)(2,1)}, u32[]{:S(2)}, u32[]{:S(2)}) collective-permute-start(bf16[8192,512]{1,0:T(8,128)(2,1)} %refs_2_), channel_id=1, source_target_pairs={{0,1},{1,0},{2,3},{3,2},{4,5},{5,4},{6,7},{7,6},{8,9},{9,8},{10,11... | collective-permute-start | bytes 25165832 | tf_op jit(solution)/shard_map/ppermute | solution.py:467
  19.8 20.4 %collective-permute-start.3 = (bf16[32,8192]{1,0:T(8,128)(2,1)S(1)}, bf16[32,8192]{1,0:T(8,128)(2,1)S(1)}, u32[]{:S(2)}, u32[]{:S(2)}) collective-permute-start(bf16[32,8192]{1,0:T(8,128)(2,1)S(1)} %collective-permute-done), channel_id=1, source_target_pairs={{0,16},{16,8},{8,24},{24,0},{1,17},{17,9},{9,25},{25,1},{2,18},{18... | collective-permute-start | bytes 1572872 | tf_op jit(solution)/shard_map/ppermute | solution.py:472
  21.4 18.8 %collective-permute-start.4 = (bf16[32,8192]{1,0:T(8,128)(2,1)}, bf16[32,8192]{1,0:T(8,128)(2,1)S(1)}, u32[]{:S(2)}, u32[]{:S(2)}) collective-permute-start(bf16[32,8192]{1,0:T(8,128)(2,1)} %collective-permute-done.1), channel_id=1, source_target_pairs={{0,24},{16,0},{8,16},{24,8},{1,25},{17,1},{9,17},{25,9},{2,26},{18... | collective-permute-start | bytes 1572872 | tf_op jit(solution)/shard_map/ppermute | solution.py:472
  34.7 6.6 %copy-start.10 = (bf16[64,8192]{1,0:T(8,128)(2,1)}, bf16[64,8192]{1,0:T(8,128)(2,1)S(1)}, u32[]{:S(2)}) copy-start(bf16[64,8192]{1,0:T(8,128)(2,1)S(1)} %get-tuple-element.114.below_ref.refs_2_) | copy-start | bytes 3145732
  37.2 15.7 %collective-permute-start.10 = (bf16[32,8192]{1,0:T(8,128)(2,1)}, bf16[32,8192]{1,0:T(8,128)(2,1)}, u32[]{:S(2)}, u32[]{:S(2)}) collective-permute-start(bf16[32,8192]{1,0:T(8,128)(2,1)} %get-tuple-element.116), channel_id=1, source_target_pairs={{0,6},{2,0},{4,2},{6,4},{1,7},{3,1},{5,3},{7,5},{8,14},{10,8},{12,... | collective-permute-start | bytes 1572872 | tf_op jit(solution)/shard_map/ppermute | solution.py:472
  40.2 16.4 %collective-permute-start.9 = (bf16[32,8192]{1,0:T(8,128)(2,1)}, bf16[32,8192]{1,0:T(8,128)(2,1)}, u32[]{:S(2)}, u32[]{:S(2)}) collective-permute-start(bf16[32,8192]{1,0:T(8,128)(2,1)} %get-tuple-element.115), channel_id=1, source_target_pairs={{0,2},{2,4},{4,6},{6,0},{1,3},{3,5},{5,7},{7,1},{8,10},{10,12},{12... | collective-permute-start | bytes 1572872 | tf_op jit(solution)/shard_map/ppermute | solution.py:472
  41.3 32.2 %collective-permute-start.7 = (bf16[64,8192]{1,0:T(8,128)(2,1)}, bf16[64,8192]{1,0:T(8,128)(2,1)S(1)}, u32[]{:S(2)}, u32[]{:S(2)}) collective-permute-start(bf16[64,8192]{1,0:T(8,128)(2,1)} %pad_maximum_fusion.refs_0_), channel_id=1, source_target_pairs={{0,6},{2,0},{4,2},{6,4},{1,7},{3,1},{5,3},{7,5},{8,14},{10,8},{12,... | collective-permute-start | bytes 3145736 | tf_op jit(solution)/shard_map/ppermute | solution.py:472
  44.5 32.3 %collective-permute-start.8 = (bf16[64,8192]{1,0:T(8,128)(2,1)}, bf16[64,8192]{1,0:T(8,128)(2,1)S(1)}, u32[]{:S(2)}, u32[]{:S(2)}) collective-permute-start(bf16[64,8192]{1,0:T(8,128)(2,1)} %pad_maximum_fusion.refs_0_), channel_id=1, source_target_pairs={{0,2},{2,4},{4,6},{6,0},{1,3},{3,5},{5,7},{7,1},{8,10},{10,12},{12... | collective-permute-start | bytes 3145736 | tf_op jit(solution)/shard_map/ppermute | solution.py:472
  56.6 12.1 %copy-start.17 = (bf16[1024,128]{1,0:T(8,128)(2,1)S(1)}, bf16[1024,128]{1,0:T(8,128)(2,1)}, u32[]{:S(2)}) copy-start(bf16[1024,128]{1,0:T(8,128)(2,1)} %copy-done.16) | copy-start | bytes 786436
  56.6 13.7 %copy-start.15 = (bf16[1024,128]{1,0:T(8,128)(2,1)S(1)}, bf16[1024,128]{1,0:T(8,128)(2,1)}, u32[]{:S(2)}) copy-start(bf16[1024,128]{1,0:T(8,128)(2,1)} %copy-done.14) | copy-start | bytes 786436
  68.7 8.1 %collective-permute-start.12 = (bf16[1024,128]{1,0:T(8,128)(2,1)S(1)}, bf16[1024,128]{1,0:T(8,128)(2,1)S(1)}, u32[]{:S(2)}, u32[]{:S(2)}) collective-permute-start(bf16[1024,128]{1,0:T(8,128)(2,1)S(1)} %copy-done.17), channel_id=1, source_target_pairs={{0,32},{32,64},{64,96},{96,0},{1,33},{33,65},{65,97},{97,1},{2,34}... | collective-permute-start | bytes 786440 | tf_op jit(solution)/shard_map/ppermute | solution.py:472
  70.3 6.6 %collective-permute-start.13 = (bf16[1024,128]{1,0:T(8,128)(2,1)S(1)}, bf16[1024,128]{1,0:T(8,128)(2,1)S(1)}, u32[]{:S(2)}, u32[]{:S(2)}) collective-permute-start(bf16[1024,128]{1,0:T(8,128)(2,1)S(1)} %copy-done.15), channel_id=1, source_target_pairs={{0,96},{32,0},{64,32},{96,64},{1,97},{33,1},{65,33},{97,65},{2,98}... | collective-permute-start | bytes 786440 | tf_op jit(solution)/shard_map/ppermute | solution.py:472
  73.5 6.8 %copy-start.1 = (bf16[64,8192]{1,0:T(8,128)(2,1)}, bf16[64,8192]{1,0:T(8,128)(2,1)S(1)}, u32[]{:S(2)}) copy-start(bf16[64,8192]{1,0:T(8,128)(2,1)S(1)} %collective-permute-done.7.above_ref.refs_1_) | copy-start | bytes 3145732
  76.8 3.5 %copy-start.2 = (bf16[64,8192]{1,0:T(8,128)(2,1)}, bf16[64,8192]{1,0:T(8,128)(2,1)S(1)}, u32[]{:S(2)}) copy-start(bf16[64,8192]{1,0:T(8,128)(2,1)S(1)} %collective-permute-done.8.below_ref.refs_2_) | copy-start | bytes 3145732
  76.8 28.9 %collective-permute-start.20 = (bf16[512,8192]{1,0:T(8,128)(2,1)}, bf16[512,8192]{1,0:T(8,128)(2,1)}, u32[]{:S(2)}, u32[]{:S(2)}) collective-permute-start(bf16[512,8192]{1,0:T(8,128)(2,1)} %refs_0_), channel_id=1, source_target_pairs={{0,1},{1,0},{2,3},{3,2},{4,5},{5,4},{6,7},{7,6},{8,9},{9,8},{10,11... | collective-permute-start | bytes 25165832 | tf_op jit(solution)/shard_map/ppermute | solution.py:467
  77.0 15.6 %collective-permute-start.14 = (bf16[32,8192]{1,0:T(8,128)(2,1)S(1)}, bf16[32,8192]{1,0:T(8,128)(2,1)S(1)}, u32[]{:S(2)}, u32[]{:S(2)}) collective-permute-start(bf16[32,8192]{1,0:T(8,128)(2,1)S(1)} %get-tuple-element.131), channel_id=1, source_target_pairs={{0,2},{2,4},{4,6},{6,0},{1,3},{3,5},{5,7},{7,1},{8,10},{10,12},{12... | collective-permute-start | bytes 1572872 | tf_op jit(solution)/shard_map/ppermute | solution.py:472
  77.1 13.9 %copy-start.13 = (bf16[1024,128]{1,0:T(8,128)(2,1)S(1)}, bf16[1024,128]{1,0:T(8,128)(2,1)}, u32[]{:S(2)}) copy-start(bf16[1024,128]{1,0:T(8,128)(2,1)} %copy-done.12) | copy-start | bytes 786436
  77.1 15.5 %copy-start.20 = (bf16[256,256]{1,0:T(8,128)(2,1)S(1)}, bf16[256,256]{1,0:T(8,128)(2,1)}, u32[]{:S(2)}) copy-start(bf16[256,256]{1,0:T(8,128)(2,1)} %get-tuple-element.146.refs_3_) | copy-start | bytes 393220
  77.1 16.1 %collective-permute-start.15 = (bf16[32,8192]{1,0:T(8,128)(2,1)S(1)}, bf16[32,8192]{1,0:T(8,128)(2,1)S(1)}, u32[]{:S(2)}, u32[]{:S(2)}) collective-permute-start(bf16[32,8192]{1,0:T(8,128)(2,1)S(1)} %get-tuple-element.132), channel_id=1, source_target_pairs={{0,6},{2,0},{4,2},{6,4},{1,7},{3,1},{5,3},{7,5},{8,14},{10,8},{12,... | collective-permute-start | bytes 1572872 | tf_op jit(solution)/shard_map/ppermute | solution.py:472
  91.0 12.8 %collective-permute-start.16 = (bf16[1024,128]{1,0:T(8,128)(2,1)S(1)}, bf16[1024,128]{1,0:T(8,128)(2,1)S(1)}, u32[]{:S(2)}, u32[]{:S(2)}) collective-permute-start(bf16[1024,128]{1,0:T(8,128)(2,1)S(1)} %add_convert_fusion), channel_id=1, source_target_pairs={{0,32},{32,64},{64,96},{96,0},{1,33},{33,65},{65,97},{97,1},{2,34}... | collective-permute-start | bytes 786440 | tf_op jit(solution)/shard_map/ppermute | solution.py:472
  92.6 12.0 %collective-permute-start.18 = (bf16[192,256]{1,0:T(8,128)(2,1)}, bf16[192,256]{1,0:T(8,128)(2,1)S(1)}, u32[]{:S(2)}, u32[]{:S(2)}) collective-permute-start(bf16[192,256]{1,0:T(8,128)(2,1)} %get-tuple-element.147.refs_4_), channel_id=1, source_target_pairs={{0,1},{1,0},{2,3},{3,2},{4,5},{5,4},{6,7},{7,6},{8,9},{9,8},{10,11... | collective-permute-start | bytes 294920 | tf_op jit(solution)/shard_map/ppermute | solution.py:467
  92.6 0.8 copy-start.18
  92.6 12.0 %collective-permute-start.17 = (bf16[256,256]{1,0:T(8,128)(2,1)S(1)}, bf16[256,256]{1,0:T(8,128)(2,1)S(1)}, u32[]{:S(2)}, u32[]{:S(2)}) collective-permute-start(bf16[256,256]{1,0:T(8,128)(2,1)S(1)} %copy-done.20), channel_id=1, source_target_pairs={{0,1},{1,0},{2,3},{3,2},{4,5},{5,4},{6,7},{7,6},{8,9},{9,8},{10,11... | collective-permute-start | bytes 393224 | tf_op jit(solution)/shard_map/ppermute | solution.py:467
  93.4 0.8 copy-start.19
  103.9 1.8 collective-permute-start.19
  104.6 1.1 copy-start.22
  104.7 1.1 copy-start.21
  105.7 0.6 copy-start.23
  120.6 15.7 %collective-permute-start.21 = (bf16[64,4096]{1,0:T(8,128)(2,1)}, bf16[64,4096]{1,0:T(8,128)(2,1)S(1)}, u32[]{:S(2)}, u32[]{:S(2)}) collective-permute-start(bf16[64,4096]{1,0:T(8,128)(2,1)} %get-tuple-element.153), channel_id=1, source_target_pairs={{0,2},{2,4},{4,6},{6,0},{1,3},{3,5},{5,7},{7,1},{8,10},{10,12},{12... | collective-permute-start | bytes 1572872 | tf_op jit(solution)/shard_map/ppermute | solution.py:472
  120.7 15.6 %collective-permute-start.22 = (bf16[64,4096]{1,0:T(8,128)(2,1)}, bf16[64,4096]{1,0:T(8,128)(2,1)S(1)}, u32[]{:S(2)}, u32[]{:S(2)}) collective-permute-start(bf16[64,4096]{1,0:T(8,128)(2,1)} %get-tuple-element.154), channel_id=1, source_target_pairs={{0,6},{2,0},{4,2},{6,4},{1,7},{3,1},{5,3},{7,5},{8,14},{10,8},{12,... | collective-permute-start | bytes 1572872 | tf_op jit(solution)/shard_map/ppermute | solution.py:472
  124.0 12.3 %copy-start.6 = (bf16[64,8192]{1,0:T(8,128)(2,1)S(1)}, bf16[64,8192]{1,0:T(8,128)(2,1)}, u32[]{:S(2)}) copy-start(bf16[64,8192]{1,0:T(8,128)(2,1)} %get-tuple-element.163.refs_0_) | copy-start | bytes 3145732
  124.0 12.3 %copy-start.7 = (bf16[64,8192]{1,0:T(8,128)(2,1)S(1)}, bf16[64,8192]{1,0:T(8,128)(2,1)}, u32[]{:S(2)}) copy-start(bf16[64,8192]{1,0:T(8,128)(2,1)} %get-tuple-element.165.refs_2_) | copy-start | bytes 3145732
  124.0 12.6 %collective-permute-start.23 = (bf16[512,128]{1,0:T(8,128)(2,1)S(1)}, bf16[512,128]{1,0:T(8,128)(2,1)S(1)}, u32[]{:S(2)}, u32[]{:S(2)}) collective-permute-start(bf16[512,128]{1,0:T(8,128)(2,1)S(1)} %add_convert_fusion.1), channel_id=1, source_target_pairs={{0,16},{16,0},{1,17},{17,1},{2,18},{18,2},{3,19},{19,3},{4,20},{20... | collective-permute-start | bytes 393224 | tf_op jit(solution)/shard_map/ppermute | solution.py:467
  135.1 4.9 %copy-start.25 = (bf16[64,4096]{1,0:T(8,128)(2,1)S(1)}, bf16[64,4096]{1,0:T(8,128)(2,1)}, u32[]{:S(2)}) copy-start(bf16[64,4096]{1,0:T(8,128)(2,1)} %get-tuple-element.186) | copy-start | bytes 1572868
  135.1 5.0 %copy-start.24 = (bf16[64,4096]{1,0:T(8,128)(2,1)S(1)}, bf16[64,4096]{1,0:T(8,128)(2,1)}, u32[]{:S(2)}) copy-start(bf16[64,4096]{1,0:T(8,128)(2,1)} %get-tuple-element.188) | copy-start | bytes 1572868
  135.1 8.2 %copy-start.11 = (f32[512,128]{1,0:T(8,128)S(1)}, f32[512,128]{1,0:T(8,128)}, u32[]{:S(2)}) copy-start(f32[512,128]{1,0:T(8,128)} %refs_4_.3) | copy-start | bytes 786436
  136.3 27.7 %copy-start = (bf16[64,8192]{1,0:T(8,128)(2,1)S(1)}, bf16[64,8192]{1,0:T(8,128)(2,1)}, u32[]{:S(2)}) copy-start(bf16[64,8192]{1,0:T(8,128)(2,1)} %get-tuple-element.177.refs_0_.refs_3_) | copy-start | bytes 3145732
  136.6 27.4 %collective-permute-start.24 = (bf16[64,8192]{1,0:T(8,128)(2,1)S(1)}, bf16[64,8192]{1,0:T(8,128)(2,1)S(1)}, u32[]{:S(2)}, u32[]{:S(2)}) collective-permute-start(bf16[64,8192]{1,0:T(8,128)(2,1)S(1)} %get-tuple-element.172), channel_id=1, source_target_pairs={{0,2},{2,4},{4,6},{6,0},{1,3},{3,5},{5,7},{7,1},{8,10},{10,12},{12... | collective-permute-start | bytes 3145736 | tf_op jit(solution)/shard_map/ppermute | solution.py:472
  136.7 27.3 %collective-permute-start.25 = (bf16[64,8192]{1,0:T(8,128)(2,1)S(1)}, bf16[64,8192]{1,0:T(8,128)(2,1)S(1)}, u32[]{:S(2)}, u32[]{:S(2)}) collective-permute-start(bf16[64,8192]{1,0:T(8,128)(2,1)S(1)} %get-tuple-element.173), channel_id=1, source_target_pairs={{0,6},{2,0},{4,2},{6,4},{1,7},{3,1},{5,3},{7,5},{8,14},{10,8},{12,... | collective-permute-start | bytes 3145736 | tf_op jit(solution)/shard_map/ppermute | solution.py:472
  140.0 33.7 %collective-permute-start.32 = (bf16[64,4096]{1,0:T(8,128)(2,1)S(1)}, bf16[64,4096]{1,0:T(8,128)(2,1)S(1)}, u32[]{:S(2)}, u32[]{:S(2)}) collective-permute-start(bf16[64,4096]{1,0:T(8,128)(2,1)S(1)} %copy-done.25), channel_id=1, source_target_pairs={{0,2},{2,4},{4,6},{6,0},{1,3},{3,5},{5,7},{7,1},{8,10},{10,12},{12... | collective-permute-start | bytes 1572872 | tf_op jit(solution)/shard_map/ppermute | solution.py:472
  140.1 33.6 %collective-permute-start.33 = (bf16[64,4096]{1,0:T(8,128)(2,1)S(1)}, bf16[64,4096]{1,0:T(8,128)(2,1)S(1)}, u32[]{:S(2)}, u32[]{:S(2)}) collective-permute-start(bf16[64,4096]{1,0:T(8,128)(2,1)S(1)} %copy-done.24), channel_id=1, source_target_pairs={{0,6},{2,0},{4,2},{6,4},{1,7},{3,1},{5,3},{7,5},{8,14},{10,8},{12,... | collective-permute-start | bytes 1572872 | tf_op jit(solution)/shard_map/ppermute | solution.py:472
  144.8 5.0 %collective-permute-start.26 = (bf16[512,128]{1,0:T(8,128)(2,1)S(1)}, bf16[512,128]{1,0:T(8,128)(2,1)S(1)}, u32[]{:S(2)}, u32[]{:S(2)}) collective-permute-start(bf16[512,128]{1,0:T(8,128)(2,1)S(1)} %get-tuple-element.175), channel_id=1, source_target_pairs={{0,16},{16,0},{1,17},{17,1},{2,18},{18,2},{3,19},{19,3},{4,20},{20... | collective-permute-start | bytes 393224 | tf_op jit(solution)/shard_map/ppermute | solution.py:467
  149.9 23.9 %copy-start.4 = (bf16[64,8192]{1,0:T(8,128)(2,1)S(1)}, bf16[64,8192]{1,0:T(8,128)(2,1)}, u32[]{:S(2)}) copy-start(bf16[64,8192]{1,0:T(8,128)(2,1)} %get-tuple-element.185.refs_0_) | copy-start | bytes 3145732
  149.9 23.9 %copy-start.5 = (bf16[64,8192]{1,0:T(8,128)(2,1)S(1)}, bf16[64,8192]{1,0:T(8,128)(2,1)}, u32[]{:S(2)}) copy-start(bf16[64,8192]{1,0:T(8,128)(2,1)} %get-tuple-element.187.refs_2_) | copy-start | bytes 3145732
  149.9 7.7 %collective-permute-start.27 = (bf16[1024,128]{1,0:T(8,128)(2,1)S(1)}, bf16[1024,128]{1,0:T(8,128)(2,1)S(1)}, u32[]{:S(2)}, u32[]{:S(2)}) collective-permute-start(bf16[1024,128]{1,0:T(8,128)(2,1)S(1)} %constant_dynamic-update-slice_fusion.refs_0_), channel_id=1, source_target_pairs={{0,32},{32,64},{64,96},{96,0},{1,33},{33,65},{65,97},{97,1},{2,34}... | collective-permute-start | bytes 786440 | tf_op jit(solution)/shard_map/ppermute | solution.py:472
  164.4 27.1 %copy-start.9 = (bf16[512,1024]{1,0:T(8,128)(2,1)S(1)}, bf16[512,1024]{1,0:T(8,128)(2,1)}, u32[]{:S(2)}) copy-start(bf16[512,1024]{1,0:T(8,128)(2,1)} %params_ref.1) | copy-start | bytes 3145732
  164.4 15.2 %collective-permute-start.29 = (bf16[64,4096]{1,0:T(8,128)(2,1)S(1)}, bf16[64,4096]{1,0:T(8,128)(2,1)S(1)}, u32[]{:S(2)}, u32[]{:S(2)}) collective-permute-start(bf16[64,4096]{1,0:T(8,128)(2,1)S(1)} %get-tuple-element.180.refs_4_), channel_id=1, source_target_pairs={{0,16},{16,8},{8,24},{24,0},{1,17},{17,9},{9,25},{25,1},{2,18},{18... | collective-permute-start | bytes 1572872 | tf_op jit(solution)/shard_map/ppermute | solution.py:472
  165.1 14.4 %collective-permute-start.30 = (bf16[64,4096]{1,0:T(8,128)(2,1)S(1)}, bf16[64,4096]{1,0:T(8,128)(2,1)S(1)}, u32[]{:S(2)}, u32[]{:S(2)}) collective-permute-start(bf16[64,4096]{1,0:T(8,128)(2,1)S(1)} %get-tuple-element.181), channel_id=1, source_target_pairs={{0,24},{16,0},{8,16},{24,8},{1,25},{17,1},{9,17},{25,9},{2,26},{18... | collective-permute-start | bytes 1572872 | tf_op jit(solution)/shard_map/ppermute | solution.py:472
  174.0 25.0 %copy-start.3 = (bf16[64,8192]{1,0:T(8,128)(2,1)S(1)}, bf16[64,8192]{1,0:T(8,128)(2,1)}, u32[]{:S(2)}) copy-start(bf16[64,8192]{1,0:T(8,128)(2,1)} %get-tuple-element.184.refs_0_) | copy-start | bytes 3145732
  174.1 25.0 %collective-permute-start.34 = (bf16[64,8192]{1,0:T(8,128)(2,1)S(1)}, bf16[64,8192]{1,0:T(8,128)(2,1)S(1)}, u32[]{:S(2)}, u32[]{:S(2)}) collective-permute-start(bf16[64,8192]{1,0:T(8,128)(2,1)S(1)} %get-tuple-element.189), channel_id=1, source_target_pairs={{0,2},{2,4},{4,6},{6,0},{1,3},{3,5},{5,7},{7,1},{8,10},{10,12},{12... | collective-permute-start | bytes 3145736 | tf_op jit(solution)/shard_map/ppermute | solution.py:472
  174.9 24.1 %collective-permute-start.35 = (bf16[64,8192]{1,0:T(8,128)(2,1)S(1)}, bf16[64,8192]{1,0:T(8,128)(2,1)S(1)}, u32[]{:S(2)}, u32[]{:S(2)}) collective-permute-start(bf16[64,8192]{1,0:T(8,128)(2,1)S(1)} %get-tuple-element.190), channel_id=1, source_target_pairs={{0,6},{2,0},{4,2},{6,4},{1,7},{3,1},{5,3},{7,5},{8,14},{10,8},{12,... | collective-permute-start | bytes 3145736 | tf_op jit(solution)/shard_map/ppermute | solution.py:472
  177.4 6.4 %collective-permute-start.28 = (bf16[1024,128]{1,0:T(8,128)(2,1)S(1)}, bf16[1024,128]{1,0:T(8,128)(2,1)S(1)}, u32[]{:S(2)}, u32[]{:S(2)}) collective-permute-start(bf16[1024,128]{1,0:T(8,128)(2,1)S(1)} %constant_dynamic-update-slice_fusion.refs_0_), channel_id=1, source_target_pairs={{0,96},{32,0},{64,32},{96,64},{1,97},{33,1},{65,33},{97,65},{2,98}... | collective-permute-start | bytes 786440 | tf_op jit(solution)/shard_map/ppermute | solution.py:472
  179.5 19.5 %collective-permute-start.36 = (bf16[64,4096]{1,0:T(8,128)(2,1)S(1)}, bf16[64,4096]{1,0:T(8,128)(2,1)S(1)}, u32[]{:S(2)}, u32[]{:S(2)}) collective-permute-start(bf16[64,4096]{1,0:T(8,128)(2,1)S(1)} %collective-permute-done.29), channel_id=1, source_target_pairs={{0,16},{16,8},{8,24},{24,0},{1,17},{17,9},{9,25},{25,1},{2,18},{18... | collective-permute-start | bytes 1572872 | tf_op jit(solution)/shard_map/ppermute | solution.py:472
  180.2 18.9 %collective-permute-start.37 = (bf16[64,4096]{1,0:T(8,128)(2,1)S(1)}, bf16[64,4096]{1,0:T(8,128)(2,1)S(1)}, u32[]{:S(2)}, u32[]{:S(2)}) collective-permute-start(bf16[64,4096]{1,0:T(8,128)(2,1)S(1)} %collective-permute-done.30), channel_id=1, source_target_pairs={{0,24},{16,0},{8,16},{24,8},{1,25},{17,1},{9,17},{25,9},{2,26},{18... | collective-permute-start | bytes 1572872 | tf_op jit(solution)/shard_map/ppermute | solution.py:472
  183.7 7.7 %collective-permute-start.31 = (bf16[1024,128]{1,0:T(8,128)(2,1)S(1)}, bf16[1024,128]{1,0:T(8,128)(2,1)S(1)}, u32[]{:S(2)}, u32[]{:S(2)}) collective-permute-start(bf16[1024,128]{1,0:T(8,128)(2,1)S(1)} %collective-permute-done.27.refs_2_), channel_id=1, source_target_pairs={{0,32},{32,64},{64,96},{96,0},{1,33},{33,65},{65,97},{97,1},{2,34}... | collective-permute-start | bytes 786440 | tf_op jit(solution)/shard_map/ppermute | solution.py:472

commit v4 on v1

--- a/solution.py
+++ b/solution.py
@@ -17,6 +17,7 @@
 Y = ("ylo", "yhi")
 HALVES = 2
 TILE = 1024
+STRIP = 256
 PIECES = (1, 1, 1, HALVES)
 MIB = 1024 * 1024
 
@@ -159,15 +160,17 @@
         def step(at, carry, part=part):
             for copy in copies_of(weights, held, arrived, first, at):
                 copy.wait()
-            span = pl.ds(pl.multiple_of(at * TILE, TILE), TILE)
-            result = jnp.dot(rows_of(), held[:, span], preferred_element_type=jnp.float32)
-            result = result.astype(jnp.bfloat16)
-            for block, pieces in enumerate(out_refs):
-                back = part * (tiles // parts) if len(pieces) == parts else 0
-                there = pl.ds(pl.multiple_of((at - back) * TILE, TILE), TILE)
-                pieces[part if len(pieces) == parts else 0][:, there] = result[
-                    block * ROWS : (block + 1) * ROWS
-                ]
+            rows = rows_of()
+            for left in range(0, TILE, STRIP):
+                strip = pl.ds(pl.multiple_of(at * TILE + left, STRIP), STRIP)
+                result = jnp.dot(rows, held[:, strip], preferred_element_type=jnp.float32)
+                result = result.astype(jnp.bfloat16)
+                for block, pieces in enumerate(out_refs):
+                    back = part * (tiles // parts) if len(pieces) == parts else 0
+                    there = pl.ds(pl.multiple_of((at - back) * TILE + left, STRIP), STRIP)
+                    pieces[part if len(pieces) == parts else 0][:, there] = result[
+                        block * ROWS : (block + 1) * ROWS
+                    ]
             return carry
 
         lax.fori_loop(part * (tiles // parts), (part + 1) * (tiles // parts), step, 0)

time: 198 us -> 199 us (level)
  no operation moved by 1% of the time
where the time goes in v4:
time: 199 us; the launch traced here: 198 us
  Pallas kernels  70.5 us (35%)
  waiting for transfers between devices  70.5 us (35%)
  starting transfers between devices  51 us (26%)
  local copies, waits for them, and re-layouts  4.04 us (2%)
    ppermute x30, waiting for transfers between devices, hop(): lax.ppermute(block, axis, [(at[i], at[(i + way) % 4]) for i in range(4)])  65.6 us
    ppermute x30, starting transfers between devices, hop(): lax.ppermute(block, axis, [(at[i], at[(i + way) % 4]) for i in range(4)])  49 us
    pallas_call x3, Pallas kernels, project(): pl.pallas_call(project_body, in_specs=[pl.BlockSpec(memory_space=pltpu.SM...  32.3 us
    pallas_call x1, Pallas kernels, attend(): pl.pallas_call(functools.partial(attend_body, order), in_specs=[pl.BlockS...  14.6 us
    pallas_call x1, Pallas kernels, output(): pl.pallas_call(output_body, in_specs=[vmem] + [pl.BlockSpec(memory_space=...  10.8 us
    ppermute x8, waiting for transfers between devices, swap(): return lax.ppermute(block, axis, [(0, 1), (1, 0)])  4.85 us
  transfers between devices with their start and end apart: 38, of which 16 were waited for; matrix products, arithmetic and copies ran while one was open for 1% of the time, Pallas kernels for 26%

profile of v4, /device:TPU:0, one launch (start us, length us, event | category | flops | bytes accessed | tf_op | source)
XLA Modules:
  0.0 198.3 jit_solution(13410821930041470734)
XLA Ops:
  0.6 3.1 %normalize.1 = (bf16[64,8192]{1,0:T(8,128)(2,1)}, bf16[32,8192]{1,0:T(8,128)(2,1)}, bf16[32,8192]{1,0:T(8,128)(2,1)}) custom-call(bf16[64,8192]{1,0:T(8,128)(2,1)} %rows_ref.1, f32[1,8192]{1,0:T(1,128)} %bitcast.22), custom_call_target="tpu_custom_call" | custom-call | flops 2097152 | bytes 3145728 | tf_op jit(solution)/shard_map/normalize/pallas_call | solution.py:55
  3.8 1.7 collective-permute-start
  5.4 1.6 collective-permute-start.1
  7.0 2.0 %collective-permute-start.5 = (bf16[64,8192]{1,0:T(8,128)(2,1)}, bf16[64,8192]{1,0:T(8,128)(2,1)S(1)}, u32[]{:S(2)}, u32[]{:S(2)}) collective-permute-start(bf16[64,8192]{1,0:T(8,128)(2,1)} %get-tuple-element.94.refs_0_), channel_id=1, source_target_pairs={{0,2},{2,4},{4,6},{6,0},{1,3},{3,5},{5,7},{7,1},{8,10},{10,12},{12... | collective-permute-start | bytes 3145736 | tf_op jit(solution)/shard_map/ppermute | solution.py:473
  9.0 2.1 %collective-permute-start.6 = (bf16[64,8192]{1,0:T(8,128)(2,1)}, bf16[64,8192]{1,0:T(8,128)(2,1)}, u32[]{:S(2)}, u32[]{:S(2)}) collective-permute-start(bf16[64,8192]{1,0:T(8,128)(2,1)} %get-tuple-element.94.refs_0_), channel_id=1, source_target_pairs={{0,6},{2,0},{4,2},{6,4},{1,7},{3,1},{5,3},{7,5},{8,14},{10,8},{12,... | collective-permute-start | bytes 3145736 | tf_op jit(solution)/shard_map/ppermute | solution.py:473
  11.1 0.8 copy.14
  12.1 1.2 terms.1
  13.3 6.4 %collective-permute-done = bf16[32,8192]{1,0:T(8,128)(2,1)S(1)} collective-permute-done((bf16[32,8192]{1,0:T(8,128)(2,1)}, bf16[32,8192]{1,0:T(8,128)(2,1)S(1)}, u32[]{:S(2)}, u32[]{:S(2)}) %collective-permute-start) | collective-permute-done | bytes 524320 | tf_op jit(solution)/shard_map/ppermute | solution.py:473
  19.8 2.9 %collective-permute-start.4 = (bf16[32,8192]{1,0:T(8,128)(2,1)}, bf16[32,8192]{1,0:T(8,128)(2,1)S(1)}, u32[]{:S(2)}, u32[]{:S(2)}) collective-permute-start(bf16[32,8192]{1,0:T(8,128)(2,1)} %collective-permute-done.1), channel_id=1, source_target_pairs={{0,24},{16,0},{8,16},{24,8},{1,25},{17,1},{9,17},{25,9},{2,26},{18... | collective-permute-start | bytes 1572872 | tf_op jit(solution)/shard_map/ppermute | solution.py:473
  22.7 11.9 %collective-permute-done.5.refs_0_ = bf16[64,8192]{1,0:T(8,128)(2,1)S(1)} collective-permute-done((bf16[64,8192]{1,0:T(8,128)(2,1)}, bf16[64,8192]{1,0:T(8,128)(2,1)S(1)}, u32[]{:S(2)}, u32[]{:S(2)}) %collective-permute-start.5) | collective-permute-done | bytes 1048608 | tf_op jit(solution)/shard_map/ppermute | solution.py:473
  34.7 2.6 %pick.2 = (bf16[32,8192]{1,0:T(8,128)(2,1)}, bf16[32,8192]{1,0:T(8,128)(2,1)}) custom-call(bf16[64,8192]{1,0:T(8,128)(2,1)S(1)} %get-tuple-element.107.below_ref.refs_2_, bf16[64,8192]{1,0:T(8,128)(2,1)} %get-tuple-element.106.above_ref.refs_1_), custom_call_target="tpu_custom_call" | custom-call | flops 100000000 | bytes 2097152 | tf_op jit(solution)/shard_map/pick/pallas_call | solution.py:334
  37.3 1.4 collective-permute-start.9
  38.7 1.9 collective-permute-start.10
  40.6 1.1 pad_maximum_fusion.refs_0_
  41.6 1.8 collective-permute-start.7
  43.7 10.0 %collective-permute-done.9.refs_3_ = bf16[32,8192]{1,0:T(8,128)(2,1)} collective-permute-done((bf16[32,8192]{1,0:T(8,128)(2,1)}, bf16[32,8192]{1,0:T(8,128)(2,1)}, u32[]{:S(2)}, u32[]{:S(2)}) %collective-permute-start.9) | collective-permute-done | bytes 524320 | tf_op jit(solution)/shard_map/ppermute | solution.py:473
  53.9 12.1 %project.3 = (bf16[256,1024]{1,0:T(8,128)(2,1)}, bf16[256,256]{1,0:T(8,128)(2,1)}) custom-call(s32[1]{0:T(128)} %bitcast.core_ref, bf16[64,8192]{1,0:T(8,128)(2,1)} %get-tuple-element.94.refs_0_, bf16[64,8192]{1,0:T(8,128)(2,1)} %get-tuple-element.106.above_ref.refs_1_, bf16[64,8192]{1,0:T(8,128)(2,1)} %copy-done.10, ...), custom_call_target="tpu_custom_call" | custom-call | flops 8053063680 | bytes 25165824 | tf_op jit(solution)/shard_map/project/pallas_call | solution.py:115
  66.0 1.6 collective-permute-start.12
  67.5 1.7 collective-permute-start.13
  69.3 4.6 %collective-permute-done.7.above_ref.refs_1_ = bf16[64,8192]{1,0:T(8,128)(2,1)S(1)} collective-permute-done((bf16[64,8192]{1,0:T(8,128)(2,1)}, bf16[64,8192]{1,0:T(8,128)(2,1)S(1)}, u32[]{:S(2)}, u32[]{:S(2)}) %collective-permute-start.7) | collective-permute-done | bytes 1048608 | tf_op jit(solution)/shard_map/ppermute | solution.py:473
  73.9 0.6 collective-permute-done.8.below_ref.refs_2_
  74.5 0.7 copy-done.20
  75.4 1.0 collective-permute-start.14
  76.3 2.3 %collective-permute-start.15 = (bf16[32,8192]{1,0:T(8,128)(2,1)S(1)}, bf16[32,8192]{1,0:T(8,128)(2,1)S(1)}, u32[]{:S(2)}, u32[]{:S(2)}) collective-permute-start(bf16[32,8192]{1,0:T(8,128)(2,1)S(1)} %get-tuple-element.124), channel_id=1, source_target_pairs={{0,6},{2,0},{4,2},{6,4},{1,7},{3,1},{5,3},{7,5},{8,14},{10,8},{12,... | collective-permute-start | bytes 1572872 | tf_op jit(solution)/shard_map/ppermute | solution.py:473
  78.7 1.6 collective-permute-start.16
  80.3 10.6 %project.4 = (bf16[192,1024]{1,0:T(8,128)(2,1)}, bf16[192,256]{1,0:T(8,128)(2,1)}) custom-call(s32[1]{0:T(128)} %bitcast.core_ref, bf16[64,8192]{1,0:T(8,128)(2,1)} %pad_maximum_fusion.refs_0_, bf16[64,8192]{1,0:T(8,128)(2,1)} %copy-done.1, bf16[64,8192]{1,0:T(8,128)(2,1)} %copy-done.2, bf16[8192,512]{1,0:T(8,128)(2,1)} %refs_2_, ...), custom_call_target="tpu_custom_call" | custom-call | flops 6039797760 | bytes 24117248 | tf_op jit(solution)/shard_map/project/pallas_call | solution.py:115
  91.0 0.6 collective-permute-start.18
  91.6 0.8 copy-done.18
  92.5 9.6 %project.5 = (bf16[64,1024]{1,0:T(8,128)(2,1)}, bf16[64,256]{1,0:T(8,128)(2,1)}) custom-call(s32[1]{0:T(128)} %bitcast.core_ref, bf16[32,8192]{1,0:T(8,128)(2,1)} %copy-done.18, bf16[32,8192]{1,0:T(8,128)(2,1)} %copy-done.19, bf16[8192,512]{1,0:T(8,128)(2,1)} %refs_2_, bf16[8192,512]{1,0:T(8,128)(2,1)} %collective-permute-done.11.refs_6_.refs_4_.refs_3_, ...), custom_call_target="tpu_custom_call" | custom-call | flops 2013265920 | bytes 22020096 | tf_op jit(solution)/shard_map/project/pallas_call | solution.py:115
  102.2 0.3 collective-permute-start.19
  102.5 0.7 concatenate.9.place_ref
  103.2 0.6 collective-permute-done.19.refs_8_
  103.8 0.6 copy-done.24
  104.4 14.6 %attend.1 = (bf16[512,1024]{1,0:T(8,128)(2,1)}, bf16[64,8192]{1,0:T(8,128)(2,1)}, bf16[64,8192]{1,0:T(8,128)(2,1)}, bf16[64,8192]{1,0:T(8,128)(2,1)}, bf16[64,40...) custom-call(s32[1]{0:T(128)} %bitcast.core_ref, s32[16]{0:T(128)} %concatenate.9.place_ref, ...), custom_call_target="tpu_custom_call" | custom-call | flops 2147483648 | bytes 18874368 | tf_op jit(solution)/shard_map/attend/pallas_call | solution.py:253
  119.0 0.5 collective-permute-start.21
  119.5 2.8 %collective-permute-start.22 = (bf16[64,4096]{1,0:T(8,128)(2,1)}, bf16[64,4096]{1,0:T(8,128)(2,1)S(1)}, u32[]{:S(2)}, u32[]{:S(2)}) collective-permute-start(bf16[64,4096]{1,0:T(8,128)(2,1)} %get-tuple-element.140), channel_id=1, source_target_pairs={{0,6},{2,0},{4,2},{6,4},{1,7},{3,1},{5,3},{7,5},{8,14},{10,8},{12,... | collective-permute-start | bytes 1572872 | tf_op jit(solution)/shard_map/ppermute | solution.py:473
  122.4 0.3 collective-permute-start.23
  122.7 10.8 %output.1 = (bf16[64,8192]{1,0:T(8,128)(2,1)}, bf16[64,8192]{1,0:T(8,128)(2,1)}, bf16[64,8192]{1,0:T(8,128)(2,1)}, bf16[64,4096]{1,0:T(8,128)(2,1)}, bf16[64,4096]{1,0:T(8,128)(2,1)}) custom-call(bf16[512,1024]{1,0:T(8,128)(2,1)} %get-tuple-element.146.mixed_ref, bf16[512,8192]{1,0:T(8,128)(2,1)} %refs_0_, ...), custom_call_target="tpu_custom_call" | custom-call | flops 4294967296 | bytes 20971520 | tf_op jit(solution)/shard_map/output/pallas_call | solution.py:290
  133.6 0.9 collective-permute-done.21.refs_1_
  134.8 0.7 collective-permute-start.24
  135.6 2.6 %collective-permute-start.25 = (bf16[64,8192]{1,0:T(8,128)(2,1)S(1)}, bf16[64,8192]{1,0:T(8,128)(2,1)S(1)}, u32[]{:S(2)}, u32[]{:S(2)}) collective-permute-start(bf16[64,8192]{1,0:T(8,128)(2,1)S(1)} %get-tuple-element.159), channel_id=1, source_target_pairs={{0,6},{2,0},{4,2},{6,4},{1,7},{3,1},{5,3},{7,5},{8,14},{10,8},{12,... | collective-permute-start | bytes 3145736 | tf_op jit(solution)/shard_map/ppermute | solution.py:473
  138.3 3.2 %collective-permute-start.33 = (bf16[64,4096]{1,0:T(8,128)(2,1)S(1)}, bf16[64,4096]{1,0:T(8,128)(2,1)S(1)}, u32[]{:S(2)}, u32[]{:S(2)}) collective-permute-start(bf16[64,4096]{1,0:T(8,128)(2,1)S(1)} %copy-done.25), channel_id=1, source_target_pairs={{0,6},{2,0},{4,2},{6,4},{1,7},{3,1},{5,3},{7,5},{8,14},{10,8},{12,... | collective-permute-start | bytes 1572872 | tf_op jit(solution)/shard_map/ppermute | solution.py:473
  141.5 1.5 outer.1
  143.0 0.8 collective-permute-start.26
  143.8 4.2 %collective-permute-done.26 = bf16[512,128]{1,0:T(8,128)(2,1)S(1)} collective-permute-done((bf16[512,128]{1,0:T(8,128)(2,1)S(1)}, bf16[512,128]{1,0:T(8,128)(2,1)S(1)}, u32[]{:S(2)}, u32[]{:S(2)}) %collective-permute-start.26) | collective-permute-done | bytes 131104 | tf_op jit(solution)/shard_map/ppermute | solution.py:468
  148.1 1.8 collective-permute-start.27
  149.9 6.1 %collective-permute-done.27.refs_2_ = bf16[1024,128]{1,0:T(8,128)(2,1)S(1)} collective-permute-done((bf16[1024,128]{1,0:T(8,128)(2,1)S(1)}, bf16[1024,128]{1,0:T(8,128)(2,1)S(1)}, u32[]{:S(2)}, u32[]{:S(2)}) %collective-permute-start.27) | collective-permute-done | bytes 262176 | tf_op jit(solution)/shard_map/ppermute | solution.py:473
  156.0 6.2 %collective-permute-done.24.refs_1_.refs_4_ = bf16[64,8192]{1,0:T(8,128)(2,1)S(1)} collective-permute-done((bf16[64,8192]{1,0:T(8,128)(2,1)S(1)}, bf16[64,8192]{1,0:T(8,128)(2,1)S(1)}, u32[]{:S(2)}, u32[]{:S(2)}) %collective-permute-start.24) | collective-permute-done | bytes 1048608 | tf_op jit(solution)/shard_map/ppermute | solution.py:473
  162.2 0.4 sums.4
  162.6 0.8 collective-permute-start.29
  163.4 2.5 %collective-permute-start.30 = (bf16[64,4096]{1,0:T(8,128)(2,1)S(1)}, bf16[64,4096]{1,0:T(8,128)(2,1)S(1)}, u32[]{:S(2)}, u32[]{:S(2)}) collective-permute-start(bf16[64,4096]{1,0:T(8,128)(2,1)S(1)} %get-tuple-element.167), channel_id=1, source_target_pairs={{0,24},{16,0},{8,16},{24,8},{1,25},{17,1},{9,17},{25,9},{2,26},{18... | collective-permute-start | bytes 1572872 | tf_op jit(solution)/shard_map/ppermute | solution.py:473
  165.9 5.8 %collective-permute-done.32.refs_1_ = bf16[64,4096]{1,0:T(8,128)(2,1)S(1)} collective-permute-done((bf16[64,4096]{1,0:T(8,128)(2,1)S(1)}, bf16[64,4096]{1,0:T(8,128)(2,1)S(1)}, u32[]{:S(2)}, u32[]{:S(2)}) %collective-permute-start.32) | collective-permute-done | bytes 524320 | tf_op jit(solution)/shard_map/ppermute | solution.py:473
  171.8 0.3 sums.5
  172.0 0.9 collective-permute-start.34
  172.9 2.4 %collective-permute-start.35 = (bf16[64,8192]{1,0:T(8,128)(2,1)S(1)}, bf16[64,8192]{1,0:T(8,128)(2,1)S(1)}, u32[]{:S(2)}, u32[]{:S(2)}) collective-permute-start(bf16[64,8192]{1,0:T(8,128)(2,1)S(1)} %get-tuple-element.176), channel_id=1, source_target_pairs={{0,6},{2,0},{4,2},{6,4},{1,7},{3,1},{5,3},{7,5},{8,14},{10,8},{12,... | collective-permute-start | bytes 3145736 | tf_op jit(solution)/shard_map/ppermute | solution.py:473
  175.4 2.2 %collective-permute-start.28 = (bf16[1024,128]{1,0:T(8,128)(2,1)S(1)}, bf16[1024,128]{1,0:T(8,128)(2,1)S(1)}, u32[]{:S(2)}, u32[]{:S(2)}) collective-permute-start(bf16[1024,128]{1,0:T(8,128)(2,1)S(1)} %constant_dynamic-update-slice_fusion.refs_0_), channel_id=1, source_target_pairs={{0,96},{32,0},{64,32},{96,64},{1,97},{33,1},{65,33},{97,65},{2,98}... | collective-permute-start | bytes 786440 | tf_op jit(solution)/shard_map/ppermute | solution.py:473
  177.6 0.7 collective-permute-start.36
  178.3 2.5 %collective-permute-start.37 = (bf16[64,4096]{1,0:T(8,128)(2,1)S(1)}, bf16[64,4096]{1,0:T(8,128)(2,1)S(1)}, u32[]{:S(2)}, u32[]{:S(2)}) collective-permute-start(bf16[64,4096]{1,0:T(8,128)(2,1)S(1)} %collective-permute-done.30), channel_id=1, source_target_pairs={{0,24},{16,0},{8,16},{24,8},{1,25},{17,1},{9,17},{25,9},{2,26},{18... | collective-permute-start | bytes 1572872 | tf_op jit(solution)/shard_map/ppermute | solution.py:473
  180.8 0.9 collective-permute-done.28.refs_1_
  181.7 1.5 collective-permute-start.31
  183.2 6.2 %collective-permute-done.31.refs_3_ = bf16[1024,128]{1,0:T(8,128)(2,1)S(1)} collective-permute-done((bf16[1024,128]{1,0:T(8,128)(2,1)S(1)}, bf16[1024,128]{1,0:T(8,128)(2,1)S(1)}, u32[]{:S(2)}, u32[]{:S(2)}) %collective-permute-start.31) | collective-permute-done | bytes 262176 | tf_op jit(solution)/shard_map/ppermute | solution.py:473
  189.5 1.8 apply.1
  191.3 5.5 %collective-permute-done.34.refs_1_ = bf16[64,8192]{1,0:T(8,128)(2,1)S(1)} collective-permute-done((bf16[64,8192]{1,0:T(8,128)(2,1)S(1)}, bf16[64,8192]{1,0:T(8,128)(2,1)S(1)}, u32[]{:S(2)}, u32[]{:S(2)}) %collective-permute-start.34) | collective-permute-done | bytes 1048608 | tf_op jit(solution)/shard_map/ppermute | solution.py:473
  196.8 1.5 finish.1
  (92 shorter events, 1.6 us)
Async XLA Ops:
  0.6 11.4 %copy-start.8 = (bf16[1,512,1024]{2,1,0:T(8,128)(2,1)S(1)}, bf16[1,512,1024]{2,1,0:T(8,128)(2,1)}, u32[]{:S(2)}) copy-start(bf16[1,512,1024]{2,1,0:T(8,128)(2,1)} %param.14) | copy-start | bytes 3145732
  3.8 16.0 %collective-permute-start.2 = (bf16[8192,128]{1,0:T(8,128)(2,1)}, bf16[8192,128]{1,0:T(8,128)(2,1)}, u32[]{:S(2)}, u32[]{:S(2)}) collective-permute-start(bf16[8192,128]{1,0:T(8,128)(2,1)} %refs_4_.2), channel_id=1, source_target_pairs={{0,1},{1,0},{2,3},{3,2},{4,5},{5,4},{6,7},{7,6},{8,9},{9,8},{10,11... | collective-permute-start | bytes 6291464 | tf_op jit(solution)/shard_map/ppermute | solution.py:468
  3.8 15.9 %collective-permute-start = (bf16[32,8192]{1,0:T(8,128)(2,1)}, bf16[32,8192]{1,0:T(8,128)(2,1)S(1)}, u32[]{:S(2)}, u32[]{:S(2)}) collective-permute-start(bf16[32,8192]{1,0:T(8,128)(2,1)} %get-tuple-element.92), channel_id=1, source_target_pairs={{0,16},{16,8},{8,24},{24,0},{1,17},{17,9},{9,25},{25,1},{2,18},{18... | collective-permute-start | bytes 1572872 | tf_op jit(solution)/shard_map/ppermute | solution.py:473
  5.4 14.4 %collective-permute-start.1 = (bf16[32,8192]{1,0:T(8,128)(2,1)}, bf16[32,8192]{1,0:T(8,128)(2,1)}, u32[]{:S(2)}, u32[]{:S(2)}) collective-permute-start(bf16[32,8192]{1,0:T(8,128)(2,1)} %get-tuple-element.93), channel_id=1, source_target_pairs={{0,24},{16,0},{8,16},{24,8},{1,25},{17,1},{9,17},{25,9},{2,26},{18... | collective-permute-start | bytes 1572872 | tf_op jit(solution)/shard_map/ppermute | solution.py:473
  7.0 27.6 %collective-permute-start.5 = (bf16[64,8192]{1,0:T(8,128)(2,1)}, bf16[64,8192]{1,0:T(8,128)(2,1)S(1)}, u32[]{:S(2)}, u32[]{:S(2)}) collective-permute-start(bf16[64,8192]{1,0:T(8,128)(2,1)} %get-tuple-element.94.refs_0_), channel_id=1, source_target_pairs={{0,2},{2,4},{4,6},{6,0},{1,3},{3,5},{5,7},{7,1},{8,10},{10,12},{12... | collective-permute-start | bytes 3145736 | tf_op jit(solution)/shard_map/ppermute | solution.py:473
  9.0 25.7 %collective-permute-start.6 = (bf16[64,8192]{1,0:T(8,128)(2,1)}, bf16[64,8192]{1,0:T(8,128)(2,1)}, u32[]{:S(2)}, u32[]{:S(2)}) collective-permute-start(bf16[64,8192]{1,0:T(8,128)(2,1)} %get-tuple-element.94.refs_0_), channel_id=1, source_target_pairs={{0,6},{2,0},{4,2},{6,4},{1,7},{3,1},{5,3},{7,5},{8,14},{10,8},{12,... | collective-permute-start | bytes 3145736 | tf_op jit(solution)/shard_map/ppermute | solution.py:473
  13.2 21.4 %copy-start.12 = (bf16[1024,128]{1,0:T(8,128)(2,1)}, bf16[1024,128]{1,0:T(8,128)(2,1)S(1)}, u32[]{:S(2)}) copy-start(bf16[1024,128]{1,0:T(8,128)(2,1)S(1)} %get-tuple-element.125) | copy-start | bytes 786436
  13.2 21.4 %copy-start.14 = (bf16[1024,128]{1,0:T(8,128)(2,1)}, bf16[1024,128]{1,0:T(8,128)(2,1)S(1)}, u32[]{:S(2)}) copy-start(bf16[1024,128]{1,0:T(8,128)(2,1)S(1)} %get-tuple-element.118) | copy-start | bytes 786436
  13.3 21.4 %copy-start.16 = (bf16[1024,128]{1,0:T(8,128)(2,1)}, bf16[1024,128]{1,0:T(8,128)(2,1)S(1)}, u32[]{:S(2)}) copy-start(bf16[1024,128]{1,0:T(8,128)(2,1)S(1)} %get-tuple-element.117) | copy-start | bytes 786436
  19.8 34.1 %collective-permute-start.11 = (bf16[8192,512]{1,0:T(8,128)(2,1)}, bf16[8192,512]{1,0:T(8,128)(2,1)}, u32[]{:S(2)}, u32[]{:S(2)}) collective-permute-start(bf16[8192,512]{1,0:T(8,128)(2,1)} %refs_2_), channel_id=1, source_target_pairs={{0,1},{1,0},{2,3},{3,2},{4,5},{5,4},{6,7},{7,6},{8,9},{9,8},{10,11... | collective-permute-start | bytes 25165832 | tf_op jit(solution)/shard_map/ppermute | solution.py:468
  19.8 20.8 %collective-permute-start.4 = (bf16[32,8192]{1,0:T(8,128)(2,1)}, bf16[32,8192]{1,0:T(8,128)(2,1)S(1)}, u32[]{:S(2)}, u32[]{:S(2)}) collective-permute-start(bf16[32,8192]{1,0:T(8,128)(2,1)} %collective-permute-done.1), channel_id=1, source_target_pairs={{0,24},{16,0},{8,16},{24,8},{1,25},{17,1},{9,17},{25,9},{2,26},{18... | collective-permute-start | bytes 1572872 | tf_op jit(solution)/shard_map/ppermute | solution.py:473
  22.7 17.8 %collective-permute-start.3 = (bf16[32,8192]{1,0:T(8,128)(2,1)S(1)}, bf16[32,8192]{1,0:T(8,128)(2,1)S(1)}, u32[]{:S(2)}, u32[]{:S(2)}) collective-permute-start(bf16[32,8192]{1,0:T(8,128)(2,1)S(1)} %collective-permute-done), channel_id=1, source_target_pairs={{0,16},{16,8},{8,24},{24,0},{1,17},{17,9},{9,25},{25,1},{2,18},{18... | collective-permute-start | bytes 1572872 | tf_op jit(solution)/shard_map/ppermute | solution.py:473
  34.7 6.9 %copy-start.10 = (bf16[64,8192]{1,0:T(8,128)(2,1)}, bf16[64,8192]{1,0:T(8,128)(2,1)S(1)}, u32[]{:S(2)}) copy-start(bf16[64,8192]{1,0:T(8,128)(2,1)S(1)} %get-tuple-element.107.below_ref.refs_2_) | copy-start | bytes 3145732
  37.3 16.4 %collective-permute-start.9 = (bf16[32,8192]{1,0:T(8,128)(2,1)}, bf16[32,8192]{1,0:T(8,128)(2,1)}, u32[]{:S(2)}, u32[]{:S(2)}) collective-permute-start(bf16[32,8192]{1,0:T(8,128)(2,1)} %get-tuple-element.108), channel_id=1, source_target_pairs={{0,2},{2,4},{4,6},{6,0},{1,3},{3,5},{5,7},{7,1},{8,10},{10,12},{12... | collective-permute-start | bytes 1572872 | tf_op jit(solution)/shard_map/ppermute | solution.py:473
  38.7 15.2 %collective-permute-start.10 = (bf16[32,8192]{1,0:T(8,128)(2,1)}, bf16[32,8192]{1,0:T(8,128)(2,1)}, u32[]{:S(2)}, u32[]{:S(2)}) collective-permute-start(bf16[32,8192]{1,0:T(8,128)(2,1)} %get-tuple-element.109), channel_id=1, source_target_pairs={{0,6},{2,0},{4,2},{6,4},{1,7},{3,1},{5,3},{7,5},{8,14},{10,8},{12,... | collective-permute-start | bytes 1572872 | tf_op jit(solution)/shard_map/ppermute | solution.py:473
  41.6 32.3 %collective-permute-start.7 = (bf16[64,8192]{1,0:T(8,128)(2,1)}, bf16[64,8192]{1,0:T(8,128)(2,1)S(1)}, u32[]{:S(2)}, u32[]{:S(2)}) collective-permute-start(bf16[64,8192]{1,0:T(8,128)(2,1)} %pad_maximum_fusion.refs_0_), channel_id=1, source_target_pairs={{0,6},{2,0},{4,2},{6,4},{1,7},{3,1},{5,3},{7,5},{8,14},{10,8},{12,... | collective-permute-start | bytes 3145736 | tf_op jit(solution)/shard_map/ppermute | solution.py:473
  43.5 31.0 %collective-permute-start.8 = (bf16[64,8192]{1,0:T(8,128)(2,1)}, bf16[64,8192]{1,0:T(8,128)(2,1)S(1)}, u32[]{:S(2)}, u32[]{:S(2)}) collective-permute-start(bf16[64,8192]{1,0:T(8,128)(2,1)} %pad_maximum_fusion.refs_0_), channel_id=1, source_target_pairs={{0,2},{2,4},{4,6},{6,0},{1,3},{3,5},{5,7},{7,1},{8,10},{10,12},{12... | collective-permute-start | bytes 3145736 | tf_op jit(solution)/shard_map/ppermute | solution.py:473
  53.9 12.1 %copy-start.17 = (bf16[1024,128]{1,0:T(8,128)(2,1)S(1)}, bf16[1024,128]{1,0:T(8,128)(2,1)}, u32[]{:S(2)}) copy-start(bf16[1024,128]{1,0:T(8,128)(2,1)} %copy-done.16) | copy-start | bytes 786436
  53.9 13.7 %copy-start.15 = (bf16[1024,128]{1,0:T(8,128)(2,1)S(1)}, bf16[1024,128]{1,0:T(8,128)(2,1)}, u32[]{:S(2)}) copy-start(bf16[1024,128]{1,0:T(8,128)(2,1)} %copy-done.14) | copy-start | bytes 786436
  66.0 12.7 %copy-start.13 = (bf16[1024,128]{1,0:T(8,128)(2,1)S(1)}, bf16[1024,128]{1,0:T(8,128)(2,1)}, u32[]{:S(2)}) copy-start(bf16[1024,128]{1,0:T(8,128)(2,1)} %copy-done.12) | copy-start | bytes 786436
  66.0 14.3 %copy-start.22 = (bf16[256,256]{1,0:T(8,128)(2,1)S(1)}, bf16[256,256]{1,0:T(8,128)(2,1)}, u32[]{:S(2)}) copy-start(bf16[256,256]{1,0:T(8,128)(2,1)} %get-tuple-element.132.refs_3_) | copy-start | bytes 393220
  66.0 8.5 %collective-permute-start.12 = (bf16[1024,128]{1,0:T(8,128)(2,1)S(1)}, bf16[1024,128]{1,0:T(8,128)(2,1)S(1)}, u32[]{:S(2)}, u32[]{:S(2)}) collective-permute-start(bf16[1024,128]{1,0:T(8,128)(2,1)S(1)} %copy-done.17), channel_id=1, source_target_pairs={{0,32},{32,64},{64,96},{96,0},{1,33},{33,65},{65,97},{97,1},{2,34}... | collective-permute-start | bytes 786440 | tf_op jit(solution)/shard_map/ppermute | solution.py:473
  67.5 7.0 %collective-permute-start.13 = (bf16[1024,128]{1,0:T(8,128)(2,1)S(1)}, bf16[1024,128]{1,0:T(8,128)(2,1)S(1)}, u32[]{:S(2)}, u32[]{:S(2)}) collective-permute-start(bf16[1024,128]{1,0:T(8,128)(2,1)S(1)} %copy-done.15), channel_id=1, source_target_pairs={{0,96},{32,0},{64,32},{96,64},{1,97},{33,1},{65,33},{97,65},{2,98}... | collective-permute-start | bytes 786440 | tf_op jit(solution)/shard_map/ppermute | solution.py:473
  73.9 6.4 %copy-start.1 = (bf16[64,8192]{1,0:T(8,128)(2,1)}, bf16[64,8192]{1,0:T(8,128)(2,1)S(1)}, u32[]{:S(2)}) copy-start(bf16[64,8192]{1,0:T(8,128)(2,1)S(1)} %collective-permute-done.7.above_ref.refs_1_) | copy-start | bytes 3145732
  74.5 5.8 %copy-start.2 = (bf16[64,8192]{1,0:T(8,128)(2,1)}, bf16[64,8192]{1,0:T(8,128)(2,1)S(1)}, u32[]{:S(2)}) copy-start(bf16[64,8192]{1,0:T(8,128)(2,1)S(1)} %collective-permute-done.8.below_ref.refs_2_) | copy-start | bytes 3145732
  74.5 0.8 copy-start.20
  75.3 28.6 %collective-permute-start.20 = (bf16[512,8192]{1,0:T(8,128)(2,1)}, bf16[512,8192]{1,0:T(8,128)(2,1)}, u32[]{:S(2)}, u32[]{:S(2)}) collective-permute-start(bf16[512,8192]{1,0:T(8,128)(2,1)} %refs_0_), channel_id=1, source_target_pairs={{0,1},{1,0},{2,3},{3,2},{4,5},{5,4},{6,7},{7,6},{8,9},{9,8},{10,11... | collective-permute-start | bytes 25165832 | tf_op jit(solution)/shard_map/ppermute | solution.py:468
  75.3 3.4 %copy-start.21 = (bf16[1024,128]{1,0:T(8,128)(2,1)S(1)}, bf16[1024,128]{1,0:T(8,128)(2,1)}, u32[]{:S(2)}) copy-start(bf16[1024,128]{1,0:T(8,128)(2,1)} %copy-done.20) | copy-start | bytes 786436
  75.4 16.2 %collective-permute-start.14 = (bf16[32,8192]{1,0:T(8,128)(2,1)S(1)}, bf16[32,8192]{1,0:T(8,128)(2,1)S(1)}, u32[]{:S(2)}, u32[]{:S(2)}) collective-permute-start(bf16[32,8192]{1,0:T(8,128)(2,1)S(1)} %get-tuple-element.123), channel_id=1, source_target_pairs={{0,2},{2,4},{4,6},{6,0},{1,3},{3,5},{5,7},{7,1},{8,10},{10,12},{12... | collective-permute-start | bytes 1572872 | tf_op jit(solution)/shard_map/ppermute | solution.py:473
  76.3 15.2 %collective-permute-start.15 = (bf16[32,8192]{1,0:T(8,128)(2,1)S(1)}, bf16[32,8192]{1,0:T(8,128)(2,1)S(1)}, u32[]{:S(2)}, u32[]{:S(2)}) collective-permute-start(bf16[32,8192]{1,0:T(8,128)(2,1)S(1)} %get-tuple-element.124), channel_id=1, source_target_pairs={{0,6},{2,0},{4,2},{6,4},{1,7},{3,1},{5,3},{7,5},{8,14},{10,8},{12,... | collective-permute-start | bytes 1572872 | tf_op jit(solution)/shard_map/ppermute | solution.py:473
  78.7 12.2 %collective-permute-start.16 = (bf16[1024,128]{1,0:T(8,128)(2,1)S(1)}, bf16[1024,128]{1,0:T(8,128)(2,1)S(1)}, u32[]{:S(2)}, u32[]{:S(2)}) collective-permute-start(bf16[1024,128]{1,0:T(8,128)(2,1)S(1)} %add_convert_fusion), channel_id=1, source_target_pairs={{0,32},{32,64},{64,96},{96,0},{1,33},{33,65},{65,97},{97,1},{2,34}... | collective-permute-start | bytes 786440 | tf_op jit(solution)/shard_map/ppermute | solution.py:473
  80.3 22.9 %collective-permute-start.17 = (bf16[256,256]{1,0:T(8,128)(2,1)S(1)}, bf16[256,256]{1,0:T(8,128)(2,1)}, u32[]{:S(2)}, u32[]{:S(2)}) collective-permute-start(bf16[256,256]{1,0:T(8,128)(2,1)S(1)} %copy-done.22), channel_id=1, source_target_pairs={{0,1},{1,0},{2,3},{3,2},{4,5},{5,4},{6,7},{7,6},{8,9},{9,8},{10,11... | collective-permute-start | bytes 393224 | tf_op jit(solution)/shard_map/ppermute | solution.py:468
  91.0 12.2 %collective-permute-start.18 = (bf16[192,256]{1,0:T(8,128)(2,1)}, bf16[192,256]{1,0:T(8,128)(2,1)S(1)}, u32[]{:S(2)}, u32[]{:S(2)}) collective-permute-start(bf16[192,256]{1,0:T(8,128)(2,1)} %get-tuple-element.133.refs_4_), channel_id=1, source_target_pairs={{0,1},{1,0},{2,3},{3,2},{4,5},{5,4},{6,7},{7,6},{8,9},{9,8},{10,11... | collective-permute-start | bytes 294920 | tf_op jit(solution)/shard_map/ppermute | solution.py:468
  91.5 0.8 copy-start.18
  91.5 1.0 copy-start.19
  102.2 1.7 collective-permute-start.19
  103.2 0.6 copy-start.23
  119.0 15.5 %collective-permute-start.21 = (bf16[64,4096]{1,0:T(8,128)(2,1)}, bf16[64,4096]{1,0:T(8,128)(2,1)S(1)}, u32[]{:S(2)}, u32[]{:S(2)}) collective-permute-start(bf16[64,4096]{1,0:T(8,128)(2,1)} %get-tuple-element.139), channel_id=1, source_target_pairs={{0,2},{2,4},{4,6},{6,0},{1,3},{3,5},{5,7},{7,1},{8,10},{10,12},{12... | collective-permute-start | bytes 1572872 | tf_op jit(solution)/shard_map/ppermute | solution.py:473
  119.5 15.0 %collective-permute-start.22 = (bf16[64,4096]{1,0:T(8,128)(2,1)}, bf16[64,4096]{1,0:T(8,128)(2,1)S(1)}, u32[]{:S(2)}, u32[]{:S(2)}) collective-permute-start(bf16[64,4096]{1,0:T(8,128)(2,1)} %get-tuple-element.140), channel_id=1, source_target_pairs={{0,6},{2,0},{4,2},{6,4},{1,7},{3,1},{5,3},{7,5},{8,14},{10,8},{12,... | collective-permute-start | bytes 1572872 | tf_op jit(solution)/shard_map/ppermute | solution.py:473
  122.4 12.1 %copy-start.6 = (bf16[64,8192]{1,0:T(8,128)(2,1)S(1)}, bf16[64,8192]{1,0:T(8,128)(2,1)}, u32[]{:S(2)}) copy-start(bf16[64,8192]{1,0:T(8,128)(2,1)} %get-tuple-element.149.refs_0_) | copy-start | bytes 3145732
  122.4 12.1 %copy-start.7 = (bf16[64,8192]{1,0:T(8,128)(2,1)S(1)}, bf16[64,8192]{1,0:T(8,128)(2,1)}, u32[]{:S(2)}) copy-start(bf16[64,8192]{1,0:T(8,128)(2,1)} %get-tuple-element.151.refs_2_) | copy-start | bytes 3145732
  122.4 12.4 %collective-permute-start.23 = (bf16[512,128]{1,0:T(8,128)(2,1)S(1)}, bf16[512,128]{1,0:T(8,128)(2,1)S(1)}, u32[]{:S(2)}, u32[]{:S(2)}) collective-permute-start(bf16[512,128]{1,0:T(8,128)(2,1)S(1)} %add_convert_fusion.1), channel_id=1, source_target_pairs={{0,16},{16,0},{1,17},{17,1},{2,18},{18,2},{3,19},{19,3},{4,20},{20... | collective-permute-start | bytes 393224 | tf_op jit(solution)/shard_map/ppermute | solution.py:468
  133.6 4.6 %copy-start.26 = (bf16[64,4096]{1,0:T(8,128)(2,1)S(1)}, bf16[64,4096]{1,0:T(8,128)(2,1)}, u32[]{:S(2)}) copy-start(bf16[64,4096]{1,0:T(8,128)(2,1)} %get-tuple-element.172) | copy-start | bytes 1572868
  133.6 4.7 %copy-start.25 = (bf16[64,4096]{1,0:T(8,128)(2,1)S(1)}, bf16[64,4096]{1,0:T(8,128)(2,1)}, u32[]{:S(2)}) copy-start(bf16[64,4096]{1,0:T(8,128)(2,1)} %get-tuple-element.174) | copy-start | bytes 1572868
  133.6 7.9 %copy-start.11 = (f32[512,128]{1,0:T(8,128)S(1)}, f32[512,128]{1,0:T(8,128)}, u32[]{:S(2)}) copy-start(f32[512,128]{1,0:T(8,128)} %refs_4_.3) | copy-start | bytes 786436
  134.5 27.7 %copy-start = (bf16[64,8192]{1,0:T(8,128)(2,1)S(1)}, bf16[64,8192]{1,0:T(8,128)(2,1)}, u32[]{:S(2)}) copy-start(bf16[64,8192]{1,0:T(8,128)(2,1)} %get-tuple-element.163.refs_0_.refs_3_) | copy-start | bytes 3145732
  134.8 27.4 %collective-permute-start.24 = (bf16[64,8192]{1,0:T(8,128)(2,1)S(1)}, bf16[64,8192]{1,0:T(8,128)(2,1)S(1)}, u32[]{:S(2)}, u32[]{:S(2)}) collective-permute-start(bf16[64,8192]{1,0:T(8,128)(2,1)S(1)} %get-tuple-element.158), channel_id=1, source_target_pairs={{0,2},{2,4},{4,6},{6,0},{1,3},{3,5},{5,7},{7,1},{8,10},{10,12},{12... | collective-permute-start | bytes 3145736 | tf_op jit(solution)/shard_map/ppermute | solution.py:473
  135.6 26.7 %collective-permute-start.25 = (bf16[64,8192]{1,0:T(8,128)(2,1)S(1)}, bf16[64,8192]{1,0:T(8,128)(2,1)S(1)}, u32[]{:S(2)}, u32[]{:S(2)}) collective-permute-start(bf16[64,8192]{1,0:T(8,128)(2,1)S(1)} %get-tuple-element.159), channel_id=1, source_target_pairs={{0,6},{2,0},{4,2},{6,4},{1,7},{3,1},{5,3},{7,5},{8,14},{10,8},{12,... | collective-permute-start | bytes 3145736 | tf_op jit(solution)/shard_map/ppermute | solution.py:473
  138.2 33.5 %collective-permute-start.32 = (bf16[64,4096]{1,0:T(8,128)(2,1)S(1)}, bf16[64,4096]{1,0:T(8,128)(2,1)S(1)}, u32[]{:S(2)}, u32[]{:S(2)}) collective-permute-start(bf16[64,4096]{1,0:T(8,128)(2,1)S(1)} %copy-done.26), channel_id=1, source_target_pairs={{0,2},{2,4},{4,6},{6,0},{1,3},{3,5},{5,7},{7,1},{8,10},{10,12},{12... | collective-permute-start | bytes 1572872 | tf_op jit(solution)/shard_map/ppermute | solution.py:473
  138.3 33.4 %collective-permute-start.33 = (bf16[64,4096]{1,0:T(8,128)(2,1)S(1)}, bf16[64,4096]{1,0:T(8,128)(2,1)S(1)}, u32[]{:S(2)}, u32[]{:S(2)}) collective-permute-start(bf16[64,4096]{1,0:T(8,128)(2,1)S(1)} %copy-done.25), channel_id=1, source_target_pairs={{0,6},{2,0},{4,2},{6,4},{1,7},{3,1},{5,3},{7,5},{8,14},{10,8},{12,... | collective-permute-start | bytes 1572872 | tf_op jit(solution)/shard_map/ppermute | solution.py:473
  143.0 5.0 %collective-permute-start.26 = (bf16[512,128]{1,0:T(8,128)(2,1)S(1)}, bf16[512,128]{1,0:T(8,128)(2,1)S(1)}, u32[]{:S(2)}, u32[]{:S(2)}) collective-permute-start(bf16[512,128]{1,0:T(8,128)(2,1)S(1)} %get-tuple-element.161), channel_id=1, source_target_pairs={{0,16},{16,0},{1,17},{17,1},{2,18},{18,2},{3,19},{19,3},{4,20},{20... | collective-permute-start | bytes 393224 | tf_op jit(solution)/shard_map/ppermute | solution.py:468
  148.1 23.7 %copy-start.4 = (bf16[64,8192]{1,0:T(8,128)(2,1)S(1)}, bf16[64,8192]{1,0:T(8,128)(2,1)}, u32[]{:S(2)}) copy-start(bf16[64,8192]{1,0:T(8,128)(2,1)} %get-tuple-element.171.refs_0_) | copy-start | bytes 3145732
  148.1 23.7 %copy-start.5 = (bf16[64,8192]{1,0:T(8,128)(2,1)S(1)}, bf16[64,8192]{1,0:T(8,128)(2,1)}, u32[]{:S(2)}) copy-start(bf16[64,8192]{1,0:T(8,128)(2,1)} %get-tuple-element.173.refs_2_) | copy-start | bytes 3145732
  148.1 7.9 %collective-permute-start.27 = (bf16[1024,128]{1,0:T(8,128)(2,1)S(1)}, bf16[1024,128]{1,0:T(8,128)(2,1)S(1)}, u32[]{:S(2)}, u32[]{:S(2)}) collective-permute-start(bf16[1024,128]{1,0:T(8,128)(2,1)S(1)} %constant_dynamic-update-slice_fusion.refs_0_), channel_id=1, source_target_pairs={{0,32},{32,64},{64,96},{96,0},{1,33},{33,65},{65,97},{97,1},{2,34}... | collective-permute-start | bytes 786440 | tf_op jit(solution)/shard_map/ppermute | solution.py:473
  162.6 26.9 %copy-start.9 = (bf16[512,1024]{1,0:T(8,128)(2,1)S(1)}, bf16[512,1024]{1,0:T(8,128)(2,1)}, u32[]{:S(2)}) copy-start(bf16[512,1024]{1,0:T(8,128)(2,1)} %params_ref.1) | copy-start | bytes 3145732
  162.6 14.9 %collective-permute-start.29 = (bf16[64,4096]{1,0:T(8,128)(2,1)S(1)}, bf16[64,4096]{1,0:T(8,128)(2,1)S(1)}, u32[]{:S(2)}, u32[]{:S(2)}) collective-permute-start(bf16[64,4096]{1,0:T(8,128)(2,1)S(1)} %get-tuple-element.166.refs_4_), channel_id=1, source_target_pairs={{0,16},{16,8},{8,24},{24,0},{1,17},{17,9},{9,25},{25,1},{2,18},{18... | collective-permute-start | bytes 1572872 | tf_op jit(solution)/shard_map/ppermute | solution.py:473
  163.4 14.1 %collective-permute-start.30 = (bf16[64,4096]{1,0:T(8,128)(2,1)S(1)}, bf16[64,4096]{1,0:T(8,128)(2,1)S(1)}, u32[]{:S(2)}, u32[]{:S(2)}) collective-permute-start(bf16[64,4096]{1,0:T(8,128)(2,1)S(1)} %get-tuple-element.167), channel_id=1, source_target_pairs={{0,24},{16,0},{8,16},{24,8},{1,25},{17,1},{9,17},{25,9},{2,26},{18... | collective-permute-start | bytes 1572872 | tf_op jit(solution)/shard_map/ppermute | solution.py:473
  172.0 24.8 %copy-start.3 = (bf16[64,8192]{1,0:T(8,128)(2,1)S(1)}, bf16[64,8192]{1,0:T(8,128)(2,1)}, u32[]{:S(2)}) copy-start(bf16[64,8192]{1,0:T(8,128)(2,1)} %get-tuple-element.170.refs_0_) | copy-start | bytes 3145732
  172.0 24.7 %collective-permute-start.34 = (bf16[64,8192]{1,0:T(8,128)(2,1)S(1)}, bf16[64,8192]{1,0:T(8,128)(2,1)S(1)}, u32[]{:S(2)}, u32[]{:S(2)}) collective-permute-start(bf16[64,8192]{1,0:T(8,128)(2,1)S(1)} %get-tuple-element.175), channel_id=1, source_target_pairs={{0,2},{2,4},{4,6},{6,0},{1,3},{3,5},{5,7},{7,1},{8,10},{10,12},{12... | collective-permute-start | bytes 3145736 | tf_op jit(solution)/shard_map/ppermute | solution.py:473
  172.9 23.9 %collective-permute-start.35 = (bf16[64,8192]{1,0:T(8,128)(2,1)S(1)}, bf16[64,8192]{1,0:T(8,128)(2,1)S(1)}, u32[]{:S(2)}, u32[]{:S(2)}) collective-permute-start(bf16[64,8192]{1,0:T(8,128)(2,1)S(1)} %get-tuple-element.176), channel_id=1, source_target_pairs={{0,6},{2,0},{4,2},{6,4},{1,7},{3,1},{5,3},{7,5},{8,14},{10,8},{12,... | collective-permute-start | bytes 3145736 | tf_op jit(solution)/shard_map/ppermute | solution.py:473
  175.4 6.4 %collective-permute-start.28 = (bf16[1024,128]{1,0:T(8,128)(2,1)S(1)}, bf16[1024,128]{1,0:T(8,128)(2,1)S(1)}, u32[]{:S(2)}, u32[]{:S(2)}) collective-permute-start(bf16[1024,128]{1,0:T(8,128)(2,1)S(1)} %constant_dynamic-update-slice_fusion.refs_0_), channel_id=1, source_target_pairs={{0,96},{32,0},{64,32},{96,64},{1,97},{33,1},{65,33},{97,65},{2,98}... | collective-permute-start | bytes 786440 | tf_op jit(solution)/shard_map/ppermute | solution.py:473
  177.6 19.2 %collective-permute-start.36 = (bf16[64,4096]{1,0:T(8,128)(2,1)S(1)}, bf16[64,4096]{1,0:T(8,128)(2,1)S(1)}, u32[]{:S(2)}, u32[]{:S(2)}) collective-permute-start(bf16[64,4096]{1,0:T(8,128)(2,1)S(1)} %collective-permute-done.29), channel_id=1, source_target_pairs={{0,16},{16,8},{8,24},{24,0},{1,17},{17,9},{9,25},{25,1},{2,18},{18... | collective-permute-start | bytes 1572872 | tf_op jit(solution)/shard_map/ppermute | solution.py:473
  178.3 18.5 %collective-permute-start.37 = (bf16[64,4096]{1,0:T(8,128)(2,1)S(1)}, bf16[64,4096]{1,0:T(8,128)(2,1)S(1)}, u32[]{:S(2)}, u32[]{:S(2)}) collective-permute-start(bf16[64,4096]{1,0:T(8,128)(2,1)S(1)} %collective-permute-done.30), channel_id=1, source_target_pairs={{0,24},{16,0},{8,16},{24,8},{1,25},{17,1},{9,17},{25,9},{2,26},{18... | collective-permute-start | bytes 1572872 | tf_op jit(solution)/shard_map/ppermute | solution.py:473
  181.7 7.8 %collective-permute-start.31 = (bf16[1024,128]{1,0:T(8,128)(2,1)S(1)}, bf16[1024,128]{1,0:T(8,128)(2,1)S(1)}, u32[]{:S(2)}, u32[]{:S(2)}) collective-permute-start(bf16[1024,128]{1,0:T(8,128)(2,1)S(1)} %collective-permute-done.27.refs_2_), channel_id=1, source_target_pairs={{0,32},{32,64},{64,96},{96,0},{1,33},{33,65},{65,97},{97,1},{2,34}... | collective-permute-start | bytes 786440 | tf_op jit(solution)/shard_map/ppermute | solution.py:473
  (1 other events, 0.6 us)
